TPU v7x, 32 devices: a whole 2x2x4 slice. The times are simulated.
32 devices in a mesh: rep: 8 (over z, x), grp: 4 (over y, core).
Axes of the slice: x: 2, y: 2, z: 4, core: 2. Of those that a mesh axis runs over, the one named last changes fastest.
Arguments:
- x_input: bfloat16 [8, 1024, 1024], P('rep', 'grp'), may hold values from -6 to 6
- norm_gain: bfloat16 [2, 2, 1024], P(None, None, 'grp'), may hold values from 0.5 to 1.5
- w_in: bfloat16 [2, 1024, 6144], P(None, 'grp'), may hold values from -0.1875 to 0.1875
- w_ab: bfloat16 [2, 1024, 16], P(None, 'grp'), may hold values from -0.1875 to 0.1875
- conv_w: bfloat16 [2, 4, 4096], P(None, None, 'grp'), may hold values from -3 to 3
- a_log: bfloat16 [2, 8], P(None, 'grp'), may hold values from -2.5 to 0
- dt_bias: bfloat16 [2, 8], P(None, 'grp'), may hold values from -5 to 0.5
- out_gain: bfloat16 [2, 256], P(None, 'grp'), may hold values from 0.5 to 1.5
- w_out: bfloat16 [2, 2048, 1024], P(None, 'grp'), may hold values from -0.25 to 0.25
- ffn_in: bfloat16 [2, 1024, 5632], P(None, 'grp'), may hold values from -0.1875 to 0.1875
- ffn_out: bfloat16 [2, 2816, 1024], P(None, 'grp'), may hold values from -0.21875 to 0.21875
- cotangent: bfloat16 [8, 1024, 1024], P('rep', 'grp'), may hold values from -6 to 6
Outputs:
- block_output: bfloat16 [8, 1024, 1024], P('rep', 'grp')
- input_grad: bfloat16 [8, 1024, 1024], P('rep', 'grp')
- grad_norm_gain: float32 [2, 2, 1024], P(None, None, 'grp')
- grad_w_in: float32 [2, 1024, 6144], P(None, 'grp')
- grad_w_ab: float32 [2, 1024, 16], P(None, 'grp')
- grad_conv_w: float32 [2, 4, 4096], P(None, None, 'grp')
- grad_a_log: float32 [2, 8], P(None, 'grp')
- grad_dt_bias: float32 [2, 8], P(None, 'grp')
- grad_out_gain: float32 [2, 256], P(None, 'grp')
- grad_w_out: float32 [2, 2048, 1024], P(None, 'grp')
- grad_ffn_in: float32 [2, 1024, 5632], P(None, 'grp')
- grad_ffn_out: float32 [2, 2816, 1024], P(None, 'grp')
All inputs are finite; a program needn't handle non-finite values.
Results may differ from a plain program's by a relative error of at most 0.03.
Values may be sent and summed in bfloat16 or wider, within the bound.
A program may use at most 640 MiB of HBM per device.

v0:
```python
from functools import partial
import math

import jax
import jax.numpy as jnp
from jax import lax
from jax.sharding import PartitionSpec as P

H = 8
DK = 128
DV = 256
FF = 2816
CONV = 4
BLOCK = 64
LAYERS = 2
HK = 1024
HV = 2048
CH = 4096


precise = lax.Precision.HIGHEST
epsilon = 1e-06
out_floor = 0.02
shard_dims = (1, 0, 0, 1, 0, 0, 0, 0, 0, 0)


def shifted(block, axis, distance):
    devices = range(lax.axis_size(axis))
    route = [(i - distance, i) for i in devices if i - distance in devices]
    return lax.ppermute(block, axis, route)


def entering(x, axis, combine, identity):
    size, mine = (lax.axis_size(axis), lax.axis_index(axis))
    everything = jax.tree.map(lambda part: lax.all_gather(part, axis), x)
    start = jax.tree.map(
        lambda part, zero: jnp.broadcast_to(jnp.asarray(zero, part.dtype), part.shape), x, identity
    )

    def entering_hop(k, before):
        reached = k < mine
        new = combine(before, jax.tree.map(lambda part: part[k], everything))
        return jax.tree.map(lambda a, b: jnp.where(reached, a, b), new, before)

    return lax.fori_loop(0, size, entering_hop, start)


def carried_in(x, axis, combine, identity):
    size, mine = (lax.axis_size(axis), lax.axis_index(axis))
    everything = jax.tree.map(
        lambda part, kind: lax.all_gather(part.astype(kind), axis),
        x,
        jax.tree.map(lambda a: jnp.bfloat16 if a.dtype == jnp.float32 else a.dtype, x),
    )
    start = jax.tree.map(
        lambda part, zero: jnp.broadcast_to(jnp.asarray(zero, part.dtype), part.shape), x, identity
    )

    def carried_hop(k, before):
        at = size - 1 - k
        reached = at > mine
        new = combine(
            before, jax.tree.map(lambda part, own: part[at].astype(own.dtype), everything, x)
        )
        return jax.tree.map(lambda a, b: jnp.where(reached, a, b), new, before)

    return lax.fori_loop(0, size, carried_hop, start)


def rounded(value):
    return lax.optimization_barrier(value.astype(jnp.bfloat16)).astype(jnp.float32)


def rms_norm(residual, gain):
    return (
        residual * lax.rsqrt(jnp.mean(residual * residual, axis=-1, keepdims=True) + epsilon) * gain
    )


def conv_piece(extended, conv_weight):
    length = extended.shape[1] - (CONV - 1)
    convolved = sum(
        (
            extended[:, tap_index : tap_index + length] * conv_weight[tap_index]
            for tap_index in range(CONV)
        )
    )
    activated = jax.nn.silu(convolved)
    key_shape = activated.shape[:2] + (H, DK)
    queries = activated[..., :HK].reshape(key_shape)
    key_part = activated[..., HK : 2 * HK].reshape(key_shape)
    values = activated[..., 2 * HK :].reshape(activated.shape[:2] + (H, DV))
    queries = (
        queries
        * lax.rsqrt(jnp.sum(queries * queries, axis=-1, keepdims=True) + epsilon)
        / math.sqrt(DK)
    )
    key_part = key_part * lax.rsqrt(jnp.sum(key_part * key_part, axis=-1, keepdims=True) + epsilon)
    return (queries, key_part, values)


def decay_piece(small_proj, alog_part, bias_part):
    strength = jax.nn.sigmoid(small_proj[..., :H])
    log_decay = -jnp.exp(alog_part) * jax.nn.softplus(small_proj[..., H:] + bias_part)
    return (strength, log_decay)


def gated_piece(mixed_heads, gate_part, gain_out):
    scaled = mixed_heads * lax.rsqrt(
        jnp.mean(mixed_heads * mixed_heads, axis=-1, keepdims=True) + out_floor
    )
    return scaled * gain_out * jax.nn.silu(gate_part)


def swiglu_piece(up_part):
    return jax.nn.silu(up_part[..., :FF]) * up_part[..., FF:]


def gram_product(left, right, narrow_grams):
    if narrow_grams:
        return jnp.einsum(
            "shck,shdk->shcd",
            left.astype(jnp.bfloat16),
            right.astype(jnp.bfloat16),
            preferred_element_type=jnp.float32,
        )
    return jnp.einsum("shck,shdk->shcd", left, right, precision=precise)


def span_pass(narrow_grams, queries, key_part, values, strength, log_decay, initial):
    seg_length = queries.shape[1]
    positions = lax.broadcasted_iota(jnp.int32, (BLOCK, BLOCK), 0)
    columns = lax.broadcasted_iota(jnp.int32, (BLOCK, BLOCK), 1)
    strict = positions > columns
    inclusive = positions >= columns
    identity_block = jnp.eye(BLOCK, dtype=jnp.float32)
    carried = initial
    results = []
    for block_index in range(seg_length // BLOCK):
        lower_edge = block_index * BLOCK

        def window(tensor):
            return jnp.moveaxis(tensor[:, lower_edge : lower_edge + BLOCK], 2, 1)

        query_block = window(queries)
        key_block = window(key_part)
        value_block = window(values)
        strength_block = window(strength)
        cumulative = jnp.cumsum(window(log_decay), axis=-1)
        spread_log = cumulative[..., :, None] - cumulative[..., None, :]
        key_gram = gram_product(key_block, key_block, narrow_grams)
        lower_part = (
            jnp.exp(jnp.where(strict, spread_log, -10000.0))
            * key_gram
            * strength_block[..., None, :]
        )
        system = identity_block + lower_part
        growth = jnp.exp(cumulative)
        right_side = value_block - growth[..., None] * jnp.einsum(
            "shck,shkw->shcw", key_block, carried, precision=precise
        )
        pseudo_values = lax.linalg.triangular_solve(
            system, right_side, left_side=True, lower=True, unit_diagonal=True
        )
        query_gram = gram_product(query_block, key_block, narrow_grams)
        mixing = (
            jnp.exp(jnp.where(inclusive, spread_log, -10000.0))
            * query_gram
            * strength_block[..., None, :]
        )
        block_result = growth[..., None] * jnp.einsum(
            "shck,shkw->shcw", query_block, carried, precision=precise
        ) + jnp.einsum("shcd,shdw->shcw", mixing, pseudo_values, precision=precise)
        tail_weight = jnp.exp(cumulative[..., -1:] - cumulative) * strength_block
        carried = jnp.exp(cumulative[..., -1])[..., None, None] * carried + jnp.einsum(
            "shck,shcw->shkw", key_block, tail_weight[..., None] * pseudo_values, precision=precise
        )
        results.append(jnp.moveaxis(block_result, 1, 2))
    return (jnp.concatenate(results, axis=1), carried)


def compose(earlier, later):
    first = jnp.einsum("shij,shjk->shik", later[0], earlier[0], precision=precise)
    second = jnp.einsum("shij,shjk->shik", later[0], earlier[1], precision=precise) + later[1]
    return (first, second)


def forward_layer(residual, full_weights, seq_count, seg_length):
    (
        norm_gains,
        in_weight,
        ab_weight,
        conv_weight,
        alog_part,
        bias_part,
        gain_out,
        out_weight,
        up_weight,
        down_weight,
    ) = full_weights
    row_count = residual.shape[0]
    normed = rms_norm(residual, norm_gains[0].astype(jnp.float32)).astype(jnp.bfloat16)
    projected = jnp.dot(normed, in_weight, preferred_element_type=jnp.float32).astype(jnp.bfloat16)
    small_proj = jnp.dot(normed, ab_weight, preferred_element_type=jnp.float32)
    conv_input = projected[:, :CH].reshape(seq_count, seg_length, CH)
    rim_rows = shifted(conv_input[:, seg_length - (CONV - 1) :], "grp", 1)
    extended = jnp.concatenate([rim_rows, conv_input], axis=1).astype(jnp.float32)
    queries, key_part, values = conv_piece(extended, conv_weight.astype(jnp.float32))
    queries, key_part, values = (rounded(queries), rounded(key_part), rounded(values))
    strength, log_decay = decay_piece(
        small_proj.reshape(seq_count, seg_length, 2 * H),
        alog_part.astype(jnp.float32),
        bias_part.astype(jnp.float32),
    )
    identity_map = jnp.broadcast_to(jnp.eye(DK, dtype=jnp.float32), (seq_count, H, DK, DK))
    zero_state = jnp.zeros((seq_count, H, DK, DV), jnp.float32)
    widened = jnp.concatenate([jnp.zeros(values.shape[:3] + (DK,), jnp.float32), values], axis=-1)
    start_both = jnp.concatenate([identity_map, zero_state], axis=-1)
    block_outs, end_states = span_pass(
        True, queries, key_part, widened, strength, log_decay, start_both
    )
    transfer = end_states[..., :DK]
    prefix_map, initial = entering(
        (transfer, end_states[..., DK:]), "grp", compose, (identity_map, zero_state)
    )
    mixed_heads = block_outs[..., DK:] + jnp.einsum(
        "sthk,shkv->sthv", block_outs[..., :DK], initial, precision=precise
    )
    gate_part = projected[:, CH:].astype(jnp.float32).reshape(seq_count, seg_length, H, DV)
    gated_out = (
        gated_piece(mixed_heads, gate_part, gain_out.astype(jnp.float32))
        .reshape(row_count, HV)
        .astype(jnp.bfloat16)
    )
    residual_mid = residual + jnp.dot(gated_out, out_weight, preferred_element_type=jnp.float32)
    normed_two = rms_norm(residual_mid, norm_gains[1].astype(jnp.float32)).astype(jnp.bfloat16)
    up_part = jnp.dot(normed_two, up_weight, preferred_element_type=jnp.float32)
    hidden = swiglu_piece(up_part).astype(jnp.bfloat16)
    residual_out = residual_mid + jnp.dot(hidden, down_weight, preferred_element_type=jnp.float32)
    kept = (
        residual,
        normed,
        projected,
        small_proj,
        rim_rows,
        initial,
        transfer,
        residual_mid,
        normed_two,
        up_part,
        hidden,
    )
    return (residual_out, kept)


def backward_layer(d_out, full_weights, kept, seq_count, seg_length):
    (
        norm_gains,
        in_weight,
        ab_weight,
        conv_weight,
        alog_part,
        bias_part,
        gain_out,
        out_weight,
        up_weight,
        down_weight,
    ) = full_weights
    (
        residual,
        normed,
        projected,
        small_proj,
        rim_rows,
        initial,
        transfer,
        residual_mid,
        normed_two,
        up_part,
        hidden,
    ) = kept
    row_count = residual.shape[0]
    d_down = d_out.astype(jnp.bfloat16)
    grad_down = jnp.einsum("rf,rd->fd", hidden, d_down, preferred_element_type=jnp.float32)
    d_hidden = jnp.einsum("rd,fd->rf", d_down, down_weight, preferred_element_type=jnp.float32)
    swiglu_value, swiglu_back = jax.vjp(swiglu_piece, up_part)
    d_up = swiglu_back(d_hidden)[0].astype(jnp.bfloat16)
    grad_up = jnp.einsum("rd,rf->df", normed_two, d_up, preferred_element_type=jnp.float32)
    d_normed_two = jnp.einsum("rf,df->rd", d_up, up_weight, preferred_element_type=jnp.float32)
    norm_value, second_back = jax.vjp(rms_norm, residual_mid, norm_gains[1].astype(jnp.float32))
    d_mid_norm, grad_gain_two = second_back(d_normed_two)
    d_mid = d_out + d_mid_norm
    d_branch = d_mid.astype(jnp.bfloat16)
    conv_input = projected[:, :CH].reshape(seq_count, seg_length, CH)
    extended = jnp.concatenate([rim_rows, conv_input], axis=1).astype(jnp.float32)
    conv_values, conv_back = jax.vjp(conv_piece, extended, conv_weight.astype(jnp.float32))
    queries, key_part, values = (
        rounded(conv_values[0]),
        rounded(conv_values[1]),
        rounded(conv_values[2]),
    )
    decay_values, decay_back = jax.vjp(
        decay_piece,
        small_proj.reshape(seq_count, seg_length, 2 * H),
        alog_part.astype(jnp.float32),
        bias_part.astype(jnp.float32),
    )
    state_values, state_back = jax.vjp(
        partial(span_pass, False),
        queries,
        key_part,
        values,
        decay_values[0],
        decay_values[1],
        initial,
    )
    gate_part = projected[:, CH:].astype(jnp.float32).reshape(seq_count, seg_length, H, DV)
    gated_value, gated_back = jax.vjp(
        gated_piece, state_values[0], gate_part, gain_out.astype(jnp.float32)
    )
    gated_out = gated_value.reshape(row_count, HV).astype(jnp.bfloat16)
    grad_out_weight = jnp.einsum(
        "rv,rd->vd", gated_out, d_branch, preferred_element_type=jnp.float32
    )
    d_gated = jnp.einsum(
        "rd,vd->rv", d_branch, out_weight, preferred_element_type=jnp.float32
    ).reshape(seq_count, seg_length, H, DV)
    d_mixed, d_gate, grad_gain_out = gated_back(d_gated)
    zero_state = jnp.zeros_like(initial)
    identity_map = jnp.broadcast_to(jnp.eye(DK, dtype=jnp.float32), transfer.shape)
    local_terms = state_back((d_mixed, zero_state))
    suffix_map, d_end = carried_in(
        (jnp.swapaxes(transfer, -1, -2), local_terms[5]), "grp", compose, (identity_map, zero_state)
    )
    d_queries, d_keys, d_values, d_strength, d_decay, d_initial = state_back((d_mixed, d_end))
    d_extended, grad_conv = conv_back((d_queries, d_keys, d_values))
    sent_back = shifted(d_extended[:, : CONV - 1].astype(jnp.bfloat16), "grp", -1).astype(
        jnp.float32
    )
    d_conv_input = d_extended[:, CONV - 1 :]
    edge = seg_length - (CONV - 1)
    d_conv_input = jnp.concatenate(
        [d_conv_input[:, :edge], d_conv_input[:, edge:] + sent_back], axis=1
    )
    d_small, grad_alog, grad_bias = decay_back((d_strength, d_decay))
    d_projected = jnp.concatenate(
        [d_conv_input.reshape(row_count, CH), d_gate.reshape(row_count, HV)], axis=1
    ).astype(jnp.bfloat16)
    d_small = d_small.reshape(row_count, 2 * H).astype(jnp.bfloat16)
    grad_in = jnp.einsum("rd,rp->dp", normed, d_projected, preferred_element_type=jnp.float32)
    grad_ab = jnp.einsum("rd,rp->dp", normed, d_small, preferred_element_type=jnp.float32)
    d_normed = jnp.einsum(
        "rp,dp->rd", d_projected, in_weight, preferred_element_type=jnp.float32
    ) + jnp.einsum("rp,dp->rd", d_small, ab_weight, preferred_element_type=jnp.float32)
    first_value, first_back = jax.vjp(rms_norm, residual, norm_gains[0].astype(jnp.float32))
    d_in_norm, grad_gain_one = first_back(d_normed)
    d_residual = d_mid + d_in_norm
    gradients = (
        jnp.stack([grad_gain_one, grad_gain_two]),
        grad_in,
        grad_ab,
        grad_conv,
        grad_alog,
        grad_bias,
        grad_gain_out,
        grad_out_weight,
        grad_up,
        grad_down,
    )
    return (d_residual, gradients)


def pack_rows(gradients, parts):
    pieces = []
    for gradient, split_dim in zip(gradients, shard_dims):
        full_shape = gradient.shape
        split = gradient.reshape(
            full_shape[:split_dim]
            + (parts, full_shape[split_dim] // parts)
            + full_shape[split_dim + 1 :]
        )
        pieces.append(jnp.moveaxis(split, split_dim, 0).reshape(parts, -1))
    return jnp.concatenate(pieces, axis=1)


def unpack_rows(flat, full_shapes, parts):
    outputs = []
    start_at = 0
    for full_shape, split_dim in zip(full_shapes, shard_dims):
        local_shape = (
            full_shape[:split_dim] + (full_shape[split_dim] // parts,) + full_shape[split_dim + 1 :]
        )
        element_count = math.prod(local_shape)
        outputs.append(flat[start_at : start_at + element_count].reshape(local_shape))
        start_at += element_count
    return outputs


def per_device(
    x_input,
    norm_gain,
    w_in,
    w_ab,
    conv_w,
    a_log,
    dt_bias,
    out_gain,
    w_out,
    ffn_in,
    ffn_out,
    cotangent,
):
    seq_count, seg_length, width = x_input.shape
    row_count = seq_count * seg_length
    parts = lax.axis_size("grp")
    replicas = lax.axis_size("rep")
    residual = x_input.astype(jnp.float32).reshape(row_count, width)
    kept_layers = []
    weight_layers = []
    for layer_index in range(LAYERS):
        full_weights = (
            lax.all_gather(norm_gain[layer_index], "grp", axis=1, tiled=True),
            lax.all_gather(w_in[layer_index], "grp", axis=0, tiled=True),
            lax.all_gather(w_ab[layer_index], "grp", axis=0, tiled=True),
            lax.all_gather(conv_w[layer_index], "grp", axis=1, tiled=True),
            lax.all_gather(a_log[layer_index], "grp", axis=0, tiled=True),
            lax.all_gather(dt_bias[layer_index], "grp", axis=0, tiled=True),
            lax.all_gather(out_gain[layer_index], "grp", axis=0, tiled=True),
            lax.all_gather(w_out[layer_index], "grp", axis=0, tiled=True),
            lax.all_gather(ffn_in[layer_index], "grp", axis=0, tiled=True),
            lax.all_gather(ffn_out[layer_index], "grp", axis=0, tiled=True),
        )
        residual, kept = forward_layer(residual, full_weights, seq_count, seg_length)
        kept_layers.append(kept)
        weight_layers.append(full_weights)
    full_shapes = [weight.shape for weight in weight_layers[0]]
    d_residual = cotangent.astype(jnp.float32).reshape(row_count, width)
    pieces = []
    flat_lengths = []
    for layer_index in reversed(range(LAYERS)):
        full_weights = (
            lax.all_gather(norm_gain[layer_index], "grp", axis=1, tiled=True),
            lax.all_gather(w_in[layer_index], "grp", axis=0, tiled=True),
            lax.all_gather(w_ab[layer_index], "grp", axis=0, tiled=True),
            lax.all_gather(conv_w[layer_index], "grp", axis=1, tiled=True),
            lax.all_gather(a_log[layer_index], "grp", axis=0, tiled=True),
            lax.all_gather(dt_bias[layer_index], "grp", axis=0, tiled=True),
            lax.all_gather(out_gain[layer_index], "grp", axis=0, tiled=True),
            lax.all_gather(w_out[layer_index], "grp", axis=0, tiled=True),
            lax.all_gather(ffn_in[layer_index], "grp", axis=0, tiled=True),
            lax.all_gather(ffn_out[layer_index], "grp", axis=0, tiled=True),
        )
        d_residual, gradients = backward_layer(
            d_residual, full_weights, kept_layers[layer_index], seq_count, seg_length
        )
        flat = pack_rows(gradients, parts)
        flat_length = flat.shape[1]
        padded_length = -(-flat_length // replicas) * replicas
        flat = jnp.pad(flat, ((0, 0), (0, padded_length - flat_length)))
        owned = lax.psum_scatter(
            flat.astype(jnp.bfloat16), "grp", scatter_dimension=0, tiled=True
        ).astype(jnp.float32)
        piece = owned.reshape(replicas, padded_length // replicas)
        pieces.insert(0, piece)
        flat_lengths.insert(0, flat_length)
    joined = jnp.concatenate(pieces, axis=1)
    joined = lax.psum_scatter(joined, "rep", scatter_dimension=0, tiled=True)
    spread = lax.all_gather(joined.astype(jnp.bfloat16), "rep", axis=0, tiled=True).astype(
        joined.dtype
    )
    collected = [[] for slot_index in range(len(shard_dims))]
    start_column = 0
    for layer_index in range(LAYERS):
        piece_width = pieces[layer_index].shape[1]
        shard_flat = spread[:, start_column : start_column + piece_width].reshape(-1)[
            : flat_lengths[layer_index]
        ]
        start_column += piece_width
        for slot_index, array_piece in enumerate(unpack_rows(shard_flat, full_shapes, parts)):
            collected[slot_index].append(array_piece)
    stacked = [jnp.stack(items_list) for items_list in collected]
    block_output = residual.reshape(x_input.shape).astype(jnp.bfloat16)
    input_grad = d_residual.reshape(x_input.shape).astype(jnp.bfloat16)
    return (
        block_output,
        input_grad,
        stacked[0],
        stacked[1],
        stacked[2],
        stacked[3],
        stacked[4],
        stacked[5],
        stacked[6],
        stacked[7],
        stacked[8],
        stacked[9],
    )


def solution(mesh):
    in_specs = (
        P("rep", "grp", None),
        P(None, None, "grp"),
        P(None, "grp", None),
        P(None, "grp", None),
        P(None, None, "grp"),
        P(None, "grp"),
        P(None, "grp"),
        P(None, "grp"),
        P(None, "grp", None),
        P(None, "grp", None),
        P(None, "grp", None),
        P("rep", "grp", None),
    )
    out_specs = (
        P("rep", "grp", None),
        P("rep", "grp", None),
        P(None, None, "grp"),
        P(None, "grp", None),
        P(None, "grp", None),
        P(None, None, "grp"),
        P(None, "grp"),
        P(None, "grp"),
        P(None, "grp"),
        P(None, "grp", None),
        P(None, "grp", None),
        P(None, "grp", None),
    )
    return jax.shard_map(
        per_device, mesh=mesh, in_specs=in_specs, out_specs=out_specs, check_vma=False
    )
```

profile of v0, /device:TPU:0, one launch (start us, length us, event | category | flops | bytes accessed | tf_op | source)
XLA Modules:
  0.0 5626.8 jit_solution(15602134831212970174)
XLA Ops:
  48.5 50.4 all-gather.47.cloned.1.call-done
  119.7 40.0 custom-call.52
  160.6 40.0 custom-call.53
  201.5 40.0 custom-call.54
  242.4 40.2 custom-call.55
  397.6 74.2 %all-gather.55.cloned.1.call-done = bf16[1,1024,5632]{2,1,0:T(8,128)(2,1)} async-done(((bf16[1,256,5632]{2,1,0:T(8,128)(2,1)}), bf16[1,1024,5632]{2,1,0:T(8,128)(2,1)}) %all-gather.55.cloned.1.call-update) | async-done | bytes 11534352 | tf_op jit(solution)/shard_map/all_gather | solution.py:430
  525.0 76.0 %all-gather.59.cloned.1.call-done = bf16[1,1024,6144]{2,1,0:T(8,128)(2,1)} async-done(((bf16[1,256,6144]{2,1,0:T(8,128)(2,1)}), bf16[1,1024,6144]{2,1,0:T(8,128)(2,1)}) %all-gather.59.cloned.1.call-update) | async-done | bytes 12582928 | tf_op jit(solution)/shard_map/all_gather | solution.py:423
  627.2 39.3 custom-call.56
  667.5 40.0 custom-call.57
  708.4 40.0 custom-call.58
  750.0 40.0 custom-call.59
  822.7 40.9 custom-call.60
  863.5 40.7 custom-call.61
  904.2 40.7 custom-call.62
  944.9 40.7 custom-call.68
  1125.8 40.7 custom-call.76
  1166.5 40.7 custom-call.77
  1207.2 40.7 custom-call.78
  1274.7 41.1 custom-call.84
  1844.5 40.5 dynamic-update-slice.13
  1885.0 108.5 %dynamic-update-slice.14 = bf16[4,4268612]{1,0:T(4,128)(2,1)} dynamic-update-slice(bf16[4,4268612]{1,0:T(4,128)(2,1)} %dynamic-update-slice.13, bf16[4,1441792]{1,0:T(4,128)(2,1)} %reshape_reshape.48, s32[]{} %constant.522, s32[]{} %constant.530) | dynamic-update-slice | bytes 23068676
  1993.5 54.9 dynamic-update-slice.15
  2048.3 34.4 pad.357
  2144.3 40.6 dynamic-update-slice.23
  2184.9 108.9 %dynamic-update-slice.24 = bf16[4,4268612]{1,0:T(4,128)(2,1)} dynamic-update-slice(bf16[4,4268612]{1,0:T(4,128)(2,1)} %dynamic-update-slice.23, bf16[4,1441792]{1,0:T(4,128)(2,1)} %reshape_reshape.43, s32[]{} %constant.522, s32[]{} %constant.530) | dynamic-update-slice | bytes 23068676
  2293.8 55.1 dynamic-update-slice.25
  2384.4 269.5 %all-reduce.107.cloned.1.call-done = bf16[4,4268616]{1,0:T(4,128)(2,1)} async-done(((bf16[4,4268616]{1,0:T(4,128)(2,1)}), bf16[4,4268616]{1,0:T(4,128)(2,1)}) %all-reduce.107.cloned.1.call-update) | async-done | bytes 34148944
  2653.9 183.3 %dynamic-slice_reduce_fusion = bf16[4268616]{0:T(1024)(128)(2,1)} fusion(bf16[4,4268616]{1,0:T(4,128)(2,1)} %all-reduce.107.cloned.1.call-done, u32[]{:T(128)} %bitcast.1030), kind=kLoop, calls=%fused_computation.46 | loop fusion | bytes 17074468
  2854.9 369.8 %all-reduce.105.cloned.1.call-done = bf16[4,4268616]{1,0:T(4,128)(2,1)} async-done(((bf16[4,4268616]{1,0:T(4,128)(2,1)}), bf16[4,4268616]{1,0:T(4,128)(2,1)}) %all-reduce.105.cloned.1.call-update) | async-done | bytes 34148944
  3224.7 183.1 %dynamic-slice_reduce_fusion.1 = bf16[4268616]{0:T(1024)(128)(2,1)} fusion(bf16[4,4268616]{1,0:T(4,128)(2,1)} %all-reduce.105.cloned.1.call-done, u32[]{:T(128)} %bitcast.1030), kind=kLoop, calls=%fused_computation.47 | loop fusion | bytes 17074468
  3452.5 1305.5 %all-reduce.108 = bf16[8,1067154]{1,0:T(8,128)(2,1)} all-reduce(f32[8,1067154]{1,0:T(8,128)} %maximum_convert_fusion), channel_id=32, replica_groups=mesh['rep'=8,'grp'=4] {'rep'}, use_global_device_ids=true, to_apply=%region_148.154.clone | all-reduce | flops 8537232 | bytes 51223392
  4776.1 638.2 %all-gather.79.cloned.1.call-done = bf16[8,1,1067154]{2,1,0:T(2,128)(2,1)} async-done(((bf16[1,1,1067154]{2,1,0:T(2,128)(2,1)}), bf16[8,1,1067154]{2,1,0:T(2,128)(2,1)}) %all-gather.79.cloned.1.call-update) | async-done | bytes 17074480 | tf_op jit(solution)/shard_map/all_gather | solution.py:468
  (1857 shorter events, 1419.2 us)
Async XLA Ops:
  7.2 91.8 %all-gather.47.cloned.1.call-start = ((), (), s32[]{:S(2)}) async-start(), calls=%async_computation | async-start | bytes 15728640 | tf_op jit(solution)/shard_map/all_gather | solution.py:423
  13.6 332.6 %all-gather.49.cloned.1.call-start = ((), (), s32[]{:S(2)}) async-start(), calls=%async_computation.1 | async-start | bytes 2621440 | tf_op jit(solution)/shard_map/all_gather | solution.py:35
  37.7 434.2 %copy-start.373 = (f32[1,1,1024]{2,1,0:T(1,128)}, f32[1,1,1024]{2,1,0:T(1,128)S(1)}, u32[]{:S(2)}) copy-start(f32[1,1,1024]{2,1,0:T(1,128)S(1)} %get-tuple-element.939) | copy-start | bytes 12292
  39.1 296.0 %copy-start.320 = (f32[1,8,64]{2,1,0:T(8,128)}, f32[1,8,64]{2,1,0:T(8,128)S(1)}, u32[]{:S(2)}) copy-start(f32[1,8,64]{2,1,0:T(8,128)S(1)} %reduce_window_sum.118) | copy-start | bytes 6148
  46.3 702.1 %copy-start.377 = (f32[64,64]{1,0:T(8,128)}, f32[64,64]{1,0:T(8,128)S(1)}, u32[]{:S(2)}) copy-start(f32[64,64]{1,0:T(8,128)S(1)} %fusion.1448) | copy-start | bytes 49156
  47.5 290.0 %copy-start.375 = (f32[8,64]{1,0:T(8,128)}, f32[8,64]{1,0:T(8,128)S(1)}, u32[]{:S(2)}) copy-start(f32[8,64]{1,0:T(8,128)S(1)} %bitcast_exponential_fusion.7) | copy-start | bytes 6148
  47.5 293.3 %copy-start.371 = (f32[8,64]{1,0:T(8,128)}, f32[8,64]{1,0:T(8,128)S(1)}, u32[]{:S(2)}) copy-start(f32[8,64]{1,0:T(8,128)S(1)} %bitcast_exponential_fusion.5) | copy-start | bytes 6148
  47.5 291.5 %copy-start.369 = (f32[8,64]{1,0:T(8,128)}, f32[8,64]{1,0:T(8,128)S(1)}, u32[]{:S(2)}) copy-start(f32[8,64]{1,0:T(8,128)S(1)} %bitcast_exponential_fusion.4) | copy-start | bytes 6148
  107.6 3.1 collective-permute-start
  118.1 694.2 %copy-start.2 = (bf16[1,256,8,128]{3,1,2,0:T(8,128)(2,1)}, bf16[1,256,8,128]{3,1,2,0:T(8,128)(2,1)S(1)}, u32[]{:S(2)}) copy-start(bf16[1,256,8,128]{3,1,2,0:T(8,128)(2,1)S(1)} %fusion.531) | copy-start | bytes 1572868
  296.7 61.0 %all-gather.51.cloned.1.call-start = ((), (), s32[]{:S(2)}) async-start(), calls=%async_computation.2 | async-start | bytes 5242880 | tf_op jit(solution)/shard_map/all_gather | solution.py:35
  297.9 95.8 %all-gather.53.cloned.1.call-start = ((), (), s32[]{:S(2)}) async-start(), calls=%async_computation.3 | async-start | bytes 5242880 | tf_op jit(solution)/shard_map/all_gather | solution.py:429
  300.9 170.9 %all-gather.55.cloned.1.call-start = ((), (), s32[]{:S(2)}) async-start(), calls=%async_computation.4 | async-start | bytes 14417920 | tf_op jit(solution)/shard_map/all_gather | solution.py:430
  306.6 210.1 %all-gather.57.cloned.1.call-start = ((), (), s32[]{:S(2)}) async-start(), calls=%async_computation.5 | async-start | bytes 7208960 | tf_op jit(solution)/shard_map/all_gather | solution.py:431
  310.4 290.6 %all-gather.59.cloned.1.call-start = ((), (), s32[]{:S(2)}) async-start(), calls=%async_computation.6 | async-start | bytes 15728640 | tf_op jit(solution)/shard_map/all_gather | solution.py:423
  311.2 696.8 %all-gather.61.cloned.1.call-start = ((), (), s32[]{:S(2)}) async-start(), calls=%async_computation.7 | async-start | bytes 2621440 | tf_op jit(solution)/shard_map/all_gather | solution.py:35
  609.4 5.0 collective-permute-start.1
  613.3 409.3 %copy-start.496 = (f32[8]{0:T(128)}, f32[8]{0:T(128)S(1)}, u32[]{:S(2)}) copy-start(f32[8]{0:T(128)S(1)} %exp.947) | copy-start | bytes 100
  623.0 380.2 %copy-start.5 = (bf16[1,256,8,128]{3,1,2,0:T(8,128)(2,1)}, bf16[1,256,8,128]{3,1,2,0:T(8,128)(2,1)S(1)}, u32[]{:S(2)}) copy-start(bf16[1,256,8,128]{3,1,2,0:T(8,128)(2,1)S(1)} %fusion.526) | copy-start | bytes 1572868
  807.9 200.0 %all-gather.63.cloned.1.call-start = ((), (), s32[]{:S(2)}) async-start(), calls=%async_computation.8 | async-start | bytes 5242880 | tf_op jit(solution)/shard_map/all_gather | solution.py:35
  810.3 233.9 %all-gather.65.cloned.1.call-start = ((), (), s32[]{:S(2)}) async-start(), calls=%async_computation.9 | async-start | bytes 5242880 | tf_op jit(solution)/shard_map/all_gather | solution.py:429
  810.9 238.4 %all-gather.67.cloned.1.call-start = ((), (), s32[]{:S(2)}) async-start(), calls=%async_computation.10 | async-start | bytes 14417920 | tf_op jit(solution)/shard_map/all_gather | solution.py:430
  811.6 248.0 %all-gather.69.cloned.1.call-start = ((), (), s32[]{:S(2)}) async-start(), calls=%async_computation.11 | async-start | bytes 7208960 | tf_op jit(solution)/shard_map/all_gather | solution.py:431
  812.2 593.4 %all-gather.71.cloned.1.call-start = ((), (), s32[]{:S(2)}) async-start(), calls=%async_computation.12 | async-start | bytes 1310720 | tf_op jit(solution)/shard_map/all_gather | solution.py:51
  1004.1 401.4 %all-gather.73.cloned.1.call-start = ((), (), s32[]{:S(2)}) async-start(), calls=%async_computation.13 | async-start | bytes 2621440 | tf_op jit(solution)/shard_map/all_gather | solution.py:51
  1121.0 627.5 %all-gather.75.cloned.1.call-start = ((), (), s32[]{:S(2)}) async-start(), calls=%async_computation.14 | async-start | bytes 1310720 | tf_op jit(solution)/shard_map/all_gather | solution.py:51
  1256.5 491.9 %all-gather.77.cloned.1.call-start = ((), (), s32[]{:S(2)}) async-start(), calls=%async_computation.15 | async-start | bytes 2621440 | tf_op jit(solution)/shard_map/all_gather | solution.py:51
  1543.5 8.3 collective-permute-start.2
  1685.3 968.6 %all-reduce.107.cloned.1.call-start = ((), (), s32[]{:S(2)}) async-start(), calls=%async_computation.18 | async-start | bytes 68298752
  1838.6 247.2 %collective-permute-start.3 = (bf16[1,3,4096]{2,1,0:T(4,128)(2,1)S(1)}, bf16[1,3,4096]{2,1,0:T(4,128)(2,1)S(1)}, u32[]{:S(2)}, u32[]{:S(2)}) collective-permute-start(bf16[1,3,4096]{2,1,0:T(4,128)(2,1)S(1)} %slice.931), channel_id=1, source_target_pairs={{1,0},{2,1},{3,2},{5,4},{6,5},{7,6},{9,8},{10,9},{11,10},{13,12},{... | collective-permute-start | bytes 73736 | tf_op jit(solution)/shard_map/ppermute | solution.py:30
  2082.7 1141.9 %all-reduce.105.cloned.1.call-start = ((), (), s32[]{:S(2)}) async-start(), calls=%async_computation.17 | async-start | bytes 68298752
  2383.2 3031.1 %all-gather.79.cloned.1.call-start = ((), (), s32[]{:S(2)}) async-start(), calls=%async_computation.16 | async-start | bytes 38421504 | tf_op jit(solution)/shard_map/all_gather | solution.py:468
  (540 other events, 8167.1 us)
Sparse Core Ops, SparseCore 0:
  13.7 85.1 all-gather.46
  296.9 24.7 all-gather.48
  323.2 34.4 all-gather.50
  359.1 34.4 all-gather.52
  395.6 76.1 all-gather.54
  473.2 43.3 all-gather.56
  518.8 82.1 all-gather.58
  808.0 22.7 all-gather.60
  832.4 34.5 all-gather.62
  868.4 34.8 all-gather.64
  904.9 76.2 all-gather.66
  982.6 43.6 all-gather.68
  1027.8 16.7 all-gather.70
  1121.1 22.9 all-gather.72
  1256.6 16.9 all-gather.74
  1685.4 24.6 all-gather.76
  2082.9 571.0 all-reduce.106
  2656.3 568.3 all-reduce.104
  4767.9 646.3 all-gather.78
where the time goes:
time: 5670 us; the launch traced here: 5630 us
  waiting for transfers between devices  1540 us (27%)
  local copies, waits for them, and re-layouts  1350 us (24%)
  blocking collectives  1350 us (24%)
  other arithmetic  833 us (15%)
  matrix products  518 us (9%)
    unnamed x2, blocking collectives  1310 us
    unnamed x1159, local copies, waits for them, and re-layouts  792 us
    another operation x21, other arithmetic, span_pass(): lax.linalg.triangular_solve(system, right_side, left_side=True, lower=Tru...  651 us
    unnamed x21, waiting for transfers between devices  642 us
    all_gather x1, waiting for transfers between devices, per_device(): lax.all_gather(joined.astype(jnp.bfloat16), 'rep', axis=0, tiled=True)  638 us
    all_gather x2, waiting for transfers between devices, per_device(): lax.all_gather(w_in[layer_index], 'grp', axis=0, tiled=True)  126 us
    another operation x10, local copies, waits for them, and re-layouts, pack_rows(): pieces.append(jnp.moveaxis(split, split_dim, 0).reshape(parts, -1))  116 us
  transfers between devices with their start and end apart: 23, of which 9 were waited for; matrix products, arithmetic and copies ran while one was open for 31% of the time, Pallas kernels for 0%

commit v1 on v0

v1 whole, which is shorter than its diff:
```python
from functools import partial
import math

import jax
import jax.numpy as jnp
from jax import lax
from jax.sharding import PartitionSpec as P
from jax.experimental import pallas as pl
from jax.experimental.pallas import tpu as pltpu

H = 8
DK = 128
DV = 256
FF = 2816
CONV = 4
LAYERS = 2
HK = 1024
HV = 2048
CH = 4096
CHUNK = 128

f32 = jnp.float32
bf16 = jnp.bfloat16
HIGH = lax.Precision.HIGHEST
epsilon = 1e-06
out_floor = 0.02
NN = ((1,), (0,))
NT = ((1,), (1,))
TN = ((0,), (0,))


def mm(left, right, dims=NN, precision=None):
    return lax.dot_general(
        left, right, (dims, ((), ())), precision=precision, preferred_element_type=f32
    )


def mh(left, right, dims=NN):
    return mm(left, right, dims, HIGH)


def grid_of(shape, dim):
    return lax.broadcasted_iota(jnp.int32, shape, dim)


def conv_chunk(x_ext, taps):
    return sum(x_ext[5 + j : 5 + j + CHUNK] * taps[j : j + 1] for j in range(CONV))


def decay_chunk(small, heads_ref):
    lane = grid_of(small.shape, 1)
    strength = jax.nn.sigmoid(small)
    shifted_logit = small + heads_ref[1:2, :]
    soft = jnp.maximum(shifted_logit, 0.0) + jnp.log1p(jnp.exp(-jnp.abs(shifted_logit)))
    log_decay = -jnp.exp(heads_ref[0:1, :]) * soft
    row = grid_of((CHUNK, CHUNK), 0)
    col = grid_of((CHUNK, CHUNK), 1)
    lower_ones = jnp.where(row >= col, 1.0, 0.0).astype(f32)
    cumulative = mh(lower_ones, log_decay)
    turned = jnp.where(lane < 2, strength, cumulative).T
    return strength, shifted_logit, log_decay, cumulative, turned


def head_inputs(activated, h):
    qa = activated[:, 128 * h : 128 * h + 128]
    ka = activated[:, 256 + 128 * h : 384 + 128 * h]
    va = activated[:, 512 + 256 * h : 768 + 256 * h]
    q_norm = lax.rsqrt(jnp.sum(qa * qa, axis=-1, keepdims=True) + epsilon)
    k_norm = lax.rsqrt(jnp.sum(ka * ka, axis=-1, keepdims=True) + epsilon)
    q = (qa * q_norm * (1.0 / math.sqrt(DK))).astype(bf16)
    k = (ka * k_norm).astype(bf16)
    return qa, ka, q_norm, k_norm, q, k, va.astype(bf16)


def unit_inverse(system):
    size = system.shape[0]
    row = grid_of((size, size), 0)
    col = grid_of((size, size), 1)
    eye = jnp.where(row == col, 1.0, 0.0).astype(f32)
    powers = jnp.where((row >> 3) == (col >> 3), -system, 0.0)
    square = mh(powers, powers)
    total = eye + powers
    total = total + mh(total, square)
    total = total + mh(total, mh(square, square))
    for bits in (3, 4, 5, 6):
        joint = ((row >> (bits + 1)) == (col >> (bits + 1))) & ((row >> bits) != (col >> bits))
        link = jnp.where(joint, system, 0.0)
        total = total - mh(total, mh(link, total))
    return total


def mixer_forward_kernel(
    proj_ref, small_ref, taps_ref, heads_ref, gain_ref,
    gated_ref, start_ref, inv_ref, pseudo_ref, mixed_ref,
    halo, state,
):
    halo[...] = jnp.zeros_like(halo)
    state[...] = jnp.zeros_like(state)
    row = grid_of((CHUNK, CHUNK), 0)
    col = grid_of((CHUNK, CHUNK), 1)

    def body(c, carry):
        rows = pl.ds(pl.multiple_of(c * CHUNK, CHUNK), CHUNK)
        x = proj_ref[rows, 0:1024].astype(f32)
        x_ext = jnp.concatenate([halo[...], x], axis=0)
        halo[...] = x[CHUNK - 8 :]
        convolved = conv_chunk(x_ext, taps_ref[...])
        activated = convolved * jax.nn.sigmoid(convolved)
        strength, shifted_logit, log_decay, cumulative, turned = decay_chunk(
            small_ref[rows, :], heads_ref
        )
        parts = []
        systems = []
        for h in range(2):
            qa, ka, q_norm, k_norm, q, k, v = head_inputs(activated, h)
            c_col = cumulative[:, 2 + h : 3 + h]
            c_row = turned[2 + h : 3 + h, :]
            beta_row = turned[h : h + 1, :]
            ratio = jnp.exp(jnp.where(row >= col, c_col - c_row, -1e4)) * beta_row
            systems.append(jnp.where(row > col, ratio * mm(k, k, NT), 0.0))
            mixing = ratio * mm(q, k, NT)
            parts.append((q, k, v, c_col, mixing))
        zero = jnp.zeros((CHUNK, CHUNK), f32)
        joint = jnp.concatenate(
            [
                jnp.concatenate([systems[0], zero], axis=1),
                jnp.concatenate([zero, systems[1]], axis=1),
            ],
            axis=0,
        )
        inverse = unit_inverse(joint)
        for h in range(2):
            q, k, v, c_col, mixing = parts[h]
            inv = inverse[128 * h : 128 * h + 128, 128 * h : 128 * h + 128]
            growth = jnp.exp(c_col)
            last = c_col[CHUNK - 1 :, :]
            before = state[h]
            start_ref[c, h] = before
            inv_ref[c, h] = inv
            read = mh(jnp.concatenate([q, k], axis=0).astype(f32), before)
            pseudo = mh(inv, v.astype(f32) - growth * read[CHUNK:])
            pseudo_ref[c, h] = pseudo
            mixed = growth * read[:CHUNK] + mh(mixing, pseudo)
            tail = jnp.exp(last - c_col) * strength[:, h : h + 1]
            state[h] = jnp.exp(last) * before + mh(k.astype(f32), tail * pseudo, TN)
            mixed_ref[rows, 256 * h : 256 * h + 256] = mixed
            gate = proj_ref[rows, 1024 + 256 * h : 1280 + 256 * h].astype(f32)
            scale = lax.rsqrt(jnp.mean(mixed * mixed, axis=-1, keepdims=True) + out_floor)
            gated = mixed * scale * gain_ref[0:1, :] * (gate * jax.nn.sigmoid(gate))
            gated_ref[rows, 256 * h : 256 * h + 256] = gated.astype(bf16)
        return carry

    lax.fori_loop(0, proj_ref.shape[0] // CHUNK, body, 0)


def mixer_forward(projected, small, taps, heads, gain):
    tokens = projected.shape[0]
    chunks = tokens // CHUNK
    vmem = pl.BlockSpec(memory_space=pltpu.VMEM)
    return pl.pallas_call(
        mixer_forward_kernel,
        out_shape=(
            jax.ShapeDtypeStruct((tokens, 512), bf16),
            jax.ShapeDtypeStruct((chunks, 2, DK, DV), f32),
            jax.ShapeDtypeStruct((chunks, 2, CHUNK, CHUNK), f32),
            jax.ShapeDtypeStruct((chunks, 2, CHUNK, DV), f32),
            jax.ShapeDtypeStruct((tokens, 512), f32),
        ),
        in_specs=[vmem] * 5,
        out_specs=(vmem,) * 5,
        scratch_shapes=[pltpu.VMEM((8, 1024), f32), pltpu.VMEM((2, DK, DV), f32)],
        compiler_params=pltpu.CompilerParams(vmem_limit_bytes=48 << 20),
        name="mixer_forward",
    )(projected, small, taps, heads, gain)


def mixer_backward_kernel(
    proj_ref, small_ref, taps_ref, heads_ref, gain_ref,
    start_ref, inv_ref, pseudo_ref, mixed_ref, dgated_ref,
    dproj_ref, dsmall_ref, gtaps_ref, gheads_ref,
    halo, dstate,
):
    halo[...] = jnp.zeros_like(halo)
    dstate[...] = jnp.zeros_like(dstate)
    gtaps_ref[...] = jnp.zeros_like(gtaps_ref)
    gheads_ref[...] = jnp.zeros_like(gheads_ref)
    row = grid_of((CHUNK, CHUNK), 0)
    col = grid_of((CHUNK, CHUNK), 1)
    lane = col
    token = grid_of((CHUNK, 1), 0)
    chunks = proj_ref.shape[0] // CHUNK

    def body(step, carry):
        c = chunks - 1 - step
        rows = pl.ds(pl.multiple_of(c * CHUNK, CHUNK), CHUNK)
        x = proj_ref[rows, 0:1024].astype(f32)
        before_rows = pl.ds(pl.multiple_of(jnp.maximum(c * CHUNK - 16, 0), 16), 16)
        x_before = proj_ref[before_rows, 0:1024].astype(f32)[8:]
        x_before = jnp.where(c > 0, x_before, 0.0)
        x_ext = jnp.concatenate([x_before, x], axis=0)
        convolved = conv_chunk(x_ext, taps_ref[...])
        sig = jax.nn.sigmoid(convolved)
        activated = convolved * sig
        strength, shifted_logit, log_decay, cumulative, turned = decay_chunk(
            small_ref[rows, :], heads_ref
        )
        d_strength = jnp.zeros((CHUNK, CHUNK), f32)
        d_cumulative = jnp.zeros((CHUNK, CHUNK), f32)
        d_q_parts, d_k_parts, d_v_parts = [], [], []
        gain_sum = jnp.zeros((1, DV), f32)
        for h in range(2):
            qa, ka, q_norm, k_norm, q, k, v = head_inputs(activated, h)
            cols = slice(256 * h, 256 * h + 256)
            mixed = mixed_ref[rows, cols]
            gate = proj_ref[rows, 1024 + 256 * h : 1280 + 256 * h].astype(f32)
            d_gated = dgated_ref[rows, cols].astype(f32)
            gate_sig = jax.nn.sigmoid(gate)
            gate_silu = gate * gate_sig
            scale = lax.rsqrt(jnp.mean(mixed * mixed, axis=-1, keepdims=True) + out_floor)
            scaled = mixed * scale
            gain = gain_ref[0:1, :]
            gain_sum = gain_sum + jnp.sum(d_gated * scaled * gate_silu, axis=0, keepdims=True)
            d_gate = d_gated * scaled * gain * (gate_sig * (1.0 + gate * (1.0 - gate_sig)))
            dproj_ref[rows, 1024 + 256 * h : 1280 + 256 * h] = d_gate.astype(bf16)
            d_scaled = d_gated * gain * gate_silu
            d_mixed = scale * (
                d_scaled - scaled * jnp.mean(d_scaled * scaled, axis=-1, keepdims=True)
            )
            c_col = cumulative[:, 2 + h : 3 + h]
            c_row = turned[2 + h : 3 + h, :]
            beta_row = turned[h : h + 1, :]
            beta_col = strength[:, h : h + 1]
            growth = jnp.exp(c_col)
            last = c_col[CHUNK - 1 :, :]
            ratio = jnp.exp(jnp.where(row >= col, c_col - c_row, -1e4))
            key_gram = mm(k, k, NT)
            query_gram = mm(q, k, NT)
            mixing = ratio * beta_row * query_gram
            fade = jnp.exp(last - c_col)
            tail = fade * beta_col
            start = start_ref[c, h]
            inv = inv_ref[c, h]
            pseudo = pseudo_ref[c, h]
            d_end = dstate[h]
            kf = k.astype(f32)
            qf = q.astype(f32)
            d_pseudo = mh(mixing, d_mixed, TN) + tail * mh(kf, d_end)
            d_right = mh(inv, d_pseudo, TN)
            pair = jnp.concatenate([d_mixed, d_right], axis=0)
            reads = mh(pair, jnp.concatenate([start, pseudo], axis=0), NT)
            read_q = reads[:CHUNK, :DK]
            read_k = reads[CHUNK:, :DK]
            read_u = mh(pseudo, d_end, NT)
            d_mixing = jnp.where(row >= col, reads[:CHUNK, DK:], 0.0) * ratio
            d_system = jnp.where(row > col, -reads[CHUNK:, DK:], 0.0) * ratio
            raw = d_mixing * query_gram + d_system * key_gram
            x_pair = jnp.concatenate([d_mixing * beta_row, d_system * beta_row], axis=0)
            by_row = mh(x_pair, kf)
            by_col = mh(x_pair, jnp.concatenate([qf, kf], axis=0), TN)
            d_q = growth * read_q + by_row[:CHUNK]
            d_k = by_row[CHUNK:] + by_col - growth * read_k + tail * read_u
            dstate[h] = jnp.exp(last) * d_end + mh(
                jnp.concatenate([growth * qf, -growth * kf], axis=0), pair, TN
            )
            u_dot = jnp.sum(read_u * kf, axis=-1, keepdims=True)
            col_raw = jnp.sum(raw, axis=0, keepdims=True)
            col_raw = jnp.broadcast_to(col_raw, (CHUNK, CHUNK)).T[:, 0:1]
            d_beta = col_raw + fade * u_dot
            d_cum = (
                jnp.sum(raw * beta_row, axis=-1, keepdims=True)
                - beta_col * col_raw
                + growth
                * (
                    jnp.sum(read_q * qf, axis=-1, keepdims=True)
                    - jnp.sum(read_k * kf, axis=-1, keepdims=True)
                )
                - tail * u_dot
            )
            at_last = jnp.sum(tail * u_dot, axis=0, keepdims=True) + jnp.exp(last) * jnp.sum(
                jnp.sum(start * d_end, axis=-1, keepdims=True), axis=0, keepdims=True
            )
            d_cum = d_cum + jnp.where(token == CHUNK - 1, at_last, 0.0)
            d_strength = jnp.where(lane == h, d_beta, d_strength)
            d_cumulative = jnp.where(lane == 2 + h, d_cum, d_cumulative)
            d_qn = d_q * (1.0 / math.sqrt(DK))
            qn = qa * q_norm
            kn = ka * k_norm
            d_q_parts.append(
                q_norm * (d_qn - qn * jnp.sum(d_qn * qn, axis=-1, keepdims=True))
            )
            d_k_parts.append(k_norm * (d_k - kn * jnp.sum(d_k * kn, axis=-1, keepdims=True)))
            d_v_parts.append(d_right)
        upper_ones = jnp.where(row <= col, 1.0, 0.0).astype(f32)
        d_log = mh(upper_ones, d_cumulative)
        d_shifted = d_log * (-jnp.exp(heads_ref[0:1, :])) * jax.nn.sigmoid(shifted_logit)
        d_small = jnp.where(lane < 2, d_strength * strength * (1.0 - strength), d_shifted)
        dsmall_ref[rows, :] = jnp.where(lane < 4, d_small, 0.0).astype(bf16)
        gheads_ref[0:1, :] += gain_sum
        gheads_ref[1:2, 0:128] += jnp.sum(d_log * log_decay, axis=0, keepdims=True)
        gheads_ref[2:3, 0:128] += jnp.sum(d_shifted, axis=0, keepdims=True)
        d_activated = jnp.concatenate(d_q_parts + d_k_parts + d_v_parts, axis=1)
        d_conv = d_activated * (sig * (1.0 + convolved * (1.0 - sig)))
        for j in range(CONV):
            gtaps_ref[j : j + 1, :] += jnp.sum(
                d_conv * x_ext[5 + j : 5 + j + CHUNK], axis=0, keepdims=True
            )
        d_ext = jnp.concatenate([d_conv, halo[...]], axis=0)
        d_x = sum(
            d_ext[CONV - 1 - j : CONV - 1 - j + CHUNK] * taps_ref[j : j + 1] for j in range(CONV)
        )
        halo[...] = d_conv[:8]
        dproj_ref[rows, 0:1024] = d_x.astype(bf16)
        return carry

    lax.fori_loop(0, chunks, body, 0)


def mixer_backward(projected, small, taps, heads, gain, saved, d_gated):
    tokens = projected.shape[0]
    vmem = pl.BlockSpec(memory_space=pltpu.VMEM)
    return pl.pallas_call(
        mixer_backward_kernel,
        out_shape=(
            jax.ShapeDtypeStruct((tokens, 1536), bf16),
            jax.ShapeDtypeStruct((tokens, 128), bf16),
            jax.ShapeDtypeStruct((8, 1024), f32),
            jax.ShapeDtypeStruct((8, DV), f32),
        ),
        in_specs=[vmem] * 10,
        out_specs=(vmem,) * 4,
        scratch_shapes=[pltpu.VMEM((8, 1024), f32), pltpu.VMEM((2, DK, DV), f32)],
        compiler_params=pltpu.CompilerParams(vmem_limit_bytes=48 << 20),
        name="mixer_backward",
    )(projected, small, taps, heads, gain, *saved, d_gated)


def rms_norm(residual, gain):
    scale = lax.rsqrt(jnp.mean(residual * residual, axis=-1, keepdims=True) + epsilon)
    return residual * scale * gain


def norm_back(residual, gain, d_out):
    scale = lax.rsqrt(jnp.mean(residual * residual, axis=-1, keepdims=True) + epsilon)
    unit = residual * scale
    d_unit = d_out * gain
    d_residual = scale * (d_unit - unit * jnp.mean(d_unit * unit, axis=-1, keepdims=True))
    return d_residual, jnp.sum(d_out * unit, axis=0)


def gather_rows(x):
    return lax.all_gather(x, "grp", axis=0, tiled=True)


def scatter_rows(x):
    return lax.psum_scatter(x.astype(bf16), "grp", scatter_dimension=0, tiled=True).astype(f32)


def dot(left, right, dims=NN):
    return mm(left, right, dims)


def per_device(
    x_input, norm_gain, w_in, w_ab, conv_w, a_log, dt_bias, out_gain, w_out, ffn_in, ffn_out,
    cotangent,
):
    parts = lax.axis_size("grp")
    replicas = lax.axis_size("rep")
    mine = lax.axis_index("grp")
    rows, width = x_input.shape[1], x_input.shape[2]
    gains = lax.all_gather(norm_gain, "grp", axis=2, tiled=True).astype(f32)
    taps_all = lax.all_gather(conv_w, "grp", axis=2, tiled=True).astype(f32)
    out_gains = lax.all_gather(out_gain, "grp", axis=1, tiled=True).astype(f32)
    ab_all = lax.all_gather(w_ab, "grp", axis=1, tiled=True)

    def own(array, start, size):
        return lax.dynamic_slice_in_dim(array, start + mine * size, size, array.ndim - 1)

    layers = []
    for l in range(LAYERS):
        pieces = jnp.stack(
            [
                jnp.concatenate(
                    [
                        w_in[l][:, 256 * t : 256 * t + 256],
                        w_in[l][:, HK + 256 * t : HK + 256 * t + 256],
                        w_in[l][:, 2 * HK + 512 * t : 2 * HK + 512 * t + 512],
                        w_in[l][:, CH + 512 * t : CH + 512 * t + 512],
                    ],
                    axis=1,
                )
                for t in range(4)
            ]
        )
        in_weight = lax.all_to_all(pieces, "grp", 0, 0).reshape(width, 1536)
        pieces = jnp.stack(
            [
                jnp.concatenate(
                    [ffn_in[l][:, 704 * t : 704 * t + 704], ffn_in[l][:, FF + 704 * t : FF + 704 * t + 704]],
                    axis=1,
                )
                for t in range(4)
            ]
        )
        up_weight = lax.all_to_all(pieces, "grp", 0, 0).reshape(width, 1408)
        ab = jnp.concatenate([own(ab_all[l], 0, 2), own(ab_all[l], H, 2)], axis=1)
        ab = jnp.pad(ab, ((0, 0), (0, 124)))
        taps = jnp.concatenate(
            [own(taps_all[l], 0, 256), own(taps_all[l], HK, 256), own(taps_all[l], 2 * HK, 512)], axis=1
        )
        taps = jnp.pad(taps, ((0, 4), (0, 0)))
        heads = jnp.pad(
            jnp.stack([a_log[l], dt_bias[l]]).astype(f32), ((0, 6), (2, 124))
        )
        gain = jnp.pad(out_gains[l][None], ((0, 7), (0, 0)))
        layers.append((gains[l], in_weight, ab, taps, heads, gain, w_out[l], up_weight, ffn_out[l]))

    residual = x_input[0].astype(f32)
    kept = []
    for l in range(LAYERS):
        gain_pair, in_weight, ab, taps, heads, gain, out_weight, up_weight, down_weight = layers[l]
        normed = gather_rows(rms_norm(residual, gain_pair[0]).astype(bf16))
        projected = dot(normed, in_weight).astype(bf16)
        small = dot(normed, ab)
        gated, *saved = mixer_forward(projected, small, taps, heads, gain)
        residual_mid = residual + scatter_rows(dot(gated, out_weight))
        normed_two = gather_rows(rms_norm(residual_mid, gain_pair[1]).astype(bf16))
        up_part = dot(normed_two, up_weight)
        hidden = (jax.nn.silu(up_part[:, :704]) * up_part[:, 704:]).astype(bf16)
        residual_out = residual_mid + scatter_rows(dot(hidden, down_weight))
        kept.append((residual, normed, projected, small, gated, saved, residual_mid, normed_two, up_part, hidden))
        residual = residual_out
    block_output = residual.astype(bf16)[None]

    d_residual = cotangent[0].astype(f32)
    big = [None] * LAYERS
    small_grads = [None] * LAYERS
    for l in reversed(range(LAYERS)):
        gain_pair, in_weight, ab, taps, heads, gain, out_weight, up_weight, down_weight = layers[l]
        residual, normed, projected, small, gated, saved, residual_mid, normed_two, up_part, hidden = kept[l]
        d_down = gather_rows(d_residual.astype(bf16))
        g_down = dot(hidden, d_down, TN).astype(bf16)
        d_hidden = dot(d_down, down_weight, NT)
        gate, up = up_part[:, :704], up_part[:, 704:]
        sig = jax.nn.sigmoid(gate)
        d_up = jnp.concatenate(
            [d_hidden * up * (sig * (1.0 + gate * (1.0 - sig))), d_hidden * gate * sig], axis=1
        ).astype(bf16)
        g_up = dot(normed_two, d_up, TN).astype(bf16)
        d_normed_two = scatter_rows(dot(d_up, up_weight, NT))
        d_norm, g_gain_two = norm_back(residual_mid, gain_pair[1], d_normed_two)
        d_mid = d_residual + d_norm
        d_branch = gather_rows(d_mid.astype(bf16))
        g_out = dot(gated, d_branch, TN).astype(bf16)
        d_gated = dot(d_branch, out_weight, NT).astype(bf16)
        d_projected, d_small, g_taps, g_heads = mixer_backward(
            projected, small, taps, heads, gain, saved, d_gated
        )
        g_in = dot(normed, d_projected, TN).astype(bf16)
        g_ab = dot(normed, d_small, TN)[:, :4]
        d_normed = scatter_rows(dot(d_projected, in_weight, NT) + dot(d_small, ab, NT))
        d_norm, g_gain_one = norm_back(residual, gain_pair[0], d_normed)
        d_residual = d_mid + d_norm
        small_grads[l] = (g_gain_one, g_gain_two, g_ab, g_taps, g_heads)
        big[l] = (g_in, g_up, g_out, g_down)
    input_grad = d_residual.astype(bf16)[None]

    w_in_grads, up_grads, out_grads, down_grads = [], [], [], []
    for l in range(LAYERS):
        g_in, g_up, g_out, g_down = big[l]

        def columns(grad):
            part = rows // replicas
            grad = grad.reshape(parts, replicas, part, grad.shape[1])
            grad = lax.psum_scatter(jnp.moveaxis(grad, 1, 0), "rep", scatter_dimension=0, tiled=False)
            grad = lax.all_to_all(grad, "grp", 0, 0)
            grad = lax.all_gather(grad, "rep", axis=0)
            return jnp.moveaxis(grad, 1, 0).reshape(parts, rows, -1)

        def plain(grad):
            grad = lax.psum_scatter(grad, "rep", scatter_dimension=0, tiled=True)
            return lax.all_gather(grad, "rep", axis=0, tiled=True)

        blocks = columns(g_in)
        w_in_grads.append(
            jnp.concatenate(
                [blocks[t][:, 0:256] for t in range(4)]
                + [blocks[t][:, 256:512] for t in range(4)]
                + [blocks[t][:, 512:1024] for t in range(4)]
                + [blocks[t][:, 1024:1536] for t in range(4)],
                axis=1,
            ).astype(f32)
        )
        blocks = columns(g_up)
        up_grads.append(
            jnp.concatenate(
                [blocks[t][:, :704] for t in range(4)] + [blocks[t][:, 704:] for t in range(4)], axis=1
            ).astype(f32)
        )
        joint = plain(jnp.concatenate([g_out, g_down], axis=0))
        out_grads.append(joint[:512].astype(f32))
        down_grads.append(joint[512:].astype(f32))

    def spread(piece, full, at):
        zero = jnp.zeros(piece.shape[:-1] + (full,), f32)
        return lax.dynamic_update_slice_in_dim(zero, piece, at, piece.ndim - 1)

    packed = []
    for l in range(LAYERS):
        g_gain_one, g_gain_two, g_ab, g_taps, g_heads = small_grads[l]
        packed.append(g_gain_one)
        packed.append(g_gain_two)
        packed.append(g_heads[0])
        packed.append(spread(g_heads[1, 2:4], H, 2 * mine))
        packed.append(spread(g_heads[2, 2:4], H, 2 * mine))
        packed.append(spread(g_taps[:4, :256], HK, 256 * mine))
        packed.append(spread(g_taps[:4, 256:512], HK, 256 * mine))
        packed.append(spread(g_taps[:4, 512:], HV, 512 * mine))
        packed.append(spread(g_ab[:, :2], H, 2 * mine))
        packed.append(spread(g_ab[:, 2:], H, 2 * mine))
    flat = lax.psum(jnp.concatenate([piece.reshape(-1) for piece in packed]), ("rep", "grp"))
    sums, at = [], 0
    for piece in packed:
        sums.append(flat[at : at + piece.size].reshape(piece.shape))
        at += piece.size
    per_layer = [sums[10 * l : 10 * l + 10] for l in range(LAYERS)]

    def owned(array, dim):
        size = array.shape[dim] // parts
        return lax.dynamic_slice_in_dim(array, mine * size, size, dim)

    grad_gain = owned(jnp.stack([jnp.stack([p[0], p[1]]) for p in per_layer]), 2)
    grad_out_gain = owned(jnp.stack([p[2] for p in per_layer]), 1)
    grad_a_log = owned(jnp.stack([p[3] for p in per_layer]), 1)
    grad_dt = owned(jnp.stack([p[4] for p in per_layer]), 1)
    grad_conv = owned(jnp.stack([jnp.concatenate(p[5:8], axis=1) for p in per_layer]), 2)
    grad_ab = owned(jnp.stack([jnp.concatenate(p[8:10], axis=1) for p in per_layer]), 1)
    return (
        block_output,
        input_grad,
        grad_gain,
        jnp.stack(w_in_grads),
        grad_ab,
        grad_conv,
        grad_a_log,
        grad_dt,
        grad_out_gain,
        jnp.stack(out_grads),
        jnp.stack(up_grads),
        jnp.stack(down_grads),
    )


def solution(mesh):
    rows = P("rep", "grp", None)
    first = P(None, "grp")
    middle = P(None, "grp", None)
    last = P(None, None, "grp")
    in_specs = (rows, last, middle, middle, last, first, first, first, middle, middle, middle, rows)
    out_specs = (rows, rows, last, middle, middle, last, first, first, first, middle, middle, middle)
    return jax.shard_map(
        per_device, mesh=mesh, in_specs=in_specs, out_specs=out_specs, check_vma=False
    )
```

time: 5670 us -> 1910 us (0.34)
  local copies, waits for them, and re-layouts: 1350 us -> 116 us
  blocking collectives: 1350 us -> 187 us
  other arithmetic: 833 us -> 79 us
  waiting for transfers between devices: 1540 us -> 1130 us
  matrix products: 518 us -> 125 us
  Pallas kernels: 0 us -> 229 us
    unnamed x2 -> x0, blocking collectives: 1310 us -> none
    unnamed x1159 -> x201, local copies, waits for them, and re-layouts: 792 us -> 16.4 us
    another operation x56 -> x36, other arithmetic: 705 us -> 40.5 us  [the longest x10 10.4 us: per_device(): jnp.stack([jnp.concatenate([w_in[l][:, 256 * t:256 * t + 256], w_in[l][:,...]
    all_gather x17 -> x14, waiting for transfers between devices: 902 us -> 319 us  [the longest x4 188 us: columns(): grad = lax.all_gather(grad, 'rep', axis=0)]
    dot_general x260 -> x30, matrix products: 464 us -> 125 us  [mm(): lax.dot_general(left, right, (dims, ((), ())), precision=precision, prefe...]
    reduce_scatter x0 -> x10, waiting for transfers between devices: none -> 260 us  [the longest x8 204 us: scatter_rows(): lax.psum_scatter(x.astype(bf16), 'grp', scatter_dimension=0, tiled=True)]
    unnamed x21 -> x27, waiting for transfers between devices: 642 us -> 388 us
    pallas_call x0 -> x4, Pallas kernels: none -> 229 us  [the longest x2 138 us: mixer_forward(): pl.pallas_call(mixer_forward_kernel, out_shape=(jax.ShapeDtypeStruct((tok...]
  transfers between devices with their start and end apart: 23 -> 30, of which waited for: 9 -> 21; matrix products, arithmetic and copies ran while one was open for 31% -> 11% of each run, Pallas kernels for 0% -> 2%
where the time goes in v1:
time: 1910 us
  waiting for transfers between devices  1130 us (59%)
  Pallas kernels  229 us (12%)
  blocking collectives  187 us (10%)
  matrix products  125 us (7%)
  local copies, waits for them, and re-layouts  116 us (6%)
  other arithmetic  79 us (4%)
    unnamed x27, waiting for transfers between devices  388 us
    reduce_scatter x8, waiting for transfers between devices, scatter_rows(): lax.psum_scatter(x.astype(bf16), 'grp', scatter_dimension=0, tiled=True)  204 us
    all_gather x4, waiting for transfers between devices, columns(): grad = lax.all_gather(grad, 'rep', axis=0)  188 us
    pallas_call x2, Pallas kernels, mixer_forward(): pl.pallas_call(mixer_forward_kernel, out_shape=(jax.ShapeDtypeStruct((tok...  138 us
    dot_general x30, matrix products, mm(): lax.dot_general(left, right, (dims, ((), ())), precision=precision, prefe...  125 us
    psum x1, waiting for transfers between devices, per_device(): lax.psum(jnp.concatenate([piece.reshape(-1) for piece in packed]), ('rep'...  122 us
    all_to_all x2, blocking collectives, per_device(): up_weight = lax.all_to_all(pieces, 'grp', 0, 0).reshape(width, 1408)  104 us
    pallas_call x2, Pallas kernels, mixer_backward(): pl.pallas_call(mixer_backward_kernel, out_shape=(jax.ShapeDtypeStruct((to...  90.9 us
  transfers between devices with their start and end apart: 30, of which 21 were waited for; matrix products, arithmetic and copies ran while one was open for 11% of the time, Pallas kernels for 2%

profile of v1, /device:TPU:0, one launch (start us, length us, event | category | flops | bytes accessed | tf_op | source)
XLA Modules:
  0.0 1905.8 jit_solution(12101316666252431425)
XLA Ops:
  29.2 45.8 %all-gather.5 = bf16[4,64,2]{1,2,0:T(2,128)(2,1)S(1)} all-gather(bf16[1,64,2]{1,2,0:T(2,128)(2,1)S(1)} %bitcast.565), channel_id=1, replica_groups=mesh['rep'=8,'grp'=4] {'grp'}, dimensions={0}, use_global_device_ids=true | all-gather | bytes 1280 | tf_op jit(solution)/shard_map/all_gather | solution.py:372
  96.2 69.2 %mixer_forward.2 = (bf16[1024,512]{1,0:T(8,128)(2,1)S(1)}, f32[8,2,128,256]{3,2,1,0:T(8,128)S(1)}, f32[8,2,128,128]{3,2,1,0:T(8,128)S(1)}, f32[8,2,128,256]{3,2,1,0:T(8,128)}, f32[1024,512]{1,0:T(8,128)}) custom-call(bf16[1024,1536]{1,0:T(8,128)(2,1)} %convolution_convert_fusion.5.proj_ref, f32[1024,128]{1,0:T(8,128)S(1)} %fusion.82.small_ref, ...), custom_call_target="tpu_custom_call" | custom-call | tf_op jit(solution)/shard_map/mixer_forward/pallas_call | solution.py:160
  178.4 23.2 %reduce-scatter.23.cloned.1.call-done = bf16[256,1024]{1,0:T(8,128)(2,1)} async-done(((bf16[1024,1024]{1,0:T(8,128)(2,1)}), bf16[256,1024]{1,0:T(8,128)(2,1)}) %reduce-scatter.23.cloned.1.call-update) | async-done | bytes 524304 | tf_op jit(solution)/shard_map/reduce_scatter | solution.py:355
  208.6 48.6 %all_to_all.40 = bf16[4,256,1408]{2,1,0:T(8,128)(2,1)} all-to-all(bf16[4,256,1408]{2,1,0:T(8,128)(2,1)S(1)} %pad_maximum_fusion.2), channel_id=1, replica_groups=mesh['rep'=8,'grp'=4] {'grp'}, dimensions={0} | all-to-all | bytes 5767168 | tf_op jit(solution)/shard_map/all_to_all | solution.py:404
  274.4 27.5 %reduce-scatter.25.cloned.1.call-done = bf16[256,1024]{1,0:T(8,128)(2,1)} async-done(((bf16[1024,1024]{1,0:T(8,128)(2,1)}), bf16[256,1024]{1,0:T(8,128)(2,1)}) %reduce-scatter.25.cloned.1.call-update) | async-done | bytes 524304 | tf_op jit(solution)/shard_map/reduce_scatter | solution.py:355
  315.8 44.6 %all-to-all-done.2 = bf16[4,256,1536]{2,1,0:T(8,128)(2,1)} async-done(((bf16[4,256,1536]{2,1,0:T(8,128)(2,1)}), bf16[4,256,1536]{2,1,0:T(8,128)(2,1)}, u32[]{:S(2)}, u32[]{:S(2)}) %all-to-all-start.2) | async-done | bytes 3145760 | tf_op jit(solution)/shard_map/all_to_all | solution.py:394
  368.9 69.1 %mixer_forward.3 = (bf16[1024,512]{1,0:T(8,128)(2,1)S(1)}, f32[8,2,128,256]{3,2,1,0:T(8,128)S(1)}, f32[8,2,128,128]{3,2,1,0:T(8,128)S(1)}, f32[8,2,128,256]{3,2,1,0:T(8,128)}, f32[1024,512]{1,0:T(8,128)}) custom-call(bf16[1024,1536]{1,0:T(8,128)(2,1)} %convolution_convert_fusion.4.proj_ref, f32[1024,128]{1,0:T(8,128)S(1)} %fusion.79.small_ref, ...), custom_call_target="tpu_custom_call" | custom-call | tf_op jit(solution)/shard_map/mixer_forward/pallas_call | solution.py:160
  443.9 31.5 %reduce-scatter.27.cloned.1.call-done = bf16[256,1024]{1,0:T(8,128)(2,1)} async-done(((bf16[1024,1024]{1,0:T(8,128)(2,1)}), bf16[256,1024]{1,0:T(8,128)(2,1)}) %reduce-scatter.27.cloned.1.call-update) | async-done | bytes 524304 | tf_op jit(solution)/shard_map/reduce_scatter | solution.py:355
  483.9 55.2 %all_to_all.41 = bf16[4,256,1408]{2,1,0:T(8,128)(2,1)} all-to-all(bf16[4,256,1408]{2,1,0:T(8,128)(2,1)S(1)} %pad_maximum_fusion.3), channel_id=1, replica_groups=mesh['rep'=8,'grp'=4] {'grp'}, dimensions={0} | all-to-all | bytes 5767168 | tf_op jit(solution)/shard_map/all_to_all | solution.py:404
  539.1 8.5 fusion.174
  547.6 7.8 multiply_convert_fusion.3
  561.8 31.5 %reduce-scatter.31.cloned.1.call-done = bf16[256,1024]{1,0:T(8,128)(2,1)} async-done(((bf16[1024,1024]{1,0:T(8,128)(2,1)}), bf16[256,1024]{1,0:T(8,128)(2,1)}) %reduce-scatter.31.cloned.1.call-update) | async-done | bytes 524304 | tf_op jit(solution)/shard_map/reduce_scatter | solution.py:355
  599.1 22.5 %all-gather.29.cloned.1.call-done = bf16[1024,1024]{1,0:T(8,128)(2,1)} async-done(((bf16[256,1024]{1,0:T(8,128)(2,1)}), bf16[1024,1024]{1,0:T(8,128)(2,1)}) %all-gather.29.cloned.1.call-update) | async-done | bytes 2097168 | tf_op jit(solution)/shard_map/all_gather | solution.py:351
  624.9 45.3 %mixer_backward.2 = (bf16[1024,1536]{1,0:T(8,128)(2,1)}, bf16[1024,128]{1,0:T(8,128)(2,1)S(1)}, f32[8,1024]{1,0:T(8,128)S(1)}, f32[8,256]{1,0:T(8,128)S(1)}) custom-call(bf16[1024,1536]{1,0:T(8,128)(2,1)} %convolution_convert_fusion.4.proj_ref, f32[1024,128]{1,0:T(8,128)S(1)} %fusion.79.small_ref, f32[8,1024]{1,0:T(8,128)S(1)} %select_maximum_fusion.taps_ref, ...), custom_call_target="tpu_custom_call" | custom-call | tf_op jit(solution)/shard_map/mixer_backward/pallas_call | solution.py:321
  683.7 26.4 %reduce-scatter.33.cloned.1.call-done = bf16[256,1024]{1,0:T(8,128)(2,1)} async-done(((bf16[1024,1024]{1,0:T(8,128)(2,1)}), bf16[256,1024]{1,0:T(8,128)(2,1)}) %reduce-scatter.33.cloned.1.call-update) | async-done | bytes 524304 | tf_op jit(solution)/shard_map/reduce_scatter | solution.py:355
  712.0 32.2 %reduce-scatter.29.cloned.1.call-done = bf16[256,1024]{1,0:T(8,128)(2,1)} async-done(((bf16[1024,1024]{1,0:T(8,128)(2,1)}), bf16[256,1024]{1,0:T(8,128)(2,1)}) %reduce-scatter.29.cloned.1.call-update) | async-done | bytes 524304 | tf_op jit(solution)/shard_map/reduce_scatter | solution.py:355
  748.3 22.5 %all-gather.31.cloned.1.call-done = bf16[1024,1024]{1,0:T(8,128)(2,1)} async-done(((bf16[256,1024]{1,0:T(8,128)(2,1)}), bf16[1024,1024]{1,0:T(8,128)(2,1)}) %all-gather.31.cloned.1.call-update) | async-done | bytes 2097168 | tf_op jit(solution)/shard_map/all_gather | solution.py:351
  783.8 31.5 %reduce-scatter.35.cloned.1.call-done = bf16[256,1024]{1,0:T(8,128)(2,1)} async-done(((bf16[1024,1024]{1,0:T(8,128)(2,1)}), bf16[256,1024]{1,0:T(8,128)(2,1)}) %reduce-scatter.35.cloned.1.call-update) | async-done | bytes 524304 | tf_op jit(solution)/shard_map/reduce_scatter | solution.py:355
  827.3 15.3 all-gather.33.cloned.1.call-done
  845.9 45.6 %mixer_backward.3 = (bf16[1024,1536]{1,0:T(8,128)(2,1)}, bf16[1024,128]{1,0:T(8,128)(2,1)S(1)}, f32[8,1024]{1,0:T(8,128)S(1)}, f32[8,256]{1,0:T(8,128)S(1)}) custom-call(bf16[1024,1536]{1,0:T(8,128)(2,1)} %convolution_convert_fusion.5.proj_ref, f32[1024,128]{1,0:T(8,128)S(1)} %fusion.82.small_ref, f32[8,1024]{1,0:T(8,128)S(1)} %select_maximum_fusion.2.taps_ref, ...), custom_call_target="tpu_custom_call" | custom-call | tf_op jit(solution)/shard_map/mixer_backward/pallas_call | solution.py:321
  951.1 14.7 concatenate.247
  965.8 56.6 %reduce-scatter.39.cloned.1.call-done = bf16[152,1024]{1,0:T(8,128)(2,1)} async-done(((bf16[1216,1024]{1,0:T(8,128)(2,1)}), bf16[152,1024]{1,0:T(8,128)(2,1)}) %reduce-scatter.39.cloned.1.call-update) | async-done | bytes 311312 | tf_op jit(solution)/shard_map/reduce_scatter | solution.py:480
  1023.2 386.4 %all-reduce.18.cloned.1.call-done = (bf16[8,4,32,1536]{3,2,0,1:T(8,128)(2,1)}, bf16[8,4,32,1536]{3,2,0,1:T(8,128)(2,1)}, bf16[8,4,32,1408]{3,2,0,1:T(8,128)(2,1)}, bf16[8,4,32,1408]{3,2,0,1:T(8,128)(2,1)}) async-done(((bf16[8,4,32,1536]{3,2,0,1:T(8,128)(2,1)}, bf16[8,4,32,1536]{3,2,0,1:T(8,128)(2,1)}, bf16[8,4,32,1408]{3,2,0,1:T(8,128)(2,1)}, bf16[8,4,32,1408]{3,2,0,1:T(8,128)(2,1)}), ...) | async-done | bytes 12058640
  1411.3 10.2 all_to_all.42
  1423.2 10.2 all_to_all.43
  1439.4 24.4 %all-gather.37.cloned.1.call-done = bf16[1216,1024]{1,0:T(8,128)(2,1)} async-done(((bf16[152,1024]{1,0:T(8,128)(2,1)}), bf16[1216,1024]{1,0:T(8,128)(2,1)}) %all-gather.37.cloned.1.call-update) | async-done | bytes 2490384 | tf_op jit(solution)/shard_map/all_gather | solution.py:481
  1471.7 122.2 %all-reduce.16.cloned.1.call-done = f32[70176]{0:T(1024)} async-done(((f32[70176]{0:T(1024)}), f32[70176]{0:T(1024)}) %all-reduce.16.cloned.1.call-update) | async-done | bytes 280720 | tf_op jit(solution)/shard_map/psum | solution.py:520
  1604.2 46.4 %all-gather.35.cloned.1.call-done = bf16[1216,1024]{1,0:T(8,128)(2,1)} async-done(((bf16[152,1024]{1,0:T(8,128)(2,1)}), bf16[1216,1024]{1,0:T(8,128)(2,1)}) %all-gather.35.cloned.1.call-update) | async-done | bytes 2490384 | tf_op jit(solution)/shard_map/all_gather | solution.py:481
  1668.5 40.8 %all-gather.47.cloned.1.call-done = bf16[32,32,1408]{2,1,0:T(8,128)(2,1)} async-done(((bf16[4,32,1408]{2,1,0:T(8,128)(2,1)}), bf16[32,32,1408]{2,1,0:T(8,128)(2,1)}) %all-gather.47.cloned.1.call-update) | async-done | bytes 2883600 | tf_op jit(solution)/shard_map/all_gather | solution.py:476
  1715.4 52.5 %all-gather.45.cloned.1.call-done = bf16[32,32,1408]{2,1,0:T(8,128)(2,1)} async-done(((bf16[4,32,1408]{2,1,0:T(8,128)(2,1)}), bf16[32,32,1408]{2,1,0:T(8,128)(2,1)}) %all-gather.45.cloned.1.call-update) | async-done | bytes 2883600 | tf_op jit(solution)/shard_map/all_gather | solution.py:476
  1793.9 35.6 %all-gather.43.cloned.1.call-done = bf16[32,32,1536]{2,1,0:T(8,128)(2,1)} async-done(((bf16[4,32,1536]{2,1,0:T(8,128)(2,1)}), bf16[32,32,1536]{2,1,0:T(8,128)(2,1)}) %all-gather.43.cloned.1.call-update) | async-done | bytes 3145744 | tf_op jit(solution)/shard_map/all_gather | solution.py:476
  1831.9 58.9 %all-gather.41.cloned.1.call-done = bf16[32,32,1536]{2,1,0:T(8,128)(2,1)} async-done(((bf16[4,32,1536]{2,1,0:T(8,128)(2,1)}), bf16[32,32,1536]{2,1,0:T(8,128)(2,1)}) %all-gather.41.cloned.1.call-update) | async-done | bytes 3145744 | tf_op jit(solution)/shard_map/all_gather | solution.py:476
  (469 shorter events, 326.9 us)
Async XLA Ops:
  7.2 80.8 %all-gather.21.cloned.1.call-start = ((), (), s32[]{:S(2)}) async-start(), calls=%async_computation.18 | async-start | bytes 2621440 | tf_op jit(solution)/shard_map/all_gather | solution.py:351
  25.2 62.7 %all-to-all-start = ((bf16[4,256,1536]{2,1,0:T(8,128)(2,1)}), bf16[4,256,1536]{2,1,0:T(8,128)(2,1)S(1)}, u32[]{:S(2)}, u32[]{:S(2)}) async-start(bf16[4,256,1536]{2,1,0:T(8,128)(2,1)} %pad_maximum_fusion), calls=%async_computation | async-start | bytes 6291456 | tf_op jit(solution)/shard_map/all_to_all | solution.py:394
  29.1 172.5 %reduce-scatter.23.cloned.1.call-start = ((), (), s32[]{:S(2)}) async-start(), calls=%async_computation.19 | async-start | bytes 2621440 | tf_op jit(solution)/shard_map/reduce_scatter | solution.py:355
  170.0 87.2 %all-gather.23.cloned.1.call-start = ((), (), s32[]{:S(2)}) async-start(), calls=%async_computation.20 | async-start | bytes 2621440 | tf_op jit(solution)/shard_map/all_gather | solution.py:351
  205.0 97.0 %reduce-scatter.25.cloned.1.call-start = ((), (), s32[]{:S(2)}) async-start(), calls=%async_computation.21 | async-start | bytes 2621440 | tf_op jit(solution)/shard_map/reduce_scatter | solution.py:355
  270.3 90.1 %all-gather.25.cloned.1.call-start = ((), (), s32[]{:S(2)}) async-start(), calls=%async_computation.22 | async-start | bytes 2621440 | tf_op jit(solution)/shard_map/all_gather | solution.py:351
  309.7 50.7 %all-to-all-start.2 = ((bf16[4,256,1536]{2,1,0:T(8,128)(2,1)}), bf16[4,256,1536]{2,1,0:T(8,128)(2,1)}, u32[]{:S(2)}, u32[]{:S(2)}) async-start(bf16[4,256,1536]{2,1,0:T(8,128)(2,1)} %pad_maximum_fusion.1), calls=%async_computation.4 | async-start | bytes 6291456 | tf_op jit(solution)/shard_map/all_to_all | solution.py:394
  314.6 160.8 %reduce-scatter.27.cloned.1.call-start = ((), (), s32[]{:S(2)}) async-start(), calls=%async_computation.23 | async-start | bytes 2621440 | tf_op jit(solution)/shard_map/reduce_scatter | solution.py:355
  368.2 73.1 %copy-start.73 = (bf16[2,512,1024]{2,1,0:T(8,128)(2,1)S(1)}, bf16[2,512,1024]{2,1,0:T(8,128)(2,1)}, u32[]{:S(2)}) copy-start(bf16[2,512,1024]{2,1,0:T(8,128)(2,1)} %param.20) | copy-start | bytes 6291460
  443.9 95.3 %all-gather.27.cloned.1.call-start = ((), (), s32[]{:S(2)}) async-start(), calls=%async_computation.24 | async-start | bytes 2621440 | tf_op jit(solution)/shard_map/all_gather | solution.py:351
  479.4 68.3 %all-gather.39.cloned.1.call-start = ((), (), s32[]{:S(2)}) async-start(), calls=%async_computation.38 | async-start | bytes 2621440 | tf_op jit(solution)/shard_map/all_gather | solution.py:351
  480.1 113.3 %reduce-scatter.31.cloned.1.call-start = ((), (), s32[]{:S(2)}) async-start(), calls=%async_computation.26 | async-start | bytes 2621440 | tf_op jit(solution)/shard_map/reduce_scatter | solution.py:355
  561.8 59.8 %all-gather.29.cloned.1.call-start = ((), (), s32[]{:S(2)}) async-start(), calls=%async_computation.27 | async-start | bytes 2621440 | tf_op jit(solution)/shard_map/all_gather | solution.py:351
  598.9 111.3 %reduce-scatter.33.cloned.1.call-start = ((), (), s32[]{:S(2)}) async-start(), calls=%async_computation.28 | async-start | bytes 2621440 | tf_op jit(solution)/shard_map/reduce_scatter | solution.py:355
  678.6 65.6 %reduce-scatter.29.cloned.1.call-start = ((), (), s32[]{:S(2)}) async-start(), calls=%async_computation.25 | async-start | bytes 2621440 | tf_op jit(solution)/shard_map/reduce_scatter | solution.py:355
  683.7 87.1 %all-gather.31.cloned.1.call-start = ((), (), s32[]{:S(2)}) async-start(), calls=%async_computation.29 | async-start | bytes 2621440 | tf_op jit(solution)/shard_map/all_gather | solution.py:351
  748.1 67.3 %reduce-scatter.35.cloned.1.call-start = ((), (), s32[]{:S(2)}) async-start(), calls=%async_computation.30 | async-start | bytes 2621440 | tf_op jit(solution)/shard_map/reduce_scatter | solution.py:355
  783.8 58.8 %all-gather.33.cloned.1.call-start = ((), (), s32[]{:S(2)}) async-start(), calls=%async_computation.31 | async-start | bytes 2621440 | tf_op jit(solution)/shard_map/all_gather | solution.py:351
  819.9 108.7 %reduce-scatter.41.cloned.1.call-start = ((), (), s32[]{:S(2)}) async-start(), calls=%async_computation.36 | async-start | bytes 2801664 | tf_op jit(solution)/shard_map/reduce_scatter | solution.py:480
  826.8 122.1 %reduce-scatter.37.cloned.1.call-start = ((), (), s32[]{:S(2)}) async-start(), calls=%async_computation.32 | async-start | bytes 2621440 | tf_op jit(solution)/shard_map/reduce_scatter | solution.py:355
  898.9 123.6 %reduce-scatter.39.cloned.1.call-start = ((), (), s32[]{:S(2)}) async-start(), calls=%async_computation.34 | async-start | bytes 2801664 | tf_op jit(solution)/shard_map/reduce_scatter | solution.py:480
  905.4 504.1 %all-reduce.18.cloned.1.call-start = ((), (), s32[]{:S(2)}) async-start(), calls=%async_computation.43 | async-start | bytes 24117248
  928.5 535.3 %all-gather.37.cloned.1.call-start = ((), (), s32[]{:S(2)}) async-start(), calls=%async_computation.37 | async-start | bytes 2801664 | tf_op jit(solution)/shard_map/all_gather | solution.py:481
  929.1 664.9 %all-reduce.16.cloned.1.call-start = ((), (), s32[]{:S(2)}) async-start(), calls=%async_computation.33 | async-start | bytes 565248 | tf_op jit(solution)/shard_map/psum | solution.py:520
  945.6 76.9 %copy-start.75 = (u32[32]{0:T(128)S(1)}, u32[32]{0:T(128)}, u32[]{:S(2)}) copy-start(u32[32]{0:T(128)} %constant.89) | copy-start | bytes 388
  965.8 684.8 %all-gather.35.cloned.1.call-start = ((), (), s32[]{:S(2)}) async-start(), calls=%async_computation.35 | async-start | bytes 2801664 | tf_op jit(solution)/shard_map/all_gather | solution.py:481
  1022.4 686.9 %all-gather.47.cloned.1.call-start = ((), (), s32[]{:S(2)}) async-start(), calls=%async_computation.42 | async-start | bytes 3244032 | tf_op jit(solution)/shard_map/all_gather | solution.py:476
  1421.5 346.5 %all-gather.45.cloned.1.call-start = ((), (), s32[]{:S(2)}) async-start(), calls=%async_computation.41 | async-start | bytes 3244032 | tf_op jit(solution)/shard_map/all_gather | solution.py:476
  1435.9 30.2 %all-to-all-start.5 = ((bf16[4,32,1536]{2,1,0:T(8,128)(2,1)}), bf16[4,32,1536]{2,1,0:T(8,128)(2,1)S(1)}, u32[]{:S(2)}, u32[]{:S(2)}) async-start(bf16[4,32,1536]{2,1,0:T(8,128)(2,1)} %dynamic-slice_bitcast_fusion), calls=%async_computation.13 | async-start | bytes 786432 | tf_op jit(solution)/shard_map/all_to_all | solution.py:475
  1439.4 390.1 %all-gather.43.cloned.1.call-start = ((), (), s32[]{:S(2)}) async-start(), calls=%async_computation.40 | async-start | bytes 3538944 | tf_op jit(solution)/shard_map/all_gather | solution.py:476
  1656.8 10.9 all-to-all-start.4
  1660.3 230.5 %all-gather.41.cloned.1.call-start = ((), (), s32[]{:S(2)}) async-start(), calls=%async_computation.39 | async-start | bytes 3538944 | tf_op jit(solution)/shard_map/all_gather | solution.py:476
  (80 other events, 1054.0 us)
Sparse Core Ops, SparseCore 0:
  17.5 32.3 all-gather.20
  170.1 31.4 reduce-scatter.22
  205.1 33.8 all-gather.22
  270.4 31.4 reduce-scatter.24
  305.5 31.4 all-gather.24
  444.0 31.3 reduce-scatter.26
  479.5 32.6 all-gather.26
  513.8 30.4 all-gather.38
  561.9 31.4 reduce-scatter.30
  599.0 22.5 all-gather.28
  678.7 31.4 reduce-scatter.32
  712.7 31.4 reduce-scatter.28
  748.2 22.5 all-gather.30
  783.9 31.4 reduce-scatter.34
  820.0 22.5 all-gather.32
  846.4 69.6 reduce-scatter.40
  918.5 30.2 reduce-scatter.36
  952.5 69.8 reduce-scatter.38
  1028.3 381.1 all-reduce.17
  1411.6 52.2 all-gather.36
  1469.8 124.1 all-reduce.15
  1596.4 54.1 all-gather.34
  1653.1 56.2 all-gather.46
  1711.6 56.2 all-gather.44
  1770.3 59.0 all-gather.42
  1831.7 59.0 all-gather.40

commit v2 on v1

--- a/solution.py
+++ b/solution.py
@@ -56,7 +56,7 @@
     row = grid_of((CHUNK, CHUNK), 0)
     col = grid_of((CHUNK, CHUNK), 1)
     lower_ones = jnp.where(row >= col, 1.0, 0.0).astype(f32)
-    cumulative = mh(lower_ones, log_decay)
+    cumulative = mm2(lower_ones.astype(bf16), log_decay)
     turned = jnp.where(lane < 2, strength, cumulative).T
     return strength, shifted_logit, log_decay, cumulative, turned
 
@@ -72,21 +72,43 @@
     return qa, ka, q_norm, k_norm, q, k, va.astype(bf16)
 
 
+def split(x):
+    high = x.astype(bf16)
+    return high, (x - high.astype(f32)).astype(bf16)
+
+
+def mm2(exact, right, dims=NN):
+    high, low = split(right)
+    return mm(exact, high, dims) + mm(exact, low, dims)
+
+
+def mm3(left, right, dims=NN):
+    lh, ll = split(left)
+    rh, rl = split(right)
+    return mm(lh, rh, dims) + (mm(lh, rl, dims) + mm(ll, rh, dims))
+
+
+def mb(left, right, dims=NN):
+    return mm(left.astype(bf16), right.astype(bf16), dims)
+
+
 def unit_inverse(system):
     size = system.shape[0]
     row = grid_of((size, size), 0)
     col = grid_of((size, size), 1)
     eye = jnp.where(row == col, 1.0, 0.0).astype(f32)
-    powers = jnp.where((row >> 3) == (col >> 3), -system, 0.0)
-    square = mh(powers, powers)
+    powers = jnp.where((row >> 2) == (col >> 2), -system, 0.0)
+    square = mb(powers, powers)
     total = eye + powers
-    total = total + mh(total, square)
-    total = total + mh(total, mh(square, square))
-    for bits in (3, 4, 5, 6):
+    total = total + mb(total, square)
+    for bits in (2, 3, 4, 5, 6):
         joint = ((row >> (bits + 1)) == (col >> (bits + 1))) & ((row >> bits) != (col >> bits))
         link = jnp.where(joint, system, 0.0)
-        total = total - mh(total, mh(link, total))
+        total = total - mb(total, mb(link, total))
     return total
+
+
+UNROLL = 2
 
 
 def mixer_forward_kernel(
@@ -98,8 +120,9 @@
     state[...] = jnp.zeros_like(state)
     row = grid_of((CHUNK, CHUNK), 0)
     col = grid_of((CHUNK, CHUNK), 1)
-
-    def body(c, carry):
+    zero = jnp.zeros((CHUNK, CHUNK), f32)
+
+    def prepare(c):
         rows = pl.ds(pl.multiple_of(c * CHUNK, CHUNK), CHUNK)
         x = proj_ref[rows, 0:1024].astype(f32)
         x_ext = jnp.concatenate([halo[...], x], axis=0)
@@ -118,9 +141,8 @@
             beta_row = turned[h : h + 1, :]
             ratio = jnp.exp(jnp.where(row >= col, c_col - c_row, -1e4)) * beta_row
             systems.append(jnp.where(row > col, ratio * mm(k, k, NT), 0.0))
-            mixing = ratio * mm(q, k, NT)
-            parts.append((q, k, v, c_col, mixing))
-        zero = jnp.zeros((CHUNK, CHUNK), f32)
+            mixing = (ratio * mm(q, k, NT)).astype(bf16)
+            parts.append((q, k, v, c_col, mixing, strength[:, h : h + 1]))
         joint = jnp.concatenate(
             [
                 jnp.concatenate([systems[0], zero], axis=1),
@@ -128,29 +150,37 @@
             ],
             axis=0,
         )
-        inverse = unit_inverse(joint)
+        return parts, unit_inverse(joint)
+
+    def advance(c, parts, inverse):
+        rows = pl.ds(pl.multiple_of(c * CHUNK, CHUNK), CHUNK)
         for h in range(2):
-            q, k, v, c_col, mixing = parts[h]
+            q, k, v, c_col, mixing, beta_col = parts[h]
             inv = inverse[128 * h : 128 * h + 128, 128 * h : 128 * h + 128]
             growth = jnp.exp(c_col)
             last = c_col[CHUNK - 1 :, :]
             before = state[h]
             start_ref[c, h] = before
             inv_ref[c, h] = inv
-            read = mh(jnp.concatenate([q, k], axis=0).astype(f32), before)
-            pseudo = mh(inv, v.astype(f32) - growth * read[CHUNK:])
+            read = mm2(jnp.concatenate([q, k], axis=0), before)
+            pseudo = mb(inv, v.astype(f32) - growth * read[CHUNK:])
             pseudo_ref[c, h] = pseudo
-            mixed = growth * read[:CHUNK] + mh(mixing, pseudo)
-            tail = jnp.exp(last - c_col) * strength[:, h : h + 1]
-            state[h] = jnp.exp(last) * before + mh(k.astype(f32), tail * pseudo, TN)
+            tail = jnp.exp(last - c_col) * beta_col
+            state[h] = jnp.exp(last) * before + mm2(k, tail * pseudo, TN)
+            mixed = growth * read[:CHUNK] + mm(mixing, pseudo.astype(bf16))
             mixed_ref[rows, 256 * h : 256 * h + 256] = mixed
             gate = proj_ref[rows, 1024 + 256 * h : 1280 + 256 * h].astype(f32)
             scale = lax.rsqrt(jnp.mean(mixed * mixed, axis=-1, keepdims=True) + out_floor)
             gated = mixed * scale * gain_ref[0:1, :] * (gate * jax.nn.sigmoid(gate))
             gated_ref[rows, 256 * h : 256 * h + 256] = gated.astype(bf16)
+
+    def body(step, carry):
+        ready = [prepare(step * UNROLL + u) for u in range(UNROLL)]
+        for u in range(UNROLL):
+            advance(step * UNROLL + u, *ready[u])
         return carry
 
-    lax.fori_loop(0, proj_ref.shape[0] // CHUNK, body, 0)
+    lax.fori_loop(0, proj_ref.shape[0] // (CHUNK * UNROLL), body, 0)
 
 
 def mixer_forward(projected, small, taps, heads, gain):
@@ -334,29 +364,1142 @@
     )(projected, small, taps, heads, gain, *saved, d_gated)
 
 
-def rms_norm(residual, gain):
-    scale = lax.rsqrt(jnp.mean(residual * residual, axis=-1, keepdims=True) + epsilon)
-    return residual * scale * gain
-
-
-def norm_back(residual, gain, d_out):
-    scale = lax.rsqrt(jnp.mean(residual * residual, axis=-1, keepdims=True) + epsilon)
-    unit = residual * scale
+SUB = 128
+LIMIT = 56 << 20
+MESH = pl.DeviceIdType.MESH
+
+
+def place():
+    me = lax.axis_index("grp")
+    y, c = me // 2, me % 2
+    return y, c
+
+
+def shard_rows(y, c, i, size):
+    return pl.ds(pl.multiple_of((2 * y + c) * size + i * SUB, SUB), SUB)
+
+
+def greet(y, c):
+    barrier = pltpu.get_barrier_semaphore()
+    for target in (2 * y + 1 - c, 2 * (1 - y) + c):
+        pl.semaphore_signal(barrier, inc=1, device_id={"grp": target}, device_id_type=MESH)
+    return lambda: pl.semaphore_wait(barrier, 2)
+
+
+def remote(src, dst, send, recv, target):
+    return pltpu.make_async_remote_copy(
+        src_ref=src, dst_ref=dst, send_sem=send, recv_sem=recv,
+        device_id={"grp": target}, device_id_type=MESH,
+    )
+
+
+class Gather:
+    def __init__(self, full, send, recv, size):
+        self.full, self.send, self.recv, self.size = full, send, recv, size
+        self.y, self.c = place()
+
+    def piece(self, kind, i):
+        y, c = self.y, self.c
+        rows = shard_rows(1 - y if kind == 2 else y, c, i, self.size)
+        target = 2 * (1 - y) + c if kind == 1 else 2 * y + 1 - c
+        view = self.full.at[rows]
+        return remote(view, view, self.send.at[kind, i], self.recv.at[kind, i], target)
+
+    def own(self, i):
+        return shard_rows(self.y, self.c, i, self.size)
+
+    def start(self, i):
+        self.piece(0, i).start()
+        self.piece(1, i).start()
+
+    def sibling(self, i):
+        self.piece(0, i).wait_recv()
+        return shard_rows(self.y, 1 - self.c, i, self.size)
+
+    def across(self, i):
+        self.piece(1, i).wait_recv()
+        self.piece(2, i).start()
+        return shard_rows(1 - self.y, self.c, i, self.size)
+
+    def diagonal(self, i):
+        self.piece(2, i).wait_recv()
+        return shard_rows(1 - self.y, 1 - self.c, i, self.size)
+
+    def finish(self):
+        for kind in range(3):
+            for i in range(self.size // SUB):
+                self.piece(kind, i).wait_send()
+
+
+class Scatter:
+    def __init__(self, out, core, keep, relay, far, send, recv, size):
+        self.out, self.core, self.keep, self.relayed, self.far = out, core, keep, relay, far
+        self.send, self.recv, self.size = send, recv, size
+        self.y, self.c = place()
+
+    def to_sibling(self, part, i):
+        rows = pl.ds(i * SUB, SUB)
+        return remote(
+            self.out.at[part, rows], self.core.at[part, rows],
+            self.send.at[part, i], self.recv.at[part, i], 2 * self.y + 1 - self.c,
+        )
+
+    def to_across(self, i):
+        rows = pl.ds(i * SUB, SUB)
+        return remote(
+            self.relayed.at[rows], self.far.at[rows],
+            self.send.at[2, i], self.recv.at[2, i], 2 * (1 - self.y) + self.c,
+        )
+
+    def give(self, part, i, value):
+        self.out[part, i * SUB : (i + 1) * SUB, :] = value.astype(bf16)
+        self.to_sibling(part, i).start()
+
+    def hold(self, part, i, value):
+        self.keep[part, i * SUB : (i + 1) * SUB, :] = value
+
+    def relay(self, i):
+        rows = slice(i * SUB, (i + 1) * SUB)
+        self.to_sibling(0, i).wait_recv()
+        self.relayed[rows, :] = (self.keep[0, rows, :] + self.core[0, rows, :].astype(f32)).astype(bf16)
+        self.to_across(i).start()
+
+    def total(self, i):
+        rows = slice(i * SUB, (i + 1) * SUB)
+        self.to_sibling(1, i).wait_recv()
+        near = self.keep[1, rows, :] + self.core[1, rows, :].astype(f32)
+        self.to_across(i).wait_recv()
+        return near + self.far[rows, :].astype(f32)
+
+    def finish(self):
+        for i in range(self.size // SUB):
+            self.to_sibling(0, i).wait_send()
+            self.to_sibling(1, i).wait_send()
+            self.to_across(i).wait_send()
+
+    @staticmethod
+    def scratch(size, width):
+        return [
+            pltpu.VMEM((2, size, width), bf16),
+            pltpu.VMEM((2, size, width), bf16),
+            pltpu.VMEM((2, size, width), f32),
+            pltpu.VMEM((size, width), bf16),
+            pltpu.VMEM((size, width), bf16),
+            pltpu.SemaphoreType.DMA((3, size // SUB)),
+            pltpu.SemaphoreType.DMA((3, size // SUB)),
+        ]
+
+
+def gather_sems(size):
+    return [pltpu.SemaphoreType.DMA((3, size // SUB)), pltpu.SemaphoreType.DMA((3, size // SUB))]
+
+
+def in_order(gather):
+    count = gather.size // SUB
+    for i in range(count):
+        yield gather.own(i)
+    for i in range(count):
+        yield gather.sibling(i)
+    for i in range(count):
+        yield gather.across(i)
+        yield gather.diagonal(i)
+
+
+def call(kernel, out_shape, inputs, scratch, collective, name, spots=()):
+    vmem = pl.BlockSpec(memory_space=pltpu.VMEM)
+    spot = pl.BlockSpec(memory_space=pl.ANY)
+    return pl.pallas_call(
+        kernel,
+        out_shape=out_shape,
+        in_specs=[vmem] * len(inputs) + [spot] * len(spots),
+        out_specs=tuple(vmem for _ in out_shape),
+        scratch_shapes=scratch,
+        compiler_params=pltpu.CompilerParams(
+            collective_id=collective, has_side_effects=True, vmem_limit_bytes=LIMIT
+        ),
+        cost_estimate=pl.CostEstimate(flops=1000, bytes_accessed=1000, transcendentals=0),
+        name=name,
+    )(*inputs, *spots)
+
+
+def relative(y, c, d):
+    dy, dc = d // 2, d % 2
+    return 2 * (y + dy - 2 * y * dy) + c + dc - 2 * c * dc
+
+
+def load_weight(own, sibling, far, whole, sems):
+    y, c = place()
+    size = own.shape[0]
+    copies = []
+
+    def add(src, d, start, count):
+        rows = pl.ds(pl.multiple_of(relative(y, c, d) * size + start, count), count)
+        copies.append(pltpu.make_async_copy(src, whole.at[rows], sems.at[len(copies)]))
+
+    add(own, 0, 0, size)
+    add(sibling, 1, 0, size)
+    if len(far.shape) == 4:
+        part = far.shape[2]
+        for k in range(far.shape[0]):
+            for d in (2, 3):
+                add(far.at[k, d - 2], d, k * part, part)
+    else:
+        for d in (2, 3):
+            add(far.at[d - 2], d, 0, size)
+    for copy in copies:
+        copy.start()
+
+    def wait():
+        for copy in copies:
+            copy.wait()
+
+    return wait
+
+
+def load_down(src, whole, sem):
+    rows = src.shape[0]
+    copy = pltpu.make_async_copy(src, whole.at[pl.ds(0, rows)], sem)
+    copy.start()
+    whole[rows:, :] = jnp.zeros((whole.shape[0] - rows, whole.shape[1]), bf16)
+    return copy.wait
+
+
+def like(*shape, dtype=f32):
+    return jax.ShapeDtypeStruct(shape, dtype)
+
+
+def normalise(x, gain):
+    return x * lax.rsqrt(jnp.mean(x * x, axis=-1, keepdims=True) + epsilon) * gain
+
+
+def normalise_back(x, gain, d_out):
+    scale = lax.rsqrt(jnp.mean(x * x, axis=-1, keepdims=True) + epsilon)
+    unit = x * scale
     d_unit = d_out * gain
-    d_residual = scale * (d_unit - unit * jnp.mean(d_unit * unit, axis=-1, keepdims=True))
-    return d_residual, jnp.sum(d_out * unit, axis=0)
-
-
-def gather_rows(x):
-    return lax.all_gather(x, "grp", axis=0, tiled=True)
-
-
-def scatter_rows(x):
-    return lax.psum_scatter(x.astype(bf16), "grp", scatter_dimension=0, tiled=True).astype(f32)
-
-
-def dot(left, right, dims=NN):
-    return mm(left, right, dims)
+    d_x = scale * (d_unit - unit * jnp.mean(d_unit * unit, axis=-1, keepdims=True))
+    return d_x, jnp.sum(d_out * unit, axis=0, keepdims=True)
+
+
+def project_kernel(
+    res_ref, gain_ref, ab_ref, own_ref, sibling_ref, far_ref,
+    normed_ref, proj_ref, small_ref, w_ref, loads, send, recv,
+):
+    loaded = load_weight(own_ref, sibling_ref, far_ref, w_ref, loads)
+    size = res_ref.shape[0]
+    y, c = place()
+    ready = greet(y, c)
+    gather = Gather(normed_ref, send, recv, size)
+    for i in range(size // SUB):
+        rows = slice(i * SUB, (i + 1) * SUB)
+        normed_ref[gather.own(i), :] = normalise(res_ref[rows, :], gain_ref[...]).astype(bf16)
+        if i == 0:
+            ready()
+        gather.start(i)
+    loaded()
+    for rows in in_order(gather):
+        normed = normed_ref[rows, :]
+        proj_ref[rows, :] = mm(normed, w_ref[...]).astype(bf16)
+        small_ref[rows, :] = mm(normed, ab_ref[...])
+    gather.finish()
+
+
+def project(residual, gain, weight, ab):
+    size, width = residual.shape
+    tokens = 4 * size
+    return call(
+        project_kernel,
+        (like(tokens, width, dtype=bf16), like(tokens, 1536, dtype=bf16), like(tokens, 128)),
+        (residual, gain, ab),
+        [pltpu.VMEM((width, 1536), bf16), pltpu.SemaphoreType.DMA((10,))] + gather_sems(size),
+        1 if len(weight[2].shape) == 4 else 6,
+        "project",
+        weight,
+    )
+
+
+def swiglu(up):
+    lane = grid_of((SUB, 128), 1)
+    gate, value, tail = up[:, :640], up[:, 640:1280], up[:, 1280:]
+    turned = pltpu.roll(tail, 64, 1)
+    head = gate * jax.nn.sigmoid(gate) * value
+    last = jnp.where(lane < 64, tail * jax.nn.sigmoid(tail) * turned, 0.0)
+    return jnp.concatenate([head, last], axis=1)
+
+
+def swiglu_back(up, d_hidden):
+    lane = grid_of((SUB, 128), 1)
+    gate, value, tail = up[:, :640], up[:, 640:1280], up[:, 1280:]
+    turned = pltpu.roll(tail, 64, 1)
+    d_head, d_tail = d_hidden[:, :640], d_hidden[:, 640:]
+    d_tail = d_tail + pltpu.roll(d_tail, 64, 1)
+    sig = jax.nn.sigmoid(gate)
+    d_gate = d_head * value * (sig * (1.0 + gate * (1.0 - sig)))
+    d_value = d_head * gate * sig
+    sig = jax.nn.sigmoid(tail)
+    side = jnp.where(
+        lane < 64,
+        turned * (sig * (1.0 + tail * (1.0 - sig))),
+        turned * jax.nn.sigmoid(turned),
+    )
+    return jnp.concatenate([d_gate, d_value, d_tail * side], axis=1)
+
+
+def ffn_forward_kernel(
+    gated_ref, wout_ref, res_ref, gain_ref, down_ref, own_ref, sibling_ref, far_ref,
+    mid_ref, normed_ref, up_ref, hidden_ref, out_ref,
+    wup_ref, wdown_ref, loads, *scratch,
+):
+    loaded = load_weight(own_ref, sibling_ref, far_ref, wup_ref, loads)
+    loaded_down = load_down(down_ref, wdown_ref, loads.at[10])
+    size = res_ref.shape[0]
+    count = size // SUB
+    y, c = place()
+    ready = greet(y, c)
+    first = Scatter(*scratch[:7], size)
+    second = Scatter(*scratch[7:14], size)
+    gather = Gather(normed_ref, *scratch[14:], size)
+
+    def branch(rows):
+        return mm(gated_ref[rows, :], wout_ref[...])
+
+    for part in range(2):
+        yy = 1 - y if part == 0 else y
+        for i in range(count):
+            value = branch(shard_rows(yy, 1 - c, i, size))
+            if part == 0 and i == 0:
+                ready()
+            first.give(part, i, value)
+            first.hold(part, i, branch(shard_rows(yy, c, i, size)))
+            if part == 0:
+                first.relay(i)
+    for i in range(count):
+        rows = slice(i * SUB, (i + 1) * SUB)
+        mid = res_ref[rows, :] + first.total(i)
+        mid_ref[rows, :] = mid
+        normed_ref[gather.own(i), :] = normalise(mid, gain_ref[...]).astype(bf16)
+        gather.start(i)
+
+    def feed(rows):
+        up = mm(normed_ref[rows, :], wup_ref[...])
+        up_ref[rows, :] = up.astype(bf16)
+        hidden = swiglu(up).astype(bf16)
+        hidden_ref[rows, :] = hidden
+        return mm(hidden, wdown_ref[...])
+
+    loaded()
+    loaded_down()
+    for i in range(count):
+        second.hold(1, i, feed(gather.own(i)))
+    for i in range(count):
+        second.give(1, i, feed(gather.sibling(i)))
+    for i in range(count):
+        near = gather.across(i)
+        second.hold(0, i, feed(near))
+        second.give(0, i, feed(gather.diagonal(i)))
+        second.relay(i)
+    for i in range(count):
+        rows = slice(i * SUB, (i + 1) * SUB)
+        out_ref[rows, :] = mid_ref[rows, :] + second.total(i)
+    first.finish()
+    second.finish()
+    gather.finish()
+
+
+def ffn_forward(gated, w_out, residual, gain, w_down, w_up):
+    size, width = residual.shape
+    tokens = 4 * size
+    return call(
+        ffn_forward_kernel,
+        (
+            like(size, width),
+            like(tokens, width, dtype=bf16),
+            like(tokens, 1408, dtype=bf16),
+            like(tokens, 768, dtype=bf16),
+            like(size, width),
+        ),
+        (gated, w_out, residual, gain),
+        [
+            pltpu.VMEM((width, 1408), bf16),
+            pltpu.VMEM((768, width), bf16),
+            pltpu.SemaphoreType.DMA((11,)),
+        ]
+        + Scatter.scratch(size, width)
+        + Scatter.scratch(size, width)
+        + gather_sems(size),
+        2,
+        "ffn_forward",
+        (w_down,) + tuple(w_up),
+    )
+
+
+def grad_place():
+    rank = lax.axis_index("rep") % 8
+    x = rank % 2
+    y, c = place()
+
+    def slot(r):
+        return r % 2 + x - 2 * (r % 2) * x
+
+    def target(d):
+        dy, dc = d // 2, d % 2
+        return 2 * (y + dy - 2 * y * dy) + c + dc - 2 * c * dc
+
+    return slot, target
+
+
+def store_columns(buf, value, row, base, slot):
+    for r in range(8):
+        buf[slot(r), r // 2, base + row : base + row + value.shape[0], :] = value[
+            :, 128 * r : 128 * r + 128
+        ].astype(bf16)
+
+
+def store_rows(buf, value, d, base, slot):
+    blocks = value.shape[1] // 128
+    for r in range(8):
+        for j in range(blocks):
+            at = base + (d * blocks + j) * 32
+            buf[slot(r), r // 2, at : at + 32, :] = value[
+                32 * r : 32 * r + 32, 128 * j : 128 * j + 128
+            ].astype(bf16)
+
+
+DOWN_AT, OUT_AT, UP_AT, FFN_ROWS = 0, 704, 1216, 2624
+SMALL_AT, IN_ROWS = 1536, 1552
+
+
+def ffn_backward_kernel(
+    dres_ref, up_ref, hidden_ref, normed_ref, mid_ref, gain_ref, gated_ref, wout_ref,
+    down_ref, own_ref, sibling_ref, far_ref,
+    dmid_ref, dgated_ref, ggain_ref, buf_ref,
+    wup_ref, wdown_ref, loads, ddown_ref, dup_ref, dbranch_ref, *scratch,
+):
+    loaded = load_weight(own_ref, sibling_ref, far_ref, wup_ref, loads)
+    loaded_down = load_down(down_ref, wdown_ref, loads.at[10])
+    size = dres_ref.shape[0]
+    count = size // SUB
+    y, c = place()
+    ready = greet(y, c)
+    slot, target = grad_place()
+    first = Gather(ddown_ref, *scratch[:2], size)
+    second = Gather(dbranch_ref, *scratch[2:4], size)
+    scatter = Scatter(*scratch[4:], size)
+    for i in range(count):
+        ddown_ref[first.own(i), :] = dres_ref[i * SUB : (i + 1) * SUB, :].astype(bf16)
+        if i == 0:
+            ready()
+        first.start(i)
+
+    def feed(rows):
+        d_hidden = mm(ddown_ref[rows, :], wdown_ref[...], NT)
+        d_up = swiglu_back(up_ref[rows, :].astype(f32), d_hidden).astype(bf16)
+        dup_ref[rows, :] = d_up
+        return mm(d_up, wup_ref[...], NT)
+
+    loaded()
+    loaded_down()
+    for i in range(count):
+        scatter.hold(1, i, feed(first.own(i)))
+    for i in range(count):
+        scatter.give(1, i, feed(first.sibling(i)))
+    for i in range(count):
+        near = first.across(i)
+        scatter.hold(0, i, feed(near))
+        scatter.give(0, i, feed(first.diagonal(i)))
+        scatter.relay(i)
+    for m in range(6):
+        wide = 128 if m < 5 else 64
+        value = mm(hidden_ref[:, 128 * m : 128 * m + 128], ddown_ref[...], TN)
+        store_columns(buf_ref, value[:wide], 128 * m, DOWN_AT, slot)
+    ggain_ref[...] = jnp.zeros_like(ggain_ref)
+    for i in range(count):
+        rows = slice(i * SUB, (i + 1) * SUB)
+        d_norm, g_gain = normalise_back(mid_ref[rows, :], gain_ref[...], scatter.total(i))
+        d_mid = dres_ref[rows, :] + d_norm
+        dmid_ref[rows, :] = d_mid
+        ggain_ref[0:1, :] += g_gain
+        dbranch_ref[second.own(i), :] = d_mid.astype(bf16)
+        second.start(i)
+    for d in range(4):
+        lanes = pl.ds(pl.multiple_of(target(d) * 256, 256), 256)
+        value = mm(normed_ref[:, lanes], dup_ref[...], TN)
+        store_rows(buf_ref, value, d, UP_AT, slot)
+    for rows in in_order(second):
+        dgated_ref[rows, :] = mm(dbranch_ref[rows, :], wout_ref[...], NT).astype(bf16)
+    for m in range(4):
+        value = mm(gated_ref[:, 128 * m : 128 * m + 128], dbranch_ref[...], TN)
+        store_columns(buf_ref, value, 128 * m, OUT_AT, slot)
+    first.finish()
+    second.finish()
+    scatter.finish()
+
+
+def ffn_backward(d_res, up, hidden, normed, mid, gain, gated, w_out, w_down, w_up):
+    size, width = d_res.shape
+    tokens = 4 * size
+    return call(
+        ffn_backward_kernel,
+        (
+            like(size, width),
+            like(tokens, 512, dtype=bf16),
+            like(8, width),
+            like(2, 4, FFN_ROWS, 128, dtype=bf16),
+        ),
+        (d_res, up, hidden, normed, mid, gain, gated, w_out),
+        [
+            pltpu.VMEM((width, 1408), bf16),
+            pltpu.VMEM((768, width), bf16),
+            pltpu.SemaphoreType.DMA((11,)),
+            pltpu.VMEM((tokens, width), bf16),
+            pltpu.VMEM((tokens, 1408), bf16),
+            pltpu.VMEM((tokens, width), bf16),
+        ]
+        + gather_sems(size)
+        + gather_sems(size)
+        + Scatter.scratch(size, width),
+        3,
+        "ffn_backward",
+        (w_down,) + tuple(w_up),
+    )
+
+
+def project_backward_kernel(
+    dproj_ref, dsmall_ref, ab_ref, normed_ref, res_ref, gain_ref, dmid_ref,
+    gtwo_ref, gtaps_ref, gheads_ref, own_ref, sibling_ref, far_ref,
+    dres_ref, buf_ref,
+    w_ref, loads, table, *scratch,
+):
+    loaded = load_weight(own_ref, sibling_ref, far_ref, w_ref, loads)
+    size = res_ref.shape[0]
+    count = size // SUB
+    y, c = place()
+    ready = greet(y, c)
+    slot, target = grad_place()
+    scatter = Scatter(*scratch, size)
+
+    def back(rows):
+        return mm(dproj_ref[rows, :], w_ref[...], NT) + mm(dsmall_ref[rows, :], ab_ref[...], NT)
+
+    def weight_grad(d):
+        lanes = pl.ds(pl.multiple_of(target(d) * 256, 256), 256)
+        value = mm(normed_ref[:, lanes], dproj_ref[...], TN)
+        store_rows(buf_ref, value, d, 0, slot)
+
+    loaded()
+    for part in range(2):
+        yy = 1 - y if part == 0 else y
+        for i in range(count):
+            value = back(shard_rows(yy, 1 - c, i, size))
+            if part == 0 and i == 0:
+                ready()
+            scatter.give(part, i, value)
+            scatter.hold(part, i, back(shard_rows(yy, c, i, size)))
+            if part == 0:
+                scatter.relay(i)
+    for d in range(4):
+        weight_grad(d)
+    ab_grad = mm(dsmall_ref[...], normed_ref[...], TN)
+    table[...] = jnp.zeros_like(table)
+    for k in range(8):
+        lanes = slice(128 * k, 128 * k + 128)
+        for j in range(4):
+            table[8 * j + k : 8 * j + k + 1, :] = gtaps_ref[j : j + 1, lanes]
+            table[32 + 8 * j + k : 33 + 8 * j + k, :] = ab_grad[j : j + 1, lanes]
+        table[72 + k : 73 + k, :] = gtwo_ref[0:1, lanes]
+    table[80:81, :] = gheads_ref[0:1, 0:128]
+    table[81:82, :] = gheads_ref[0:1, 128:256]
+    table[82:83, :] = gheads_ref[1:2, 0:128]
+    table[83:84, :] = gheads_ref[2:3, 0:128]
+    gain_sum = jnp.zeros((1, res_ref.shape[1]), f32)
+    for i in range(count):
+        rows = slice(i * SUB, (i + 1) * SUB)
+        d_norm, g_gain = normalise_back(res_ref[rows, :], gain_ref[...], scatter.total(i))
+        dres_ref[rows, :] = dmid_ref[rows, :] + d_norm
+        gain_sum = gain_sum + g_gain
+    for k in range(8):
+        table[64 + k : 65 + k, :] = gain_sum[:, 128 * k : 128 * k + 128]
+    for r in range(8):
+        buf_ref[slot(r), r // 2, SMALL_AT:IN_ROWS, :] = table[16 * r : 16 * r + 16, :].astype(bf16)
+    scatter.finish()
+
+
+def project_backward(d_proj, d_small, weight, ab, normed, residual, gain, d_mid, g_two, g_taps, g_heads):
+    size, width = residual.shape
+    return call(
+        project_backward_kernel,
+        (like(size, width), like(2, 4, IN_ROWS, 128, dtype=bf16)),
+        (d_proj, d_small, ab, normed, residual, gain, d_mid, g_two, g_taps, g_heads),
+        [
+            pltpu.VMEM((width, 1536), bf16),
+            pltpu.SemaphoreType.DMA((10,)),
+            pltpu.VMEM((128, 128), f32),
+        ]
+        + Scatter.scratch(size, width),
+        4 if len(weight[2].shape) == 4 else 7,
+        "project_backward",
+        weight,
+    )
+
+
+def collect(final_ref, pieces, sems):
+    copy = pltpu.make_async_copy(final_ref, pieces, sems.at[0])
+    copy.start()
+    copy.wait()
+
+
+def offset_of(s):
+    y, c = place()
+    sy, sc = s // 2, s % 2
+    return 2 * (y + sy - 2 * y * sy) + c + sc - 2 * c * sc
+
+
+def assemble_ffn_kernel(layer, earlier, final_ref, *refs):
+    down_ref, out_ref, up_ref, pieces, down, out, up, sems = refs[earlier:]
+    collect(final_ref, pieces, sems)
+    stores = [
+        pltpu.make_async_copy(down, down_ref.at[layer], sems.at[8]),
+        pltpu.make_async_copy(out, out_ref.at[layer], sems.at[9]),
+        pltpu.make_async_copy(up, up_ref.at[layer], sems.at[10]),
+    ]
+    for r in range(8):
+        lanes = slice(128 * r, 128 * r + 128)
+        down[:, lanes] = pieces[r, DOWN_AT:OUT_AT, :].astype(f32)
+    stores[0].start()
+    for r in range(8):
+        lanes = slice(128 * r, 128 * r + 128)
+        out[:, lanes] = pieces[r, OUT_AT:UP_AT, :].astype(f32)
+    stores[1].start()
+    left = grid_of((32, 128), 1) < 64
+
+    def turn(tile):
+        return pltpu.roll(tile, 64, 1)
+
+    def body(r, carry):
+        rows = pl.ds(pl.multiple_of(32 * r, 32), 32)
+        for m in range(2):
+            tiles = []
+            for s in (2 * m, 2 * m + 1):
+                at = UP_AT + offset_of(s) * 352
+                tiles.append(
+                    [
+                        pieces[r, pl.ds(pl.multiple_of(at + 32 * j, 32), 32), :].astype(f32)
+                        for j in range(11)
+                    ]
+                )
+            for side in range(2):
+                even = tiles[0][5 * side : 5 * side + 5]
+                odd = [turn(tile) for tile in tiles[1][5 * side : 5 * side + 5]]
+                even_tail = tiles[0][10] if side == 0 else turn(tiles[0][10])
+                odd_tail = turn(tiles[1][10]) if side == 0 else tiles[1][10]
+                row = even + [jnp.where(left, even_tail, odd[0])]
+                row += [jnp.where(left, odd[j - 1], odd[j]) for j in range(1, 5)]
+                row += [jnp.where(left, odd[4], odd_tail)]
+                base = FF * side + 1408 * m
+                for j, tile in enumerate(row):
+                    up[rows, base + 128 * j : base + 128 * j + 128] = tile
+        return carry
+
+    lax.fori_loop(0, 8, body, 0)
+    stores[2].start()
+    for store in stores:
+        store.wait()
+
+
+def assemble_in_kernel(layer, earlier, final_ref, *refs):
+    in_ref, table_ref, pieces, whole, sems = refs[earlier:]
+    collect(final_ref, pieces, sems)
+    store = pltpu.make_async_copy(whole, in_ref.at[layer], sems.at[8])
+
+    def body(r, carry):
+        rows = pl.ds(pl.multiple_of(32 * r, 32), 32)
+        for s in range(4):
+            at = offset_of(s) * 384
+            for j in range(12):
+                if j < 2:
+                    column = 256 * s + 128 * j
+                elif j < 4:
+                    column = HK + 256 * s + 128 * (j - 2)
+                elif j < 8:
+                    column = 2 * HK + 512 * s + 128 * (j - 4)
+                else:
+                    column = CH + 512 * s + 128 * (j - 8)
+                tile = pieces[r, pl.ds(pl.multiple_of(at + 32 * j, 32), 32), :]
+                whole[rows, column : column + 128] = tile.astype(f32)
+        return carry
+
+    lax.fori_loop(0, 8, body, 0)
+    store.start()
+    for r in range(8):
+        table_ref[16 * r : 16 * r + 16, :] = pieces[r, SMALL_AT:IN_ROWS, :].astype(f32)
+    store.wait()
+
+
+def assemble(kernel, layer, final, earlier, shapes, table, scratch, name):
+    spot = pl.BlockSpec(memory_space=pl.ANY)
+    out_shape = tuple(like(LAYERS, *shape) for shape in shapes)
+    out_specs = (spot,) * len(shapes)
+    if table:
+        out_shape += (like(128, 128),)
+        out_specs += (pl.BlockSpec(memory_space=pltpu.VMEM),)
+    return pl.pallas_call(
+        partial(kernel, layer, len(earlier)),
+        out_shape=out_shape,
+        in_specs=[spot] * (1 + len(earlier)),
+        out_specs=out_specs,
+        scratch_shapes=[pltpu.VMEM(final.shape, bf16)]
+        + [pltpu.VMEM(shape, f32) for shape in scratch]
+        + [pltpu.SemaphoreType.DMA((11,))],
+        input_output_aliases={1 + k: k for k in range(len(earlier))},
+        compiler_params=pltpu.CompilerParams(vmem_limit_bytes=LIMIT),
+        name=name,
+    )(final, *earlier)
+
+
+def assemble_ffn(layer, final, earlier):
+    shapes = [(704, 1024), (512, 1024), (256, 2 * FF)]
+    return assemble(
+        assemble_ffn_kernel, layer, final, earlier, shapes, False, shapes, "assemble_ffn"
+    )
+
+
+def assemble_in(layer, final, earlier):
+    shapes = [(256, CH + HV)]
+    return assemble(
+        assemble_in_kernel, layer, final, earlier, shapes, True, shapes, "assemble_in"
+    )
+
+
+FFN_MOVE, IN_MOVE = (UP_AT, 352), (0, 384)
+
+
+def add_into(dst, left, right):
+    dst[...] = (left[...].astype(f32) + right[...].astype(f32)).astype(bf16)
+
+
+class Group:
+    def __init__(self, number, piece, moved, final, move, sems):
+        self.number, self.piece, self.moved, self.final = number, piece, moved, final
+        self.at, self.part = move
+        self.send, self.recv, self.local = sems
+        rank = lax.axis_index("rep")
+        self.rank, self.x, self.z = rank, rank % 2, (rank % 8) // 2
+        self.y, self.c = place()
+
+    def swap(self, d):
+        dy, dc = d // 2, d % 2
+        target = 2 * (self.y + dy - 2 * self.y * dy) + self.c + dc - 2 * self.c * dc
+        rows = pl.ds(self.at + d * self.part, self.part)
+        return pltpu.make_async_remote_copy(
+            src_ref=self.piece.at[rows], dst_ref=self.moved.at[rows],
+            send_sem=self.send.at[self.number, d], recv_sem=self.recv.at[self.number, d],
+            device_id={"grp": target}, device_id_type=MESH,
+        )
+
+    def start_swap(self):
+        for d in range(1, 4):
+            self.swap(d).start()
+        first = self.at + self.part
+        self.moved[0:first, :] = self.piece[0:first, :]
+        rest = self.at + 4 * self.part
+        if rest < self.piece.shape[0]:
+            self.moved[rest:, :] = self.piece[rest:, :]
+
+    def wait_swap(self):
+        for d in range(1, 4):
+            self.swap(d).wait_recv()
+
+    def move(self, step, source_z, kind):
+        owner = 2 * source_z + self.x
+        src = self.moved if step == 0 else self.final.at[owner]
+        side = 4 * kind if kind < 2 else 8
+        slot = side + (abs(step) if kind < 2 else step + 3)
+        target = (self.rank + 2, self.rank - 2, self.rank + 1 - 2 * self.x)[kind]
+        return pltpu.make_async_remote_copy(
+            src_ref=src, dst_ref=self.final.at[owner],
+            send_sem=self.send.at[self.number, 4 + slot],
+            recv_sem=self.recv.at[self.number, 4 + (slot if kind < 2 else 8)],
+            device_id={"rep": target}, device_id_type=MESH,
+        )
+
+    def x_move(self, step, source_z):
+        owner = 2 * source_z + self.x
+        src = self.moved if step == 0 else self.final.at[owner]
+        return pltpu.make_async_remote_copy(
+            src_ref=src, dst_ref=self.final.at[owner],
+            send_sem=self.send.at[self.number, 12 + step + 3],
+            recv_sem=self.recv.at[self.number, 12 + source_z],
+            device_id={"rep": self.rank + 1 - 2 * self.x}, device_id_type=MESH,
+        )
+
+    def own_copy(self):
+        return pltpu.make_async_copy(
+            self.moved, self.final.at[2 * self.z + self.x], self.local.at[self.number]
+        )
+
+    def begin(self):
+        self.x_move(0, self.z).start()
+
+        @pl.when(self.z < 3)
+        def _():
+            self.move(0, self.z, 0).start()
+
+        @pl.when(self.z > 0)
+        def _():
+            self.move(0, self.z, 1).start()
+
+        self.own_copy().start()
+
+    def forward(self, k, act):
+        z = self.z
+
+        @pl.when(z >= k)
+        def _():
+            source = z - k
+            act(self, k, source, 0)
+
+            @pl.when(z < 3)
+            def _():
+                act(self, k, source, 2)
+
+        @pl.when(z + k <= 3)
+        def _():
+            source = z + k
+            act(self, -k, source, 1)
+
+            @pl.when(z > 0)
+            def _():
+                act(self, -k, source, 3)
+
+    def relay(self, k):
+        def act(self, step, source, what):
+            if what == 0:
+                self.move(step - 1, source, 0).wait_recv()
+                self.x_move(step, source).start()
+            elif what == 1:
+                self.move(step + 1, source, 1).wait_recv()
+                self.x_move(step, source).start()
+            elif what == 2:
+                self.move(step, source, 0).start()
+            else:
+                self.move(step, source, 1).start()
+
+        self.forward(k, act)
+
+    def finish(self):
+        def act(self, step, source, what):
+            if what < 2:
+                self.x_move(step, source).wait_send()
+            elif what == 2:
+                self.move(step, source, 0).wait_send()
+            else:
+                self.move(step, source, 1).wait_send()
+
+        for k in range(1, 4):
+            self.forward(k, act)
+        self.x_move(0, self.z).wait_send()
+
+        @pl.when(self.z < 3)
+        def _():
+            self.move(0, self.z, 0).wait_send()
+
+        @pl.when(self.z > 0)
+        def _():
+            self.move(0, self.z, 1).wait_send()
+
+        for source in range(4):
+            self.x_move(0, source).wait_recv()
+        self.own_copy().wait()
+        for d in range(1, 4):
+            self.swap(d).wait_send()
+
+
+class Line:
+    def __init__(self, values, right, left, send, recv):
+        self.values, self.right, self.left = values, right, left
+        self.send, self.recv = send, recv
+        self.rank = lax.axis_index("rep")
+        self.z = (self.rank % 8) // 2
+
+    def go(self, o, toward):
+        land = self.right if toward == 0 else self.left
+        return pltpu.make_async_remote_copy(
+            src_ref=self.values.at[o], dst_ref=land.at[o],
+            send_sem=self.send.at[toward, o], recv_sem=self.recv.at[toward, o],
+            device_id={"rep": self.rank + 2 - 4 * toward}, device_id_type=MESH,
+        )
+
+    def edges(self):
+        @pl.when(self.z == 0)
+        def _():
+            for o in (3, 2, 1):
+                self.go(o, 0).start()
+
+        @pl.when(self.z == 3)
+        def _():
+            for o in (0, 1, 2):
+                self.go(o, 1).start()
+
+    def inner(self):
+        z = self.z
+        for o in (3, 2):
+
+            @pl.when((z > 0) & (z < o))
+            def _():
+                self.go(o, 0).wait_recv()
+                add_into(self.values.at[o], self.values.at[o], self.right.at[o])
+                self.go(o, 0).start()
+
+            @pl.when((z < 3) & (z > 3 - o))
+            def _():
+                self.go(3 - o, 1).wait_recv()
+                add_into(self.values.at[3 - o], self.values.at[3 - o], self.left.at[3 - o])
+                self.go(3 - o, 1).start()
+
+    def total(self, out):
+        z = self.z
+        for o in range(4):
+
+            @pl.when(z == o)
+            def _():
+                value = self.values[o].astype(f32)
+                if o > 0:
+                    self.go(o, 0).wait_recv()
+                    value = value + self.right[o].astype(f32)
+                if o < 3:
+                    self.go(o, 1).wait_recv()
+                    value = value + self.left[o].astype(f32)
+                out[...] = value.astype(bf16)
+
+    def finish(self):
+        for o in range(4):
+
+            @pl.when(self.z < o)
+            def _():
+                self.go(o, 0).wait_send()
+
+            @pl.when(self.z > o)
+            def _():
+                self.go(o, 1).wait_send()
+
+
+def finish_kernel(
+    p1, p2, s3, b4, f1, f2, f3, f4,
+    q1, q2, q3, q4, e1, e2, e3, e4, v3, r3, l3, v4, x4, r4, l4,
+    send, recv, local, send3, recv3, send4, recv4, send5, recv5, loads,
+):
+    rank = lax.axis_index("rep")
+    x, z = rank % 2, (rank % 8) // 2
+    y, c = place()
+    loaded = [
+        pltpu.make_async_copy(p1, q1, loads.at[0]),
+        pltpu.make_async_copy(p2, q2, loads.at[1]),
+        pltpu.make_async_copy(s3, v3, loads.at[2]),
+        pltpu.make_async_copy(b4.at[0], v4, loads.at[3]),
+    ]
+    for load in loaded:
+        load.start()
+    barrier = pltpu.get_barrier_semaphore()
+    pl.semaphore_signal(
+        barrier, inc=1, device_id={"rep": rank + 1 - 2 * x}, device_id_type=MESH
+    )
+    for d in range(1, 4):
+        dy, dc = d // 2, d % 2
+        target = 2 * (y + dy - 2 * y * dy) + c + dc - 2 * c * dc
+        pl.semaphore_signal(barrier, inc=1, device_id={"grp": target}, device_id_type=MESH)
+
+    @pl.when(z > 0)
+    def _():
+        pl.semaphore_signal(barrier, inc=1, device_id={"rep": rank - 2}, device_id_type=MESH)
+
+    @pl.when(z < 3)
+    def _():
+        pl.semaphore_signal(barrier, inc=1, device_id={"rep": rank + 2}, device_id_type=MESH)
+
+    @pl.when((z > 0) & (z < 3))
+    def _():
+        pl.semaphore_wait(barrier, 6)
+
+    @pl.when((z == 0) | (z == 3))
+    def _():
+        pl.semaphore_wait(barrier, 5)
+
+    def halves(o):
+        return pltpu.make_async_remote_copy(
+            src_ref=b4.at[1, o], dst_ref=x4.at[o], send_sem=send5.at[o], recv_sem=recv5.at[o],
+            device_id={"rep": rank + 1 - 2 * x}, device_id_type=MESH,
+        )
+
+    for o in (3, 0, 2, 1):
+        halves(o).start()
+    sems = (send, recv, local)
+    g1 = Group(0, q1, e1, f1, FFN_MOVE, sems)
+    g2 = Group(1, q2, e2, f2, IN_MOVE, sems)
+    g3 = Group(2, q3, e3, f3, FFN_MOVE, sems)
+    g4 = Group(3, q4, e4, f4, IN_MOVE, sems)
+    line3 = Line(v3, r3, l3, send3, recv3)
+    line4 = Line(v4, r4, l4, send4, recv4)
+    loaded[0].wait()
+    g1.start_swap()
+    loaded[1].wait()
+    g2.start_swap()
+    loaded[2].wait()
+    line3.edges()
+    g1.wait_swap()
+    g1.begin()
+    g2.wait_swap()
+    g2.begin()
+    line3.inner()
+    loaded[3].wait()
+    for o in (3, 0, 2, 1):
+        halves(o).wait_recv()
+        add_into(v4.at[o], v4.at[o], x4.at[o])
+    line4.edges()
+    line3.total(q3)
+    g3.start_swap()
+    g1.relay(1)
+    g3.wait_swap()
+    g3.begin()
+    line4.inner()
+    g2.relay(1)
+    line4.total(q4)
+    g4.start_swap()
+    g1.relay(2)
+    g4.wait_swap()
+    g4.begin()
+    g2.relay(2)
+    g3.relay(1)
+    g1.relay(3)
+    g4.relay(1)
+    g2.relay(3)
+    g3.relay(2)
+    g4.relay(2)
+    g3.relay(3)
+    g4.relay(3)
+    for group in (g1, g2, g3, g4):
+        group.finish()
+    line3.finish()
+    line4.finish()
+    for o in range(4):
+        halves(o).wait_send()
+
+
+def finish_reduction(p1, p2, s3, b4):
+    spot = pl.BlockSpec(memory_space=pl.ANY)
+    big, small = p1.shape, p2.shape
+    dma = pltpu.SemaphoreType.DMA
+    return pl.pallas_call(
+        finish_kernel,
+        out_shape=tuple(like(8, *shape, dtype=bf16) for shape in (big, small, big, small)),
+        in_specs=[spot] * 4,
+        out_specs=(spot,) * 4,
+        scratch_shapes=[
+            pltpu.VMEM(shape, bf16)
+            for shape in [big, small] * 4
+            + [(4,) + big] * 3
+            + [(4,) + small] * 4
+        ]
+        + [dma((4, 20)), dma((4, 20)), dma((4,))]
+        + [dma((2, 4))] * 4
+        + [dma((4,)), dma((4,)), dma((4,))],
+        compiler_params=pltpu.CompilerParams(
+            collective_id=5, has_side_effects=True, vmem_limit_bytes=LIMIT
+        ),
+        cost_estimate=pl.CostEstimate(flops=1000, bytes_accessed=1000, transcendentals=0),
+        name="finish_reduction",
+    )(p1, p2, s3, b4)
+
+
+def swap_route(bit, count):
+    return [(i, i ^ bit) for i in range(count)]
+
+
+def planes_of(replicas):
+    return [
+        [8 * b + 2 * z + x for z in range(4)] for b in range(replicas // 8) for x in range(2)
+    ]
+
+
+def swap_x(array, replicas):
+    return lax.ppermute(array, "rep", swap_route(1, replicas))
+
+
+def add_arrived(kept, arrived):
+    return (kept.astype(f32) + arrived.astype(f32)).astype(bf16)
+
+
+def reduce_z(summed, replicas):
+    piece = lax.psum_scatter(
+        summed, "rep", scatter_dimension=0, tiled=False, axis_index_groups=planes_of(replicas)
+    )
+    blocks = replicas // 8
+    if blocks > 1:
+        piece = lax.psum(
+            piece, "rep", axis_index_groups=[[8 * b + r for b in range(blocks)] for r in range(8)]
+        )
+    return piece
+
+
+def exchange(piece, at, part):
+    moved = [piece[: at + part]]
+    for d in range(1, 4):
+        moved.append(
+            lax.ppermute(piece[at + d * part : at + (d + 1) * part], "grp", swap_route(d, 4))
+        )
+    moved.append(piece[at + 4 * part :])
+    return jnp.concatenate(moved, axis=0)
+
+
+def gather_z(piece, replicas):
+    return lax.all_gather(piece, "rep", axis=0, axis_index_groups=planes_of(replicas))
+
+
+def spread(piece, replicas):
+    owned = gather_z(piece, replicas)
+    other = swap_x(owned, replicas)
+    odd = lax.axis_index("rep") % 2 == 1
+    pair = jnp.stack([jnp.where(odd, other, owned), jnp.where(odd, owned, other)], axis=1)
+    return pair.reshape((8,) + piece.shape)
+
+
+def finish_all(piece1, piece2, summed3, buf4, replicas):
+    if replicas == 8:
+        return finish_reduction(piece1, piece2, summed3, buf4)
+    piece3 = reduce_z(summed3, replicas)
+    piece4 = reduce_z(add_arrived(buf4[0], swap_x(buf4[1], replicas)), replicas)
+    return [
+        spread(exchange(piece, *move), replicas)
+        for piece, move in (
+            (piece1, FFN_MOVE), (piece2, IN_MOVE), (piece3, FFN_MOVE), (piece4, IN_MOVE)
+        )
+    ]
+
+
+def tie(*values):
+    return lax.optimization_barrier(values)
+
+
+def by_source(blocks, mine):
+    y, c = mine // 2 == 1, mine % 2 == 1
+    blocks = jnp.where(c, jnp.stack([blocks[k ^ 1] for k in range(4)]), blocks)
+    return jnp.where(y, jnp.stack([blocks[k ^ 2] for k in range(4)]), blocks)
+
+
+def swap(array, d):
+    return lax.ppermute(array, "grp", swap_route(d, 4))
+
+
+def reshard_near(pieces_of, mine):
+    pieces = [pieces_of(mine ^ d, 0, None) for d in range(4)]
+    return pieces[0], swap(pieces[1], 1), jnp.stack([swap(pieces[2], 2), swap(pieces[3], 3)])
+
+
+def reshard_wide(pieces_of, mine, replicas):
+    z = (lax.axis_index("rep") % 8) // 2
+    own, sibling = pieces_of(mine, 0, None), swap(pieces_of(mine ^ 1, 0, None), 1)
+    part = own.shape[0] // 4
+    far = [swap(pieces_of(mine ^ d, part * z, part), d) for d in (2, 3)]
+    far = lax.all_gather(jnp.stack(far), "rep", axis=0, axis_index_groups=planes_of(replicas))
+    return own, sibling, far
 
 
 def per_device(
@@ -367,186 +1510,180 @@
     replicas = lax.axis_size("rep")
     mine = lax.axis_index("grp")
     rows, width = x_input.shape[1], x_input.shape[2]
-    gains = lax.all_gather(norm_gain, "grp", axis=2, tiled=True).astype(f32)
-    taps_all = lax.all_gather(conv_w, "grp", axis=2, tiled=True).astype(f32)
-    out_gains = lax.all_gather(out_gain, "grp", axis=1, tiled=True).astype(f32)
-    ab_all = lax.all_gather(w_ab, "grp", axis=1, tiled=True)
-
-    def own(array, start, size):
-        return lax.dynamic_slice_in_dim(array, start + mine * size, size, array.ndim - 1)
-
-    layers = []
+    shard = w_in.shape[1]
+
+    def cut(array, start, size):
+        return lax.dynamic_slice_in_dim(array, start, size, array.ndim - 1)
+
+    small_sizes = [part.size for part in (norm_gain, conv_w, out_gain, w_ab)]
+    packed = jnp.concatenate(
+        [part.reshape(-1) for part in (norm_gain, conv_w, out_gain, w_ab)]
+    )
+    packed = jnp.stack([packed] + [swap(packed, d) for d in range(1, 4)])
+    packed = by_source(packed, mine)
+    at = [sum(small_sizes[:k]) for k in range(5)]
+
+    def unpack(k, shape, dim):
+        part = packed[:, at[k] : at[k + 1]].reshape((parts,) + shape)
+        part = jnp.moveaxis(part, 0, dim)
+        return part.reshape(shape[:dim] + (parts * shape[dim],) + shape[dim + 1 :])
+
+    gains = unpack(0, norm_gain.shape, 2).astype(f32)
+    taps_all = unpack(1, conv_w.shape, 2).astype(f32)
+    out_gains = unpack(2, out_gain.shape, 1).astype(f32)
+    ab_all = unpack(3, w_ab.shape, 1)
+
+    def in_pieces(l):
+        def piece(t, start, count):
+            rows = w_in[l] if count is None else lax.dynamic_slice_in_dim(w_in[l], start, count, 0)
+            return jnp.concatenate(
+                [
+                    cut(rows, 256 * t, 256),
+                    cut(rows, HK + 256 * t, 256),
+                    cut(rows, 2 * HK + 512 * t, 512),
+                    cut(rows, CH + 512 * t, 512),
+                ],
+                axis=1,
+            )
+
+        return piece
+
+    def up_pieces(l):
+        def piece(t, start, count):
+            rows = ffn_in[l]
+            if count is not None:
+                rows = lax.dynamic_slice_in_dim(rows, start, count, 0)
+            gate = cut(rows, 704 * t, 704)
+            value = cut(rows, FF + 704 * t, 704)
+            return jnp.concatenate(
+                [gate[:, :640], value[:, :640], gate[:, 640:], value[:, 640:]], axis=1
+            )
+
+        return piece
+
+    small_weights = []
     for l in range(LAYERS):
-        pieces = jnp.stack(
-            [
-                jnp.concatenate(
-                    [
-                        w_in[l][:, 256 * t : 256 * t + 256],
-                        w_in[l][:, HK + 256 * t : HK + 256 * t + 256],
-                        w_in[l][:, 2 * HK + 512 * t : 2 * HK + 512 * t + 512],
-                        w_in[l][:, CH + 512 * t : CH + 512 * t + 512],
-                    ],
-                    axis=1,
-                )
-                for t in range(4)
-            ]
-        )
-        in_weight = lax.all_to_all(pieces, "grp", 0, 0).reshape(width, 1536)
-        pieces = jnp.stack(
-            [
-                jnp.concatenate(
-                    [ffn_in[l][:, 704 * t : 704 * t + 704], ffn_in[l][:, FF + 704 * t : FF + 704 * t + 704]],
-                    axis=1,
-                )
-                for t in range(4)
-            ]
-        )
-        up_weight = lax.all_to_all(pieces, "grp", 0, 0).reshape(width, 1408)
-        ab = jnp.concatenate([own(ab_all[l], 0, 2), own(ab_all[l], H, 2)], axis=1)
+        ab = jnp.concatenate([cut(ab_all[l], 2 * mine, 2), cut(ab_all[l], H + 2 * mine, 2)], axis=1)
         ab = jnp.pad(ab, ((0, 0), (0, 124)))
         taps = jnp.concatenate(
-            [own(taps_all[l], 0, 256), own(taps_all[l], HK, 256), own(taps_all[l], 2 * HK, 512)], axis=1
+            [
+                cut(taps_all[l], 256 * mine, 256),
+                cut(taps_all[l], HK + 256 * mine, 256),
+                cut(taps_all[l], 2 * HK + 512 * mine, 512),
+            ],
+            axis=1,
         )
         taps = jnp.pad(taps, ((0, 4), (0, 0)))
-        heads = jnp.pad(
-            jnp.stack([a_log[l], dt_bias[l]]).astype(f32), ((0, 6), (2, 124))
-        )
+        heads = jnp.pad(jnp.stack([a_log[l], dt_bias[l]]).astype(f32), ((0, 6), (2, 124)))
         gain = jnp.pad(out_gains[l][None], ((0, 7), (0, 0)))
-        layers.append((gains[l], in_weight, ab, taps, heads, gain, w_out[l], up_weight, ffn_out[l]))
+        small_weights.append((gains[l, 0:1], gains[l, 1:2], ab, taps, heads, gain, w_out[l], ffn_out[l]))
 
     residual = x_input[0].astype(f32)
     kept = []
+    in_weights = [reshard_near(in_pieces(0), mine)]
+    up_weights = [reshard_wide(up_pieces(0), mine, replicas)]
+    in_weights.append(reshard_wide(in_pieces(1), mine, replicas))
+    up_weights.append(reshard_wide(up_pieces(1), mine, replicas))
     for l in range(LAYERS):
-        gain_pair, in_weight, ab, taps, heads, gain, out_weight, up_weight, down_weight = layers[l]
-        normed = gather_rows(rms_norm(residual, gain_pair[0]).astype(bf16))
-        projected = dot(normed, in_weight).astype(bf16)
-        small = dot(normed, ab)
+        gain_one, gain_two, ab, taps, heads, gain, out_weight, down_weight = small_weights[l]
+        normed, projected, small = project(residual, gain_one, in_weights[l], ab)
         gated, *saved = mixer_forward(projected, small, taps, heads, gain)
-        residual_mid = residual + scatter_rows(dot(gated, out_weight))
-        normed_two = gather_rows(rms_norm(residual_mid, gain_pair[1]).astype(bf16))
-        up_part = dot(normed_two, up_weight)
-        hidden = (jax.nn.silu(up_part[:, :704]) * up_part[:, 704:]).astype(bf16)
-        residual_out = residual_mid + scatter_rows(dot(hidden, down_weight))
-        kept.append((residual, normed, projected, small, gated, saved, residual_mid, normed_two, up_part, hidden))
+        mid, normed_two, up, hidden, residual_out = ffn_forward(
+            gated, out_weight, residual, gain_two, down_weight, up_weights[l]
+        )
+        kept.append((residual, normed, projected, small, gated, saved, mid, normed_two, up, hidden))
         residual = residual_out
     block_output = residual.astype(bf16)[None]
 
     d_residual = cotangent[0].astype(f32)
-    big = [None] * LAYERS
-    small_grads = [None] * LAYERS
-    for l in reversed(range(LAYERS)):
-        gain_pair, in_weight, ab, taps, heads, gain, out_weight, up_weight, down_weight = layers[l]
-        residual, normed, projected, small, gated, saved, residual_mid, normed_two, up_part, hidden = kept[l]
-        d_down = gather_rows(d_residual.astype(bf16))
-        g_down = dot(hidden, d_down, TN).astype(bf16)
-        d_hidden = dot(d_down, down_weight, NT)
-        gate, up = up_part[:, :704], up_part[:, 704:]
-        sig = jax.nn.sigmoid(gate)
-        d_up = jnp.concatenate(
-            [d_hidden * up * (sig * (1.0 + gate * (1.0 - sig))), d_hidden * gate * sig], axis=1
-        ).astype(bf16)
-        g_up = dot(normed_two, d_up, TN).astype(bf16)
-        d_normed_two = scatter_rows(dot(d_up, up_weight, NT))
-        d_norm, g_gain_two = norm_back(residual_mid, gain_pair[1], d_normed_two)
-        d_mid = d_residual + d_norm
-        d_branch = gather_rows(d_mid.astype(bf16))
-        g_out = dot(gated, d_branch, TN).astype(bf16)
-        d_gated = dot(d_branch, out_weight, NT).astype(bf16)
-        d_projected, d_small, g_taps, g_heads = mixer_backward(
-            projected, small, taps, heads, gain, saved, d_gated
-        )
-        g_in = dot(normed, d_projected, TN).astype(bf16)
-        g_ab = dot(normed, d_small, TN)[:, :4]
-        d_normed = scatter_rows(dot(d_projected, in_weight, NT) + dot(d_small, ab, NT))
-        d_norm, g_gain_one = norm_back(residual, gain_pair[0], d_normed)
-        d_residual = d_mid + d_norm
-        small_grads[l] = (g_gain_one, g_gain_two, g_ab, g_taps, g_heads)
-        big[l] = (g_in, g_up, g_out, g_down)
+
+    def ffn_part(l, d_residual):
+        gain_one, gain_two, ab, taps, heads, gain, out_weight, down_weight = small_weights[l]
+        residual, normed, projected, small, gated, saved, mid, normed_two, up, hidden = kept[l]
+        return ffn_backward(
+            d_residual, up, hidden, normed_two, mid, gain_two, gated, out_weight, down_weight,
+            up_weights[l],
+        )
+
+    def mixer_part(l, d_gated):
+        gain_one, gain_two, ab, taps, heads, gain, out_weight, down_weight = small_weights[l]
+        residual, normed, projected, small, gated, saved, mid, normed_two, up, hidden = kept[l]
+        return mixer_backward(projected, small, taps, heads, gain, saved, d_gated)
+
+    def project_part(l, d_mid, g_gain_two, mixed):
+        gain_one, gain_two, ab, taps, heads, gain, out_weight, down_weight = small_weights[l]
+        residual, normed, projected, small, gated, saved, mid, normed_two, up, hidden = kept[l]
+        d_projected, d_small, g_taps, g_heads = mixed
+        return project_backward(
+            d_projected, d_small, in_weights[l], ab, normed, residual, gain_one, d_mid,
+            g_gain_two, g_taps, g_heads,
+        )
+
+    d_mid, d_gated, g_gain_two, buf1 = ffn_part(1, d_residual)
+    arrived1 = swap_x(buf1[1], replicas)
+    mixed = mixer_part(1, d_gated)
+    d_residual, buf2 = project_part(1, d_mid, g_gain_two, mixed)
+    d_residual, arrived1 = tie(d_residual, arrived1)
+    piece1 = reduce_z(add_arrived(buf1[0], arrived1), replicas)
+    arrived2 = swap_x(buf2[1], replicas)
+    d_mid, d_gated, g_gain_two, buf3 = ffn_part(0, d_residual)
+    d_gated, piece1, arrived2 = tie(d_gated, piece1, arrived2)
+    piece2 = reduce_z(add_arrived(buf2[0], arrived2), replicas)
+    arrived3 = swap_x(buf3[1], replicas)
+    mixed = mixer_part(0, d_gated)
+    d_residual, buf4 = project_part(0, d_mid, g_gain_two, mixed)
+    d_residual, arrived3 = tie(d_residual, arrived3)
+    summed3 = add_arrived(buf3[0], arrived3)
+    final1, final2, final3, final4 = finish_all(piece1, piece2, summed3, buf4, replicas)
+    ffn_grads = assemble_ffn(1, final1, ())
+    *in_grads, table_one = assemble_in(1, final2, ())
+    down_grads, out_grads, up_grads = assemble_ffn(0, final3, tuple(ffn_grads))
+    w_in_grads, table_zero = assemble_in(0, final4, tuple(in_grads))
     input_grad = d_residual.astype(bf16)[None]
 
-    w_in_grads, up_grads, out_grads, down_grads = [], [], [], []
-    for l in range(LAYERS):
-        g_in, g_up, g_out, g_down = big[l]
-
-        def columns(grad):
-            part = rows // replicas
-            grad = grad.reshape(parts, replicas, part, grad.shape[1])
-            grad = lax.psum_scatter(jnp.moveaxis(grad, 1, 0), "rep", scatter_dimension=0, tiled=False)
-            grad = lax.all_to_all(grad, "grp", 0, 0)
-            grad = lax.all_gather(grad, "rep", axis=0)
-            return jnp.moveaxis(grad, 1, 0).reshape(parts, rows, -1)
-
-        def plain(grad):
-            grad = lax.psum_scatter(grad, "rep", scatter_dimension=0, tiled=True)
-            return lax.all_gather(grad, "rep", axis=0, tiled=True)
-
-        blocks = columns(g_in)
-        w_in_grads.append(
-            jnp.concatenate(
-                [blocks[t][:, 0:256] for t in range(4)]
-                + [blocks[t][:, 256:512] for t in range(4)]
-                + [blocks[t][:, 512:1024] for t in range(4)]
-                + [blocks[t][:, 1024:1536] for t in range(4)],
-                axis=1,
-            ).astype(f32)
-        )
-        blocks = columns(g_up)
-        up_grads.append(
-            jnp.concatenate(
-                [blocks[t][:, :704] for t in range(4)] + [blocks[t][:, 704:] for t in range(4)], axis=1
-            ).astype(f32)
-        )
-        joint = plain(jnp.concatenate([g_out, g_down], axis=0))
-        out_grads.append(joint[:512].astype(f32))
-        down_grads.append(joint[512:].astype(f32))
-
-    def spread(piece, full, at):
-        zero = jnp.zeros(piece.shape[:-1] + (full,), f32)
-        return lax.dynamic_update_slice_in_dim(zero, piece, at, piece.ndim - 1)
-
-    packed = []
-    for l in range(LAYERS):
-        g_gain_one, g_gain_two, g_ab, g_taps, g_heads = small_grads[l]
-        packed.append(g_gain_one)
-        packed.append(g_gain_two)
-        packed.append(g_heads[0])
-        packed.append(spread(g_heads[1, 2:4], H, 2 * mine))
-        packed.append(spread(g_heads[2, 2:4], H, 2 * mine))
-        packed.append(spread(g_taps[:4, :256], HK, 256 * mine))
-        packed.append(spread(g_taps[:4, 256:512], HK, 256 * mine))
-        packed.append(spread(g_taps[:4, 512:], HV, 512 * mine))
-        packed.append(spread(g_ab[:, :2], H, 2 * mine))
-        packed.append(spread(g_ab[:, 2:], H, 2 * mine))
-    flat = lax.psum(jnp.concatenate([piece.reshape(-1) for piece in packed]), ("rep", "grp"))
-    sums, at = [], 0
-    for piece in packed:
-        sums.append(flat[at : at + piece.size].reshape(piece.shape))
-        at += piece.size
-    per_layer = [sums[10 * l : 10 * l + 10] for l in range(LAYERS)]
-
-    def owned(array, dim):
-        size = array.shape[dim] // parts
-        return lax.dynamic_slice_in_dim(array, mine * size, size, dim)
-
-    grad_gain = owned(jnp.stack([jnp.stack([p[0], p[1]]) for p in per_layer]), 2)
-    grad_out_gain = owned(jnp.stack([p[2] for p in per_layer]), 1)
-    grad_a_log = owned(jnp.stack([p[3] for p in per_layer]), 1)
-    grad_dt = owned(jnp.stack([p[4] for p in per_layer]), 1)
-    grad_conv = owned(jnp.stack([jnp.concatenate(p[5:8], axis=1) for p in per_layer]), 2)
-    grad_ab = owned(jnp.stack([jnp.concatenate(p[8:10], axis=1) for p in per_layer]), 1)
+    tables = jnp.stack([table_zero, table_one])
+    everyone = lax.all_gather(tables, "grp", axis=0)
+    sums = jnp.sum(everyone[:, :, 64:82], axis=0)
+    grad_gain = lax.dynamic_slice_in_dim(
+        sums[:, :16].reshape(LAYERS, 2, width), mine * shard, shard, 2
+    )
+    grad_out_gain = lax.dynamic_slice_in_dim(
+        sums[:, 16:18].reshape(LAYERS, DV), mine * (DV // 4), DV // 4, 1
+    )
+    grad_a_log = tables[:, 82, 2:4]
+    grad_dt = tables[:, 83, 2:4]
+    taps_sum = everyone[:, :, 0:32].reshape(4, LAYERS, 4, 1024)
+
+    def side_by_side(array):
+        return jnp.moveaxis(array, 0, 2).reshape(LAYERS, 4, -1)
+
+    conv_full = jnp.concatenate(
+        [
+            side_by_side(taps_sum[..., :256]),
+            side_by_side(taps_sum[..., 256:512]),
+            side_by_side(taps_sum[..., 512:]),
+        ],
+        axis=2,
+    )
+    grad_conv = lax.dynamic_slice_in_dim(conv_full, mine * 1024, 1024, 2)
+    ab_sum = everyone[:, :, 32:64].reshape(4, LAYERS, 4, width)
+    ab_sum = lax.dynamic_slice_in_dim(ab_sum, mine * shard, shard, 3)
+    grad_ab = jnp.transpose(ab_sum.reshape(4, LAYERS, 2, 2, shard), (1, 4, 2, 0, 3)).reshape(
+        LAYERS, shard, 2 * H
+    )
     return (
         block_output,
         input_grad,
         grad_gain,
-        jnp.stack(w_in_grads),
+        w_in_grads,
         grad_ab,
         grad_conv,
         grad_a_log,
         grad_dt,
         grad_out_gain,
-        jnp.stack(out_grads),
-        jnp.stack(up_grads),
-        jnp.stack(down_grads),
+        out_grads,
+        up_grads,
+        down_grads,
     )
 
 

time: 1910 us -> 914 us (0.48)
  waiting for transfers between devices: 1130 us -> 31.6 us
  Pallas kernels: 229 us -> 709 us
  blocking collectives: 187 us -> 9.2 us
  matrix products: 125 us -> 0 us
  other arithmetic: 79 us -> 37.3 us
  local copies, waits for them, and re-layouts: 116 us -> 84 us
    pallas_call x0 -> x13, Pallas kernels: none -> 559 us  [the longest x8 272 us: call(): pl.pallas_call(kernel, out_shape=out_shape, in_specs=[vmem] * len(inputs)...]
    unnamed x27 -> x5, waiting for transfers between devices: 388 us -> 0.08 us
    all_gather x14 -> x3, waiting for transfers between devices: 319 us -> 0.02 us  [reshard_wide(): lax.all_gather(jnp.stack(far), 'rep', axis=0, axis_index_groups=planes_of...]
    reduce_scatter x10 -> x2, waiting for transfers between devices: 260 us -> 0.01 us  [reduce_z(): lax.psum_scatter(summed, 'rep', scatter_dimension=0, tiled=False, axis_in...]
    dot_general x30 -> x0, matrix products: 125 us -> none  [mm(): lax.dot_general(left, right, (dims, ((), ())), precision=precision, prefe...]
    all_to_all x4 -> x0, blocking collectives: 124 us -> none  [the longest x2 104 us: per_device(): up_weight = lax.all_to_all(pieces, 'grp', 0, 0).reshape(width, 1408)]
    psum x1 -> x0, waiting for transfers between devices: 122 us -> none  [per_device(): lax.psum(jnp.concatenate([piece.reshape(-1) for piece in packed]), ('rep'...]
    pallas_call x2, Pallas kernels: 138 us -> 58.5 us  [mixer_forward(): pl.pallas_call(mixer_forward_kernel, out_shape=(jax.ShapeDtypeStruct((tok...]
  transfers between devices with their start and end apart: 30 -> 23, of which waited for: 21 -> 4; matrix products, arithmetic and copies ran while one was open for 11% -> 10% of each run, Pallas kernels for 2% -> 36%
where the time goes in v2:
time: 914 us; the launch traced here: 905 us
  Pallas kernels  709 us (78%)
  local copies, waits for them, and re-layouts  84 us (9%)
  other arithmetic  37.3 us (4%)
  waiting for transfers between devices  31.6 us (3%)
  starting transfers between devices  18.7 us (2%)
  between operations  15.1 us (2%)
  blocking collectives  9.2 us (1%)
    pallas_call x8, Pallas kernels, call(): pl.pallas_call(kernel, out_shape=out_shape, in_specs=[vmem] * len(inputs)...  272 us
    pallas_call x1, Pallas kernels, finish_reduction(): pl.pallas_call(finish_kernel, out_shape=tuple((like(8, *shape, dtype=bf16...  261 us
    pallas_call x2, Pallas kernels, mixer_backward(): pl.pallas_call(mixer_backward_kernel, out_shape=(jax.ShapeDtypeStruct((to...  90.8 us
    pallas_call x2, Pallas kernels, mixer_forward(): pl.pallas_call(mixer_forward_kernel, out_shape=(jax.ShapeDtypeStruct((tok...  58.5 us
    ppermute x15, waiting for transfers between devices, swap(): return lax.ppermute(array, 'grp', swap_route(d, 4))  31.5 us
    pallas_call x4, Pallas kernels, assemble(): pl.pallas_call(partial(kernel, layer, len(earlier)), out_shape=out_shape,...  26.3 us
    unnamed x124, local copies, waits for them, and re-layouts  20.7 us
  transfers between devices with their start and end apart: 23, of which 4 were waited for; matrix products, arithmetic and copies ran while one was open for 10% of the time, Pallas kernels for 36%

profile of v2, /device:TPU:0, one launch (start us, length us, event | category | flops | bytes accessed | tf_op | source)
XLA Modules:
  0.0 904.7 jit_solution(13239540410637011316)
XLA Ops:
  14.4 3.0 collective-permute-start.2
  17.6 4.6 fusion.28
  22.2 3.1 dynamic-slice_bitcast_fusion.34
  38.7 3.2 slice_bitcast_fusion.5
  46.0 5.2 dynamic-slice_bitcast_fusion
  84.8 5.2 collective-permute-done.11
  91.9 3.4 collective-permute-done.10
  103.9 7.3 collective-permute-done.5
  113.0 15.5 %collective-permute-done.4 = bf16[256,1536]{1,0:T(8,128)(2,1)} collective-permute-done((bf16[256,1536]{1,0:T(8,128)(2,1)}, bf16[256,1536]{1,0:T(8,128)(2,1)}, u32[]{:S(2)}, u32[]{:S(2)}) %collective-permute-start.4) | collective-permute-done | bytes 786464 | tf_op jit(solution)/shard_map/ppermute | solution.py:1488
  132.3 19.8 %project.2 = (bf16[1024,1024]{1,0:T(8,128)(2,1)}, bf16[1024,1536]{1,0:T(8,128)(2,1)}, f32[1024,128]{1,0:T(8,128)}) custom-call(f32[256,1024]{1,0:T(8,128)} %bitcast_convert_fusion.1.res_ref, f32[1,1024]{1,0:T(1,128)} %get-tuple-element.253.gain_ref, bf16[1024,128]{1,0:T(8,128)(2,1)} %pad.32.ab_ref, bf16[256,1536]{1,0:T(8,128)(2,1)} %pad_maximum_fusion.1.own_ref, ...), custom_call_target="tpu_custom_call" | custom-call | flops 1000 | bytes 1000 | tf_op jit(solution)/shard_map/project/pallas_call | solution.py:511
  153.2 29.2 %mixer_forward.2 = (bf16[1024,512]{1,0:T(8,128)(2,1)S(1)}, f32[8,2,128,256]{3,2,1,0:T(8,128)S(1)}, f32[8,2,128,128]{3,2,1,0:T(8,128)S(1)}, f32[8,2,128,256]{3,2,1,0:T(8,128)}, f32[1024,512]{1,0:T(8,128)}) custom-call(bf16[1024,1536]{1,0:T(8,128)(2,1)} %get-tuple-element.79.proj_ref, f32[1024,128]{1,0:T(8,128)S(1)} %copy-done.4, ...), custom_call_target="tpu_custom_call" | custom-call | tf_op jit(solution)/shard_map/mixer_forward/pallas_call | solution.py:190
  184.4 44.5 %ffn_forward.2 = (f32[256,1024]{1,0:T(8,128)}, bf16[1024,1024]{1,0:T(8,128)(2,1)}, bf16[1024,1408]{1,0:T(8,128)(2,1)}, bf16[1024,768]{1,0:T(8,128)(2,1)}, f32[256,1024]{1,0:T(8,128)}) custom-call(bf16[1024,512]{1,0:T(8,128)(2,1)} %copy-done, bf16[512,1024]{1,0:T(8,128)(2,1)} %get-tuple-element.227.wout_ref, f32[256,1024]{1,0:T(8,128)} %bitcast_convert_fusion.1.res_ref, ...), custom_call_target="tpu_custom_call" | custom-call | flops 1000 | bytes 1000 | tf_op jit(solution)/shard_map/ffn_forward/pallas_call | solution.py:511
  229.7 18.9 %project.3 = (bf16[1024,1024]{1,0:T(8,128)(2,1)}, bf16[1024,1536]{1,0:T(8,128)(2,1)}, f32[1024,128]{1,0:T(8,128)}) custom-call(f32[256,1024]{1,0:T(8,128)} %get-tuple-element.82.res_ref, f32[1,1024]{1,0:T(1,128)} %get-tuple-element.251.gain_ref, bf16[1024,128]{1,0:T(8,128)(2,1)} %pad.37.ab_ref, bf16[256,1536]{1,0:T(8,128)(2,1)} %pad_maximum_fusion.5.own_ref, ...), custom_call_target="tpu_custom_call" | custom-call | flops 1000 | bytes 1000 | tf_op jit(solution)/shard_map/project/pallas_call | solution.py:511
  249.7 29.3 %mixer_forward.3 = (bf16[1024,512]{1,0:T(8,128)(2,1)S(1)}, f32[8,2,128,256]{3,2,1,0:T(8,128)S(1)}, f32[8,2,128,128]{3,2,1,0:T(8,128)S(1)}, f32[8,2,128,256]{3,2,1,0:T(8,128)}, f32[1024,512]{1,0:T(8,128)}) custom-call(bf16[1024,1536]{1,0:T(8,128)(2,1)} %get-tuple-element.83.proj_ref, f32[1024,128]{1,0:T(8,128)S(1)} %copy-done.6, ...), custom_call_target="tpu_custom_call" | custom-call | tf_op jit(solution)/shard_map/mixer_forward/pallas_call | solution.py:190
  281.3 44.4 %ffn_forward.3 = (f32[256,1024]{1,0:T(8,128)}, bf16[1024,1024]{1,0:T(8,128)(2,1)}, bf16[1024,1408]{1,0:T(8,128)(2,1)}, bf16[1024,768]{1,0:T(8,128)(2,1)}, f32[256,1024]{1,0:T(8,128)}) custom-call(bf16[1024,512]{1,0:T(8,128)(2,1)} %copy-done.1, bf16[512,1024]{1,0:T(8,128)(2,1)} %get-tuple-element.226.wout_ref, f32[256,1024]{1,0:T(8,128)} %get-tuple-element.82.res_ref, ...), custom_call_target="tpu_custom_call" | custom-call | flops 1000 | bytes 1000 | tf_op jit(solution)/shard_map/ffn_forward/pallas_call | solution.py:511
  325.7 48.3 %ffn_backward.2 = (f32[256,1024]{1,0:T(8,128)}, bf16[1024,512]{1,0:T(8,128)(2,1)}, f32[8,1024]{1,0:T(8,128)}, bf16[2,4,2624,128]{3,2,1,0:T(8,128)(2,1)}) custom-call(f32[256,1024]{1,0:T(8,128)} %bitcast_convert_fusion.dres_ref, bf16[1024,1408]{1,0:T(8,128)(2,1)} %get-tuple-element.95.up_ref, bf16[1024,768]{1,0:T(8,128)(2,1)} %get-tuple-element.96.hidden_ref, ...), custom_call_target="tpu_custom_call" | custom-call | flops 1000 | bytes 1000 | tf_op jit(solution)/shard_map/ffn_backward/pallas_call | solution.py:511
  374.0 3.6 slice_bitcast_fusion.1
  379.1 45.2 %mixer_backward.2 = (bf16[1024,1536]{1,0:T(8,128)(2,1)}, bf16[1024,128]{1,0:T(8,128)(2,1)S(1)}, f32[8,1024]{1,0:T(8,128)S(1)}, f32[8,256]{1,0:T(8,128)S(1)}) custom-call(bf16[1024,1536]{1,0:T(8,128)(2,1)} %get-tuple-element.83.proj_ref, f32[1024,128]{1,0:T(8,128)S(1)} %copy-done.7, f32[8,1024]{1,0:T(8,128)S(1)} %select_maximum_fusion.taps_ref, ...), custom_call_target="tpu_custom_call" | custom-call | tf_op jit(solution)/shard_map/mixer_backward/pallas_call | solution.py:351
  426.3 23.8 %project_backward.2 = (f32[256,1024]{1,0:T(8,128)}, bf16[2,4,1552,128]{3,2,1,0:T(8,128)(2,1)}) custom-call(bf16[1024,1536]{1,0:T(8,128)(2,1)} %get-tuple-element.100.dproj_ref, bf16[1024,128]{1,0:T(8,128)(2,1)} %copy-done.12, bf16[1024,128]{1,0:T(8,128)(2,1)} %pad.37.ab_ref, bf16[1024,1024]{1,0:T(8,128)(2,1)} %get-tuple-element.102.normed_ref, ...), custom_call_target="tpu_custom_call" | custom-call | flops 1000 | bytes 1000 | tf_op jit(solution)/shard_map/project_backward/pallas_call | solution.py:511
  450.1 4.0 fusion.1
  456.6 48.3 %ffn_backward.3 = (f32[256,1024]{1,0:T(8,128)}, bf16[1024,512]{1,0:T(8,128)(2,1)}, f32[8,1024]{1,0:T(8,128)}, bf16[2,4,2624,128]{3,2,1,0:T(8,128)(2,1)}) custom-call(f32[256,1024]{1,0:T(8,128)} %get-tuple-element.109.dres_ref, bf16[1024,1408]{1,0:T(8,128)(2,1)} %get-tuple-element.110.up_ref, bf16[1024,768]{1,0:T(8,128)(2,1)} %get-tuple-element.111.hidden_ref, ...), custom_call_target="tpu_custom_call" | custom-call | flops 1000 | bytes 1000 | tf_op jit(solution)/shard_map/ffn_backward/pallas_call | solution.py:511
  505.0 3.4 slice_bitcast_fusion
  510.0 3.5 fusion.2
  518.1 45.6 %mixer_backward.3 = (bf16[1024,1536]{1,0:T(8,128)(2,1)}, bf16[1024,128]{1,0:T(8,128)(2,1)S(1)}, f32[8,1024]{1,0:T(8,128)S(1)}, f32[8,256]{1,0:T(8,128)S(1)}) custom-call(bf16[1024,1536]{1,0:T(8,128)(2,1)} %get-tuple-element.79.proj_ref, f32[1024,128]{1,0:T(8,128)S(1)} %copy-done.5, f32[8,1024]{1,0:T(8,128)S(1)} %select_maximum_fusion.2.taps_ref, ...), custom_call_target="tpu_custom_call" | custom-call | tf_op jit(solution)/shard_map/mixer_backward/pallas_call | solution.py:351
  565.6 24.6 %project_backward.3 = (f32[256,1024]{1,0:T(8,128)}, bf16[2,4,1552,128]{3,2,1,0:T(8,128)(2,1)}) custom-call(bf16[1024,1536]{1,0:T(8,128)(2,1)} %get-tuple-element.118.dproj_ref, bf16[1024,128]{1,0:T(8,128)(2,1)} %copy-done.13, bf16[1024,128]{1,0:T(8,128)(2,1)} %pad.32.ab_ref, bf16[1024,1024]{1,0:T(8,128)(2,1)} %get-tuple-element.120.normed_ref, ...), custom_call_target="tpu_custom_call" | custom-call | flops 1000 | bytes 1000 | tf_op jit(solution)/shard_map/project_backward/pallas_call | solution.py:511
  592.3 4.0 fusion.s3
  596.2 260.7 %finish_reduction.1 = (bf16[8,2624,128]{2,1,0:T(8,128)(2,1)}, bf16[8,1552,128]{2,1,0:T(8,128)(2,1)}, bf16[8,2624,128]{2,1,0:T(8,128)(2,1)}, bf16[8,1552,128]{2,1,0:T(8,128)(2,1)}) custom-call(bf16[2624,128]{1,0:T(8,128)(2,1)} %bitcast.219, bf16[1552,128]{1,0:T(8,128)(2,1)} %bitcast.221, bf16[4,2624,128]{2,1,0:T(8,128)(2,1)} %fusion.s3, ...), custom_call_target="tpu_custom_call" | custom-call | flops 1000 | bytes 1000 | tf_op jit(solution)/shard_map/finish_reduction/pallas_call | solution.py:1390
  856.9 6.0 assemble_in.2
  862.9 6.0 assemble_in.3
  871.2 9.2 %all-gather.3 = f32[8,128,128]{2,1,0:T(8,128)S(1)} all-gather(f32[2,128,128]{2,1,0:T(8,128)S(1)} %pad_maximum_fusion.12), channel_id=5, replica_groups=mesh['rep'=8,'grp'=4] {'grp'}, dimensions={0}, use_global_device_ids=true | all-gather | bytes 655360 | tf_op jit(solution)/shard_map/all_gather | solution.py:1645
  882.1 7.2 assemble_ffn.2
  890.6 7.2 assemble_ffn.3
  (295 shorter events, 102.6 us)
Async XLA Ops:
  7.2 177.2 %all-gather.8.cloned.1.call-start = ((), (), s32[]{:S(2)}) async-start(), calls=%async_computation.4 | async-start | bytes 1802240 | tf_op jit(solution)/shard_map/all_gather | solution.py:1501
  14.4 61.2 %collective-permute-start.2 = (bf16[17536]{0:T(1024)(128)(2,1)}, bf16[17536]{0:T(1024)(128)(2,1)}, u32[]{:S(2)}, u32[]{:S(2)}) collective-permute-start(bf16[17536]{0:T(1024)(128)(2,1)} %dynamic-update-slice.3), channel_id=1, source_target_pairs={{0,2},{1,3},{2,0},{3,1},{4,6},{5,7},{6,4},{7,5},{8,10},{9,11},{10,... | collective-permute-start | bytes 105224 | tf_op jit(solution)/shard_map/ppermute | solution.py:1488
  17.4 60.4 %collective-permute-start.1 = (bf16[17536]{0:T(1024)(128)(2,1)}, bf16[17536]{0:T(1024)(128)(2,1)}, u32[]{:S(2)}, u32[]{:S(2)}) collective-permute-start(bf16[17536]{0:T(1024)(128)(2,1)} %dynamic-update-slice.3), channel_id=1, source_target_pairs={{0,3},{1,2},{2,1},{3,0},{4,7},{5,6},{6,5},{7,4},{8,11},{9,10},{10,... | collective-permute-start | bytes 105224 | tf_op jit(solution)/shard_map/ppermute | solution.py:1488
  17.4 61.7 %collective-permute-start = (bf16[17536]{0:T(1024)(128)(2,1)}, bf16[17536]{0:T(1024)(128)(2,1)}, u32[]{:S(2)}, u32[]{:S(2)}) collective-permute-start(bf16[17536]{0:T(1024)(128)(2,1)} %dynamic-update-slice.3), channel_id=1, source_target_pairs={{0,1},{1,0},{2,3},{3,2},{4,5},{5,4},{6,7},{7,6},{8,9},{9,8},{10,11... | collective-permute-start | bytes 105224 | tf_op jit(solution)/shard_map/ppermute | solution.py:1488
  22.2 16.5 %copy-start.19 = (bf16[1,256,5632]{2,1,0:T(8,128)(2,1)}, bf16[1,256,5632]{2,1,0:T(8,128)(2,1)S(1)}, u32[]{:S(2)}) copy-start(bf16[1,256,5632]{2,1,0:T(8,128)(2,1)S(1)} %get-tuple-element.174) | copy-start | bytes 8650756
  22.2 12.6 %copy-start.31 = (bf16[1,256,1024]{2,1,0:T(8,128)(2,1)S(1)}, bf16[1,256,1024]{2,1,0:T(8,128)(2,1)}, u32[]{:S(2)}) copy-start(bf16[1,256,1024]{2,1,0:T(8,128)(2,1)} %param.12) | copy-start | bytes 1572868
  28.2 52.8 %collective-permute-start.7 = (bf16[64,1408]{1,0:T(8,128)(2,1)}, bf16[64,1408]{1,0:T(8,128)(2,1)}, u32[]{:S(2)}, u32[]{:S(2)}) collective-permute-start(bf16[64,1408]{1,0:T(8,128)(2,1)} %concatenate.75), channel_id=1, source_target_pairs={{0,2},{1,3},{2,0},{3,1},{4,6},{5,7},{6,4},{7,5},{8,10},{9,11},{10,... | collective-permute-start | bytes 540680 | tf_op jit(solution)/shard_map/ppermute | solution.py:1488
  34.8 47.7 %collective-permute-start.8 = (bf16[64,1408]{1,0:T(8,128)(2,1)}, bf16[64,1408]{1,0:T(8,128)(2,1)}, u32[]{:S(2)}, u32[]{:S(2)}) collective-permute-start(bf16[64,1408]{1,0:T(8,128)(2,1)} %concatenate.76), channel_id=1, source_target_pairs={{0,3},{1,2},{2,1},{3,0},{4,7},{5,6},{6,5},{7,4},{8,11},{9,10},{10,... | collective-permute-start | bytes 540680 | tf_op jit(solution)/shard_map/ppermute | solution.py:1488
  34.9 8.9 slice-start
  56.4 9.3 %copy-start.29 = (bf16[256,704]{1,0:T(8,128)(2,1)S(1)}, bf16[256,704]{1,0:T(8,128)(2,1)}, u32[]{:S(2)}) copy-start(bf16[256,704]{1,0:T(8,128)(2,1)} %get-tuple-element.212) | copy-start | bytes 1081348
  57.3 8.5 copy-start.27
  72.5 8.6 copy-start.42
  72.5 10.1 %copy-start.41 = (bf16[64,1536]{1,0:T(8,128)(2,1)S(1)}, bf16[64,1536]{1,0:T(8,128)(2,1)}, u32[]{:S(2)}) copy-start(bf16[64,1536]{1,0:T(8,128)(2,1)} %pad_maximum_fusion.10) | copy-start | bytes 589828
  75.7 22.8 %collective-permute-start.13 = (bf16[64,1408]{1,0:T(8,128)(2,1)S(1)}, bf16[64,1408]{1,0:T(8,128)(2,1)S(1)}, u32[]{:S(2)}, u32[]{:S(2)}) collective-permute-start(bf16[64,1408]{1,0:T(8,128)(2,1)S(1)} %copy-done.43), channel_id=1, source_target_pairs={{0,2},{1,3},{2,0},{3,1},{4,6},{5,7},{6,4},{7,5},{8,10},{9,11},{10,... | collective-permute-start | bytes 540680 | tf_op jit(solution)/shard_map/ppermute | solution.py:1488
  77.8 20.7 %collective-permute-start.14 = (bf16[64,1408]{1,0:T(8,128)(2,1)S(1)}, bf16[64,1408]{1,0:T(8,128)(2,1)S(1)}, u32[]{:S(2)}, u32[]{:S(2)}) collective-permute-start(bf16[64,1408]{1,0:T(8,128)(2,1)S(1)} %concatenate.86), channel_id=1, source_target_pairs={{0,3},{1,2},{2,1},{3,0},{4,7},{5,6},{6,5},{7,4},{8,11},{9,10},{10,... | collective-permute-start | bytes 540680 | tf_op jit(solution)/shard_map/ppermute | solution.py:1488
  79.1 105.3 %collective-permute-start.6 = (bf16[256,1408]{1,0:T(8,128)(2,1)}, bf16[256,1408]{1,0:T(8,128)(2,1)}, u32[]{:S(2)}, u32[]{:S(2)}) collective-permute-start(bf16[256,1408]{1,0:T(8,128)(2,1)} %concatenate.74), channel_id=1, source_target_pairs={{0,1},{1,0},{2,3},{3,2},{4,5},{5,4},{6,7},{7,6},{8,9},{9,8},{10,11... | collective-permute-start | bytes 2162696 | tf_op jit(solution)/shard_map/ppermute | solution.py:1488
  81.1 8.9 collective-permute-start.11
  82.6 12.7 %collective-permute-start.10 = (bf16[64,1536]{1,0:T(8,128)(2,1)S(1)}, bf16[64,1536]{1,0:T(8,128)(2,1)S(1)}, u32[]{:S(2)}, u32[]{:S(2)}) collective-permute-start(bf16[64,1536]{1,0:T(8,128)(2,1)S(1)} %copy-done.41), channel_id=1, source_target_pairs={{0,2},{1,3},{2,0},{3,1},{4,6},{5,7},{6,4},{7,5},{8,10},{9,11},{10,... | collective-permute-start | bytes 589832 | tf_op jit(solution)/shard_map/ppermute | solution.py:1488
  84.7 144.2 %all-gather.10.cloned.1.call-start = ((), (), s32[]{:S(2)}) async-start(), calls=%async_computation.5 | async-start | bytes 1966080 | tf_op jit(solution)/shard_map/all_gather | solution.py:1501
  90.0 21.2 %collective-permute-start.5 = (bf16[256,1536]{1,0:T(8,128)(2,1)}, bf16[256,1536]{1,0:T(8,128)(2,1)}, u32[]{:S(2)}, u32[]{:S(2)}) collective-permute-start(bf16[256,1536]{1,0:T(8,128)(2,1)} %pad_maximum_fusion.4), channel_id=1, source_target_pairs={{0,3},{1,2},{2,1},{3,0},{4,7},{5,6},{6,5},{7,4},{8,11},{9,10},{10,... | collective-permute-start | bytes 2359304 | tf_op jit(solution)/shard_map/ppermute | solution.py:1488
  95.3 33.3 %collective-permute-start.4 = (bf16[256,1536]{1,0:T(8,128)(2,1)}, bf16[256,1536]{1,0:T(8,128)(2,1)}, u32[]{:S(2)}, u32[]{:S(2)}) collective-permute-start(bf16[256,1536]{1,0:T(8,128)(2,1)} %pad_maximum_fusion.3), channel_id=1, source_target_pairs={{0,2},{1,3},{2,0},{3,1},{4,6},{5,7},{6,4},{7,5},{8,10},{9,11},{10,... | collective-permute-start | bytes 2359304 | tf_op jit(solution)/shard_map/ppermute | solution.py:1488
  97.5 183.8 %all-gather.12.cloned.1.call-start = ((), (), s32[]{:S(2)}) async-start(), calls=%async_computation.6 | async-start | bytes 1802240 | tf_op jit(solution)/shard_map/all_gather | solution.py:1501
  98.5 32.9 %collective-permute-start.3 = (bf16[256,1536]{1,0:T(8,128)(2,1)}, bf16[256,1536]{1,0:T(8,128)(2,1)S(1)}, u32[]{:S(2)}, u32[]{:S(2)}) collective-permute-start(bf16[256,1536]{1,0:T(8,128)(2,1)} %pad_maximum_fusion.2), channel_id=1, source_target_pairs={{0,1},{1,0},{2,3},{3,2},{4,5},{5,4},{6,7},{7,6},{8,9},{9,8},{10,11... | collective-permute-start | bytes 2359304 | tf_op jit(solution)/shard_map/ppermute | solution.py:1488
  98.5 130.3 %collective-permute-start.9 = (bf16[256,1536]{1,0:T(8,128)(2,1)}, bf16[256,1536]{1,0:T(8,128)(2,1)S(1)}, u32[]{:S(2)}, u32[]{:S(2)}) collective-permute-start(bf16[256,1536]{1,0:T(8,128)(2,1)} %pad_maximum_fusion.6), channel_id=1, source_target_pairs={{0,1},{1,0},{2,3},{3,2},{4,5},{5,4},{6,7},{7,6},{8,9},{9,8},{10,11... | collective-permute-start | bytes 2359304 | tf_op jit(solution)/shard_map/ppermute | solution.py:1488
  99.8 410.2 %reduce-scatter.3.cloned.1.call-start = ((), (), s32[]{:S(2)}) async-start(), calls=%async_computation.2 | async-start | bytes 3358720 | tf_op jit(solution)/shard_map/reduce_scatter | solution.py:1431
  111.2 170.1 %collective-permute-start.12 = (bf16[256,1408]{1,0:T(8,128)(2,1)}, bf16[256,1408]{1,0:T(8,128)(2,1)}, u32[]{:S(2)}, u32[]{:S(2)}) collective-permute-start(bf16[256,1408]{1,0:T(8,128)(2,1)} %concatenate.84), channel_id=1, source_target_pairs={{0,1},{1,0},{2,3},{3,2},{4,5},{5,4},{6,7},{7,6},{8,9},{9,8},{10,11... | collective-permute-start | bytes 2162696 | tf_op jit(solution)/shard_map/ppermute | solution.py:1488
  377.6 72.5 %collective-permute-start.15 = (bf16[4,2624,128]{2,1,0:T(8,128)(2,1)}, bf16[4,2624,128]{2,1,0:T(8,128)(2,1)S(1)}, u32[]{:S(2)}, u32[]{:S(2)}) collective-permute-start(bf16[4,2624,128]{2,1,0:T(8,128)(2,1)} %slice_bitcast_fusion.1), channel_id=1, source_target_pairs={{0,4},{4,0},{8,12},{12,8},{16,20},{20,16},{24,28},{28,24},{1,5},{5... | collective-permute-start | bytes 8060936 | tf_op jit(solution)/shard_map/ppermute | solution.py:1423
  454.0 142.2 %reduce-scatter.5.cloned.1.call-start = ((), (), s32[]{:S(2)}) async-start(), calls=%async_computation.3 | async-start | bytes 1986560 | tf_op jit(solution)/shard_map/reduce_scatter | solution.py:1431
  456.0 54.0 %collective-permute-start.16 = (bf16[4,1552,128]{2,1,0:T(8,128)(2,1)S(1)}, bf16[4,1552,128]{2,1,0:T(8,128)(2,1)}, u32[]{:S(2)}, u32[]{:S(2)}) collective-permute-start(bf16[4,1552,128]{2,1,0:T(8,128)(2,1)S(1)} %slice_bitcast_fusion.2), channel_id=1, source_target_pairs={{0,4},{4,0},{8,12},{12,8},{16,20},{20,16},{24,28},{28,24},{1,5},{5... | collective-permute-start | bytes 4767752 | tf_op jit(solution)/shard_map/ppermute | solution.py:1423
  508.4 81.8 %collective-permute-start.17 = (bf16[4,2624,128]{2,1,0:T(8,128)(2,1)}, bf16[4,2624,128]{2,1,0:T(8,128)(2,1)}, u32[]{:S(2)}, u32[]{:S(2)}) collective-permute-start(bf16[4,2624,128]{2,1,0:T(8,128)(2,1)} %slice_bitcast_fusion), channel_id=1, source_target_pairs={{0,4},{4,0},{8,12},{12,8},{16,20},{20,16},{24,28},{28,24},{1,5},{5... | collective-permute-start | bytes 8060936 | tf_op jit(solution)/shard_map/ppermute | solution.py:1423
  565.0 27.3 %slice-start.2 = ((s8[5373952]{0:T(1024)(128)(4,1)}), s8[4194304]{0:T(1024)(128)(4,1)S(1)}, s32[]{:S(2)}) async-start(s8[5373952]{0:T(1024)(128)(4,1)} %bitcast.212), calls=%async_computation.9 | async-start | bytes 8388608
  565.6 26.7 %slice-start.3 = ((s8[5373952]{0:T(1024)(128)(4,1)}), s8[1179648]{0:T(1024)(128)(4,1)S(1)}, s32[]{:S(2)}) async-start(s8[5373952]{0:T(1024)(128)(4,1)} %bitcast.212), calls=%async_computation.10 | async-start | bytes 2359296
  (45 other events, 170.2 us)
Sparse Core Ops, SparseCore 0:
  84.8 36.3 all-gather.7
  123.3 35.9 all-gather.9
  160.9 33.8 all-gather.11
  454.2 52.6 reduce-scatter.2
  513.6 36.1 reduce-scatter.4

commit v3 on v2

--- a/solution.py
+++ b/solution.py
@@ -112,10 +112,24 @@
 
 
 def mixer_forward_kernel(
-    proj_ref, small_ref, taps_ref, heads_ref, gain_ref,
-    gated_ref, start_ref, inv_ref, pseudo_ref, mixed_ref,
-    halo, state,
+    layer, proj_ref, small_ref, taps_ref, heads_ref, gain_ref, *refs
 ):
+    if layer == 0:
+        up_source, in_source, *refs = refs
+        *outs, up_whole, near, far = refs[:8]
+        halo, state, *sems = refs[8:]
+    else:
+        up_source, *refs = refs
+        *outs, up_whole = refs[:6]
+        halo, state, *sems = refs[6:]
+    gated_ref, start_ref, inv_ref, pseudo_ref, mixed_ref = outs
+    ready = greet_wide(*place())
+    shard = Reshard(up_source.at[layer], up_lanes, up_whole, *sems[:5])
+    if layer == 0:
+        quarter = Quarter(in_source.at[1], in_lanes, near, far, *sems[5:])
+    ready()
+    shard.start_far(0)
+    shard.start_near()
     halo[...] = jnp.zeros_like(halo)
     state[...] = jnp.zeros_like(state)
     row = grid_of((CHUNK, CHUNK), 0)
@@ -178,30 +192,58 @@
         ready = [prepare(step * UNROLL + u) for u in range(UNROLL)]
         for u in range(UNROLL):
             advance(step * UNROLL + u, *ready[u])
+        @pl.when(step == 0)
+        def _():
+            shard.start_far(1)
+            if layer == 0:
+                quarter.start_near()
+
+        @pl.when(step == 1)
+        def _():
+            shard.forward(0)
+            if layer == 0:
+                quarter.start_quarter()
+
+        @pl.when(step == 2)
+        def _():
+            shard.forward(1)
+
         return carry
 
     lax.fori_loop(0, proj_ref.shape[0] // (CHUNK * UNROLL), body, 0)
-
-
-def mixer_forward(projected, small, taps, heads, gain):
+    shard.wait()
+    shard.finish()
+    if layer == 0:
+        quarter.wait_quarter()
+
+
+def mixer_forward(layer, projected, small, taps, heads, gain, sources):
     tokens = projected.shape[0]
     chunks = tokens // CHUNK
     vmem = pl.BlockSpec(memory_space=pltpu.VMEM)
+    spot = pl.BlockSpec(memory_space=pl.ANY)
+    wholes = (jax.ShapeDtypeStruct((1024, 1536), bf16),)
+    if layer == 0:
+        wholes = wholes * 2 + (jax.ShapeDtypeStruct((2, PART, 1536), bf16),)
     return pl.pallas_call(
-        mixer_forward_kernel,
+        partial(mixer_forward_kernel, layer),
         out_shape=(
             jax.ShapeDtypeStruct((tokens, 512), bf16),
             jax.ShapeDtypeStruct((chunks, 2, DK, DV), f32),
             jax.ShapeDtypeStruct((chunks, 2, CHUNK, CHUNK), f32),
             jax.ShapeDtypeStruct((chunks, 2, CHUNK, DV), f32),
             jax.ShapeDtypeStruct((tokens, 512), f32),
+        )
+        + wholes,
+        in_specs=[vmem] * 5 + [spot] * len(sources),
+        out_specs=(vmem,) * 5 + (spot,) * len(wholes),
+        scratch_shapes=[pltpu.VMEM((8, 1024), f32), pltpu.VMEM((2, DK, DV), f32)]
+        + Reshard.scratch() * len(sources),
+        compiler_params=pltpu.CompilerParams(
+            collective_id=8 + layer, has_side_effects=True, vmem_limit_bytes=LIMIT
         ),
-        in_specs=[vmem] * 5,
-        out_specs=(vmem,) * 5,
-        scratch_shapes=[pltpu.VMEM((8, 1024), f32), pltpu.VMEM((2, DK, DV), f32)],
-        compiler_params=pltpu.CompilerParams(vmem_limit_bytes=48 << 20),
         name="mixer_forward",
-    )(projected, small, taps, heads, gain)
+    )(projected, small, taps, heads, gain, *sources)
 
 
 def mixer_backward_kernel(
@@ -274,22 +316,22 @@
             d_end = dstate[h]
             kf = k.astype(f32)
             qf = q.astype(f32)
-            d_pseudo = mh(mixing, d_mixed, TN) + tail * mh(kf, d_end)
-            d_right = mh(inv, d_pseudo, TN)
+            d_pseudo = mb(mixing, d_mixed, TN) + tail * mm(k, d_end.astype(bf16))
+            d_right = mm3(inv, d_pseudo, TN)
             pair = jnp.concatenate([d_mixed, d_right], axis=0)
-            reads = mh(pair, jnp.concatenate([start, pseudo], axis=0), NT)
+            reads = mm3(pair, jnp.concatenate([start, pseudo], axis=0), NT)
             read_q = reads[:CHUNK, :DK]
             read_k = reads[CHUNK:, :DK]
-            read_u = mh(pseudo, d_end, NT)
+            read_u = mm3(pseudo, d_end, NT)
             d_mixing = jnp.where(row >= col, reads[:CHUNK, DK:], 0.0) * ratio
             d_system = jnp.where(row > col, -reads[CHUNK:, DK:], 0.0) * ratio
             raw = d_mixing * query_gram + d_system * key_gram
             x_pair = jnp.concatenate([d_mixing * beta_row, d_system * beta_row], axis=0)
-            by_row = mh(x_pair, kf)
-            by_col = mh(x_pair, jnp.concatenate([qf, kf], axis=0), TN)
+            by_row = mm(x_pair.astype(bf16), k)
+            by_col = mm(x_pair.astype(bf16), jnp.concatenate([q, k], axis=0), TN)
             d_q = growth * read_q + by_row[:CHUNK]
             d_k = by_row[CHUNK:] + by_col - growth * read_k + tail * read_u
-            dstate[h] = jnp.exp(last) * d_end + mh(
+            dstate[h] = jnp.exp(last) * d_end + mb(
                 jnp.concatenate([growth * qf, -growth * kf], axis=0), pair, TN
             )
             u_dot = jnp.sum(read_u * kf, axis=-1, keepdims=True)
@@ -321,7 +363,7 @@
             d_k_parts.append(k_norm * (d_k - kn * jnp.sum(d_k * kn, axis=-1, keepdims=True)))
             d_v_parts.append(d_right)
         upper_ones = jnp.where(row <= col, 1.0, 0.0).astype(f32)
-        d_log = mh(upper_ones, d_cumulative)
+        d_log = mm2(upper_ones.astype(bf16), d_cumulative)
         d_shifted = d_log * (-jnp.exp(heads_ref[0:1, :])) * jax.nn.sigmoid(shifted_logit)
         d_small = jnp.where(lane < 2, d_strength * strength * (1.0 - strength), d_shifted)
         dsmall_ref[rows, :] = jnp.where(lane < 4, d_small, 0.0).astype(bf16)
@@ -527,41 +569,148 @@
     return 2 * (y + dy - 2 * y * dy) + c + dc - 2 * c * dc
 
 
-def load_weight(own, sibling, far, whole, sems):
+def load_whole(src, whole, sem):
+    copy = pltpu.make_async_copy(src, whole, sem)
+    copy.start()
+    return copy.wait
+
+
+def load_down(src, whole, sem):
     y, c = place()
-    size = own.shape[0]
-    copies = []
-
-    def add(src, d, start, count):
-        rows = pl.ds(pl.multiple_of(relative(y, c, d) * size + start, count), count)
-        copies.append(pltpu.make_async_copy(src, whole.at[rows], sems.at[len(copies)]))
-
-    add(own, 0, 0, size)
-    add(sibling, 1, 0, size)
-    if len(far.shape) == 4:
-        part = far.shape[2]
-        for k in range(far.shape[0]):
+    rows, extra = src.shape[0], whole.shape[0] - src.shape[0]
+    whole[:extra, :] = jnp.zeros((extra, whole.shape[1]), bf16)
+    whole[rows:, :] = jnp.zeros((extra, whole.shape[1]), bf16)
+    spot = pl.ds(pl.multiple_of(extra * c, extra), rows)
+    copy = pltpu.make_async_copy(src, whole.at[spot], sem)
+    copy.start()
+    return copy.wait
+
+
+def flip(rank):
+    return rank + 1 - 2 * (rank % 2)
+
+
+def greet_wide(y, c):
+    barrier = pltpu.get_barrier_semaphore()
+    for d in range(1, 4):
+        pl.semaphore_signal(
+            barrier, inc=1, device_id={"grp": relative(y, c, d)}, device_id_type=MESH
+        )
+    pl.semaphore_signal(
+        barrier, inc=1, device_id={"rep": flip(lax.axis_index("rep"))}, device_id_type=MESH
+    )
+    return lambda: pl.semaphore_wait(barrier, 4)
+
+
+PART = 64
+
+
+def in_lanes(t):
+    return (
+        (256 * t, 256, 0),
+        (HK + 256 * t, 256, 256),
+        (2 * HK + 512 * t, 512, 512),
+        (CH + 512 * t, 512, 1024),
+    )
+
+
+def up_lanes(t):
+    first = 1408 * (t // 2) + 640 * (t % 2)
+    return ((first, 768, 0), (FF + first, 768, 768))
+
+
+class Reshard:
+    def __init__(self, source, lanes, whole, send, recv, passed, arrived, local):
+        self.source, self.lanes, self.whole = source, lanes, whole
+        self.send, self.recv, self.passed, self.arrived = send, recv, passed, arrived
+        self.local = local
+        self.y, self.c = place()
+        rank = lax.axis_index("rep")
+        self.x, self.other = rank % 2, flip(rank)
+        self.size = source.shape[0]
+
+    def at(self, index, offset, count):
+        return pl.ds(pl.multiple_of(index * self.size + offset, PART), count)
+
+    def pieces(self, d, q):
+        y, c = self.y, self.c
+        target = relative(y, c, d)
+        start = 0 if d < 2 else self.size // 2 * self.x + PART * q
+        count = self.size if d < 2 else PART
+        copies = []
+        for k, (lane, wide, to) in enumerate(self.lanes(target)):
+            src = self.source.at[
+                pl.ds(pl.multiple_of(start, PART), count) if d >= 2 else pl.ds(0, count),
+                pl.ds(pl.multiple_of(lane, 128), wide),
+            ]
+            dst = self.whole.at[self.at(2 * y + c, start, count), pl.ds(to, wide)]
+            if d == 0:
+                copies.append(pltpu.make_async_copy(src, dst, self.local.at[k]))
+            else:
+                copies.append(
+                    pltpu.make_async_remote_copy(
+                        src_ref=src, dst_ref=dst,
+                        send_sem=self.send.at[d, q, k], recv_sem=self.recv.at[d, q, k],
+                        device_id={"grp": target}, device_id_type=MESH,
+                    )
+                )
+        return copies
+
+    def onward(self, d, q):
+        source = relative(self.y, self.c, d)
+        rows = self.at(source, self.size // 2 * self.x + PART * q, PART)
+        return pltpu.make_async_remote_copy(
+            src_ref=self.whole.at[rows], dst_ref=self.whole.at[rows],
+            send_sem=self.passed.at[d - 2, q], recv_sem=self.arrived.at[d - 2, q],
+            device_id={"rep": self.other}, device_id_type=MESH,
+        )
+
+    def parts(self):
+        return range(self.size // 2 // PART)
+
+    def start_far(self, q):
+        for d in (2, 3):
+            for copy in self.pieces(d, q):
+                copy.start()
+
+    def start_near(self):
+        for copy in self.pieces(1, 0):
+            copy.start()
+
+    def start_own(self):
+        for copy in self.pieces(0, 0):
+            copy.start()
+
+    def forward(self, q):
+        for d in (2, 3):
+            for copy in self.pieces(d, q):
+                copy.wait_recv()
+            self.onward(d, q).start()
+
+    def wait_own(self):
+        for copy in self.pieces(0, 0):
+            copy.wait()
+
+    def wait(self):
+        for copy in self.pieces(1, 0):
+            copy.wait_recv()
+        for q in self.parts():
             for d in (2, 3):
-                add(far.at[k, d - 2], d, k * part, part)
-    else:
-        for d in (2, 3):
-            add(far.at[d - 2], d, 0, size)
-    for copy in copies:
-        copy.start()
-
-    def wait():
-        for copy in copies:
-            copy.wait()
-
-    return wait
-
-
-def load_down(src, whole, sem):
-    rows = src.shape[0]
-    copy = pltpu.make_async_copy(src, whole.at[pl.ds(0, rows)], sem)
-    copy.start()
-    whole[rows:, :] = jnp.zeros((whole.shape[0] - rows, whole.shape[1]), bf16)
-    return copy.wait
+                self.onward(d, q).wait_recv()
+
+    def finish(self):
+        for copy in self.pieces(1, 0):
+            copy.wait_send()
+        for q in self.parts():
+            for d in (2, 3):
+                for copy in self.pieces(d, q):
+                    copy.wait_send()
+                self.onward(d, q).wait_send()
+
+    @staticmethod
+    def scratch():
+        dma = pltpu.SemaphoreType.DMA
+        return [dma((4, 2, 4)), dma((4, 2, 4)), dma((2, 2)), dma((2, 2)), dma((4,))]
 
 
 def like(*shape, dtype=f32):
@@ -580,11 +729,203 @@
     return d_x, jnp.sum(d_out * unit, axis=0, keepdims=True)
 
 
-def project_kernel(
-    res_ref, gain_ref, ab_ref, own_ref, sibling_ref, far_ref,
-    normed_ref, proj_ref, small_ref, w_ref, loads, send, recv,
+class Quarter(Reshard):
+    def __init__(self, source, lanes, whole, far, *sems):
+        super().__init__(source, lanes, whole, *sems)
+        self.far = far
+        self.z = (lax.axis_index("rep") % 8) // 2
+
+    def quarters(self, d):
+        target = relative(self.y, self.c, d)
+        copies = []
+        for k, (lane, wide, to) in enumerate(self.lanes(target)):
+            copies.append(
+                pltpu.make_async_remote_copy(
+                    src_ref=self.source.at[
+                        pl.ds(pl.multiple_of(PART * self.z, PART), PART),
+                        pl.ds(pl.multiple_of(lane, 128), wide),
+                    ],
+                    dst_ref=self.far.at[d - 2, :, pl.ds(to, wide)],
+                    send_sem=self.send.at[d, 0, k], recv_sem=self.recv.at[d, 0, k],
+                    device_id={"grp": target}, device_id_type=MESH,
+                )
+            )
+        return copies
+
+    def start_quarter(self):
+        for d in (2, 3):
+            for copy in self.quarters(d):
+                copy.start()
+
+    def wait_quarter(self):
+        for copy in self.pieces(1, 0):
+            copy.wait_recv()
+            copy.wait_send()
+        for d in (2, 3):
+            for copy in self.quarters(d):
+                copy.wait_recv()
+                copy.wait_send()
+
+
+def load_shard(parts, whole, sems):
+    y, c = place()
+    copies = []
+
+    def add(src, dst):
+        copies.append(pltpu.make_async_copy(src, dst, sems.at[len(copies)]))
+
+    if len(parts) == 1:
+        add(parts[0], whole)
+    else:
+        raw, lanes, near, *far = parts
+        size = whole.shape[0] // 4
+
+        def block(index, count):
+            return pl.ds(pl.multiple_of(index * size, size), count * size)
+
+        own, sibling, across = block(2 * y + c, 1), block(2 * y + 1 - c, 1), block(2 - 2 * y, 2)
+        for lane, wide, to in lanes(2 * y + c):
+            src = raw.at[pl.ds(0, size), pl.ds(pl.multiple_of(lane, 128), wide)]
+            add(src, whole.at[own, pl.ds(to, wide)])
+        add(near.at[sibling], whole.at[sibling])
+        if not far:
+            add(near.at[across], whole.at[across])
+        else:
+            for z in range(4):
+                for d in (2, 3):
+                    at = relative(y, c, d) * size + PART * z
+                    spot = pl.ds(pl.multiple_of(at, PART), PART)
+                    add(far[0].at[z, d - 2], whole.at[spot])
+    for copy in copies:
+        copy.start()
+
+    def wait():
+        for copy in copies:
+            copy.wait()
+
+    return wait
+
+
+def in_parts(parts):
+    return parts if len(parts) == 1 else (parts[0].at[1], in_lanes) + tuple(parts[1:])
+
+
+GAIN_AT, TAPS_AT, AB_AT, OUT_GAIN_AT, PACK_ROWS = 0, 8, 72, 136, 144
+
+
+def start_kernel(
+    x_ref, pack_ref, win_ref,
+    normed_ref, proj_ref, small_ref, whole_ref,
+    gain0, gain1, gain2, gain3, taps0, taps1, ab0, ab1, out0, out1,
+    everyone, ab_rows, *scratch,
 ):
-    loaded = load_weight(own_ref, sibling_ref, far_ref, w_ref, loads)
+    size = x_ref.shape[0]
+    y, c = place()
+    me = 2 * y + c
+    ready = greet_wide(y, c)
+    shard = Reshard(win_ref.at[0], in_lanes, whole_ref, *scratch[:5])
+    psend, precv = scratch[5:7]
+    gather = Gather(normed_ref, *scratch[7:], size)
+    everyone[me] = pack_ref[...]
+    ready()
+
+    def share(d):
+        return pltpu.make_async_remote_copy(
+            src_ref=pack_ref, dst_ref=everyone.at[me],
+            send_sem=psend.at[d], recv_sem=precv.at[d],
+            device_id={"grp": relative(y, c, d)}, device_id_type=MESH,
+        )
+
+    for d in (2, 3, 1):
+        share(d).start()
+    for q in shard.parts():
+        shard.start_far(q)
+    shard.start_near()
+    shard.start_own()
+    for d in (1, 2, 3):
+        share(d).wait_recv()
+    for k, ref in enumerate((gain0, gain1, gain2, gain3)):
+        for s in range(4):
+            for b in range(2):
+                row = GAIN_AT + 2 * k + b
+                ref[0:1, 256 * s + 128 * b : 256 * s + 128 * b + 128] = everyone[s, row : row + 1, :]
+    for i in range(size // SUB):
+        rows = slice(i * SUB, (i + 1) * SUB)
+        normed = normalise(x_ref[rows, :].astype(f32), gain0[...])
+        normed_ref[gather.own(i), :] = normed.astype(bf16)
+        gather.start(i)
+    for l, (taps, ab, out) in enumerate(((taps0, ab0, out0), (taps1, ab1, out1))):
+        taps[...] = jnp.zeros_like(taps)
+        out[...] = jnp.zeros_like(out)
+        ab_rows[...] = jnp.zeros_like(ab_rows)
+        for j in range(4):
+            base = TAPS_AT + (4 * l + j) * 8
+            for b in range(8):
+                if b < 2:
+                    s, row = 0, base + 2 * me + b
+                elif b < 4:
+                    s, row = 1, base + 2 * me + b - 2
+                else:
+                    s, row = 2 + y, base + 4 * c + b - 4
+                taps[j : j + 1, 128 * b : 128 * b + 128] = everyone[s, pl.ds(row, 1), :]
+            column = 2 * me + j if j < 2 else H + 2 * me + j - 2
+            for s in range(4):
+                for b in range(2):
+                    row = AB_AT + (16 * l + column) * 2 + b
+                    ab_rows[j : j + 1, 256 * s + 128 * b : 256 * s + 128 * b + 128] = everyone[
+                        s, pl.ds(row, 1), :
+                    ]
+        ab[...] = ab_rows[...].T.astype(bf16)
+        for s in range(4):
+            out[0:1, 64 * s : 64 * s + 64] = everyone[
+                s, OUT_GAIN_AT : OUT_GAIN_AT + 1, 64 * l : 64 * l + 64
+            ]
+    for q in shard.parts():
+        shard.forward(q)
+    shard.wait()
+    shard.wait_own()
+    for rows in in_order(gather):
+        normed = normed_ref[rows, :]
+        proj_ref[rows, :] = mm(normed, whole_ref[...]).astype(bf16)
+        small_ref[rows, :] = mm(normed, ab0[...])
+    gather.finish()
+    shard.finish()
+    for d in (1, 2, 3):
+        share(d).wait_send()
+
+
+def start(x, pack, w_in):
+    size, width = x.shape
+    tokens = 4 * size
+    row = like(1, width)
+    dma = pltpu.SemaphoreType.DMA
+    return call(
+        start_kernel,
+        (
+            like(tokens, width, dtype=bf16),
+            like(tokens, 1536, dtype=bf16),
+            like(tokens, 128),
+            like(width, 1536, dtype=bf16),
+            row, row, row, row,
+            like(8, width), like(8, width),
+            like(width, 128, dtype=bf16), like(width, 128, dtype=bf16),
+            like(8, DV), like(8, DV),
+        ),
+        (x, pack),
+        [pltpu.VMEM((4, PACK_ROWS, 128), f32), pltpu.VMEM((128, width), f32)]
+        + Reshard.scratch()
+        + [dma((4,)), dma((4,))]
+        + gather_sems(size),
+        1,
+        "start",
+        (w_in,),
+    )
+
+
+def project_kernel(count, res_ref, gain_ref, ab_ref, *refs):
+    parts, refs = refs[:count], refs[count:]
+    normed_ref, proj_ref, small_ref, w_ref, loads, send, recv = refs
+    loaded = load_shard(in_parts(parts), w_ref, loads)
     size = res_ref.shape[0]
     y, c = place()
     ready = greet(y, c)
@@ -603,54 +944,40 @@
     gather.finish()
 
 
-def project(residual, gain, weight, ab):
+def project(residual, gain, ab, weight):
     size, width = residual.shape
     tokens = 4 * size
     return call(
-        project_kernel,
+        partial(project_kernel, len(weight)),
         (like(tokens, width, dtype=bf16), like(tokens, 1536, dtype=bf16), like(tokens, 128)),
         (residual, gain, ab),
-        [pltpu.VMEM((width, 1536), bf16), pltpu.SemaphoreType.DMA((10,))] + gather_sems(size),
-        1 if len(weight[2].shape) == 4 else 6,
+        [pltpu.VMEM((width, 1536), bf16), pltpu.SemaphoreType.DMA((13,))] + gather_sems(size),
+        6,
         "project",
         weight,
     )
 
 
 def swiglu(up):
-    lane = grid_of((SUB, 128), 1)
-    gate, value, tail = up[:, :640], up[:, 640:1280], up[:, 1280:]
-    turned = pltpu.roll(tail, 64, 1)
-    head = gate * jax.nn.sigmoid(gate) * value
-    last = jnp.where(lane < 64, tail * jax.nn.sigmoid(tail) * turned, 0.0)
-    return jnp.concatenate([head, last], axis=1)
+    gate, value = up[:, :768], up[:, 768:]
+    return gate * jax.nn.sigmoid(gate) * value
 
 
 def swiglu_back(up, d_hidden):
-    lane = grid_of((SUB, 128), 1)
-    gate, value, tail = up[:, :640], up[:, 640:1280], up[:, 1280:]
-    turned = pltpu.roll(tail, 64, 1)
-    d_head, d_tail = d_hidden[:, :640], d_hidden[:, 640:]
-    d_tail = d_tail + pltpu.roll(d_tail, 64, 1)
+    gate, value = up[:, :768], up[:, 768:]
     sig = jax.nn.sigmoid(gate)
-    d_gate = d_head * value * (sig * (1.0 + gate * (1.0 - sig)))
-    d_value = d_head * gate * sig
-    sig = jax.nn.sigmoid(tail)
-    side = jnp.where(
-        lane < 64,
-        turned * (sig * (1.0 + tail * (1.0 - sig))),
-        turned * jax.nn.sigmoid(turned),
-    )
-    return jnp.concatenate([d_gate, d_value, d_tail * side], axis=1)
+    d_gate = d_hidden * value * (sig * (1.0 + gate * (1.0 - sig)))
+    return jnp.concatenate([d_gate, d_hidden * gate * sig], axis=1)
 
 
 def ffn_forward_kernel(
-    gated_ref, wout_ref, res_ref, gain_ref, down_ref, own_ref, sibling_ref, far_ref,
+    layer, gated_ref, res_ref, gain_ref, raw_ref, down_ref, ffn_ref, whole_ref,
     mid_ref, normed_ref, up_ref, hidden_ref, out_ref,
-    wup_ref, wdown_ref, loads, *scratch,
+    wup_ref, wdown_ref, wout_ref, loads, shard_loads, *scratch,
 ):
-    loaded = load_weight(own_ref, sibling_ref, far_ref, wup_ref, loads)
-    loaded_down = load_down(down_ref, wdown_ref, loads.at[10])
+    loaded_out = load_whole(raw_ref.at[layer], wout_ref, loads.at[2])
+    loaded = load_shard((ffn_ref.at[layer], up_lanes, whole_ref), wup_ref, shard_loads)
+    loaded_down = load_down(down_ref.at[layer], wdown_ref, loads.at[1])
     size = res_ref.shape[0]
     count = size // SUB
     y, c = place()
@@ -658,6 +985,8 @@
     first = Scatter(*scratch[:7], size)
     second = Scatter(*scratch[7:14], size)
     gather = Gather(normed_ref, *scratch[14:], size)
+
+    loaded_out()
 
     def branch(rows):
         return mm(gated_ref[rows, :], wout_ref[...])
@@ -705,82 +1034,113 @@
     gather.finish()
 
 
-def ffn_forward(gated, w_out, residual, gain, w_down, w_up):
+def ffn_forward(layer, gated, residual, gain, w_out, w_down, w_up):
     size, width = residual.shape
     tokens = 4 * size
     return call(
-        ffn_forward_kernel,
+        partial(ffn_forward_kernel, layer),
         (
             like(size, width),
             like(tokens, width, dtype=bf16),
-            like(tokens, 1408, dtype=bf16),
+            like(tokens, 1536, dtype=bf16),
             like(tokens, 768, dtype=bf16),
             like(size, width),
         ),
-        (gated, w_out, residual, gain),
+        (gated, residual, gain),
         [
-            pltpu.VMEM((width, 1408), bf16),
+            pltpu.VMEM((width, 1536), bf16),
             pltpu.VMEM((768, width), bf16),
-            pltpu.SemaphoreType.DMA((11,)),
+            pltpu.VMEM((512, width), bf16),
+            pltpu.SemaphoreType.DMA((3,)),
+            pltpu.SemaphoreType.DMA((13,)),
         ]
         + Scatter.scratch(size, width)
         + Scatter.scratch(size, width)
         + gather_sems(size),
-        2,
+        (2, 12)[layer],
         "ffn_forward",
-        (w_down,) + tuple(w_up),
+        (w_out, w_down) + w_up,
     )
 
 
-def grad_place():
-    rank = lax.axis_index("rep") % 8
-    x = rank % 2
-    y, c = place()
-
-    def slot(r):
-        return r % 2 + x - 2 * (r % 2) * x
-
-    def target(d):
-        dy, dc = d // 2, d % 2
-        return 2 * (y + dy - 2 * y * dy) + c + dc - 2 * c * dc
-
-    return slot, target
-
-
-def store_columns(buf, value, row, base, slot):
+class Owners:
+    def __init__(self, keep, send):
+        self.keep, self.send = keep, send
+        self.x = lax.axis_index("rep") % 2
+
+    def put(self, r, store):
+        @pl.when(self.x == r % 2)
+        def _():
+            store(self.keep.at[r // 2])
+
+        @pl.when(self.x != r % 2)
+        def _():
+            store(self.send.at[r // 2])
+
+
+def store_columns(buf, value, at):
+    rows = pl.ds(at, value.shape[0])
     for r in range(8):
-        buf[slot(r), r // 2, base + row : base + row + value.shape[0], :] = value[
-            :, 128 * r : 128 * r + 128
-        ].astype(bf16)
-
-
-def store_rows(buf, value, d, base, slot):
+
+        def store(ref):
+            ref[rows, :] = value[:, 128 * r : 128 * r + 128].astype(bf16)
+
+        buf.put(r, store)
+
+
+def store_up(buf, staged, d, c):
+    own_half = (grid_of((32, 128), 1) >> 6) == c
+    for r in range(8):
+        rows = slice(32 * r, 32 * r + 32)
+
+        def tile(side, j):
+            lane = pl.multiple_of(768 * side + 128 * j, 128)
+            return staged[rows, pl.ds(lane, 128)]
+
+        tiles = [tile(j // 5, j % 5 + c) for j in range(10)]
+        turned = pltpu.roll(tile(1, 5 - 5 * c), 64, 1)
+        tiles.append(jnp.where(own_half, tile(0, 5 - 5 * c), turned))
+
+        def store(ref):
+            for j, value in enumerate(tiles):
+                at = UP_AT + (d * 11 + j) * 32
+                ref[at : at + 32, :] = value.astype(bf16)
+
+        buf.put(r, store)
+
+
+def store_rows(buf, value, d, base):
     blocks = value.shape[1] // 128
     for r in range(8):
-        for j in range(blocks):
-            at = base + (d * blocks + j) * 32
-            buf[slot(r), r // 2, at : at + 32, :] = value[
-                32 * r : 32 * r + 32, 128 * j : 128 * j + 128
-            ].astype(bf16)
-
-
-DOWN_AT, OUT_AT, UP_AT, FFN_ROWS = 0, 704, 1216, 2624
+
+        def store(ref):
+            for j in range(blocks):
+                at = base + (d * blocks + j) * 32
+                ref[at : at + 32, :] = value[
+                    32 * r : 32 * r + 32, 128 * j : 128 * j + 128
+                ].astype(bf16)
+
+        buf.put(r, store)
+
+
+UP_AT, DOWN_AT, OUT_AT, FFN_ROWS = 0, 1408, 2112, 2624
 SMALL_AT, IN_ROWS = 1536, 1552
 
 
 def ffn_backward_kernel(
-    dres_ref, up_ref, hidden_ref, normed_ref, mid_ref, gain_ref, gated_ref, wout_ref,
-    down_ref, own_ref, sibling_ref, far_ref,
-    dmid_ref, dgated_ref, ggain_ref, buf_ref,
-    wup_ref, wdown_ref, loads, ddown_ref, dup_ref, dbranch_ref, *scratch,
+    layer, dres_ref, up_ref, hidden_ref, normed_ref, mid_ref, gain_ref, gated_ref,
+    raw_ref, down_ref, ffn_ref, whole_ref,
+    dmid_ref, dgated_ref, ggain_ref, keep_ref, send_ref,
+    wup_ref, wdown_ref, wout_ref, loads, shard_loads, ddown_ref, dup_ref, dbranch_ref, staged, *scratch,
 ):
-    loaded = load_weight(own_ref, sibling_ref, far_ref, wup_ref, loads)
-    loaded_down = load_down(down_ref, wdown_ref, loads.at[10])
+    buf_ref = Owners(keep_ref, send_ref)
+    loaded_out = load_whole(raw_ref.at[layer], wout_ref, loads.at[2])
+    loaded = load_shard((ffn_ref.at[layer], up_lanes, whole_ref), wup_ref, shard_loads)
+    loaded_down = load_down(down_ref.at[layer], wdown_ref, loads.at[1])
     size = dres_ref.shape[0]
     count = size // SUB
     y, c = place()
     ready = greet(y, c)
-    slot, target = grad_place()
     first = Gather(ddown_ref, *scratch[:2], size)
     second = Gather(dbranch_ref, *scratch[2:4], size)
     scatter = Scatter(*scratch[4:], size)
@@ -808,9 +1168,8 @@
         scatter.give(0, i, feed(first.diagonal(i)))
         scatter.relay(i)
     for m in range(6):
-        wide = 128 if m < 5 else 64
         value = mm(hidden_ref[:, 128 * m : 128 * m + 128], ddown_ref[...], TN)
-        store_columns(buf_ref, value[:wide], 128 * m, DOWN_AT, slot)
+        store_columns(buf_ref, value, pl.multiple_of(DOWN_AT + 128 * m - 64 * c, 64))
     ggain_ref[...] = jnp.zeros_like(ggain_ref)
     for i in range(count):
         rows = slice(i * SUB, (i + 1) * SUB)
@@ -821,69 +1180,74 @@
         dbranch_ref[second.own(i), :] = d_mid.astype(bf16)
         second.start(i)
     for d in range(4):
-        lanes = pl.ds(pl.multiple_of(target(d) * 256, 256), 256)
-        value = mm(normed_ref[:, lanes], dup_ref[...], TN)
-        store_rows(buf_ref, value, d, UP_AT, slot)
+        lanes = pl.ds(pl.multiple_of(relative(y, c, d) * 256, 256), 256)
+        staged[...] = mm(normed_ref[:, lanes], dup_ref[...], TN)
+        store_up(buf_ref, staged, d, c)
+    loaded_out()
     for rows in in_order(second):
         dgated_ref[rows, :] = mm(dbranch_ref[rows, :], wout_ref[...], NT).astype(bf16)
     for m in range(4):
         value = mm(gated_ref[:, 128 * m : 128 * m + 128], dbranch_ref[...], TN)
-        store_columns(buf_ref, value, 128 * m, OUT_AT, slot)
+        store_columns(buf_ref, value, OUT_AT + 128 * m)
     first.finish()
     second.finish()
     scatter.finish()
 
 
-def ffn_backward(d_res, up, hidden, normed, mid, gain, gated, w_out, w_down, w_up):
+def ffn_backward(layer, d_res, up, hidden, normed, mid, gain, gated, w_out, w_down, w_up):
     size, width = d_res.shape
     tokens = 4 * size
     return call(
-        ffn_backward_kernel,
+        partial(ffn_backward_kernel, layer),
         (
             like(size, width),
             like(tokens, 512, dtype=bf16),
             like(8, width),
-            like(2, 4, FFN_ROWS, 128, dtype=bf16),
+            like(4, FFN_ROWS, 128, dtype=bf16),
+            like(4, FFN_ROWS, 128, dtype=bf16),
         ),
-        (d_res, up, hidden, normed, mid, gain, gated, w_out),
+        (d_res, up, hidden, normed, mid, gain, gated),
         [
-            pltpu.VMEM((width, 1408), bf16),
+            pltpu.VMEM((width, 1536), bf16),
             pltpu.VMEM((768, width), bf16),
-            pltpu.SemaphoreType.DMA((11,)),
+            pltpu.VMEM((512, width), bf16),
+            pltpu.SemaphoreType.DMA((3,)),
+            pltpu.SemaphoreType.DMA((13,)),
             pltpu.VMEM((tokens, width), bf16),
-            pltpu.VMEM((tokens, 1408), bf16),
+            pltpu.VMEM((tokens, 1536), bf16),
             pltpu.VMEM((tokens, width), bf16),
+            pltpu.VMEM((256, 1536), f32),
         ]
         + gather_sems(size)
         + gather_sems(size)
         + Scatter.scratch(size, width),
-        3,
+        (3, 13)[layer],
         "ffn_backward",
-        (w_down,) + tuple(w_up),
+        (w_out, w_down) + w_up,
     )
 
 
 def project_backward_kernel(
-    dproj_ref, dsmall_ref, ab_ref, normed_ref, res_ref, gain_ref, dmid_ref,
-    gtwo_ref, gtaps_ref, gheads_ref, own_ref, sibling_ref, far_ref,
-    dres_ref, buf_ref,
-    w_ref, loads, table, *scratch,
+    parts, dproj_ref, dsmall_ref, ab_ref, normed_ref, res_ref, gain_ref, dmid_ref,
+    gtwo_ref, gtaps_ref, gheads_ref, *refs
 ):
-    loaded = load_weight(own_ref, sibling_ref, far_ref, w_ref, loads)
+    parts, refs = refs[:parts], refs[parts:]
+    dres_ref, keep_ref, send_ref, w_ref, loads, table, *scratch = refs
+    buf_ref = Owners(keep_ref, send_ref)
+    loaded = load_shard(in_parts(parts), w_ref, loads)
     size = res_ref.shape[0]
     count = size // SUB
     y, c = place()
     ready = greet(y, c)
-    slot, target = grad_place()
     scatter = Scatter(*scratch, size)
 
     def back(rows):
         return mm(dproj_ref[rows, :], w_ref[...], NT) + mm(dsmall_ref[rows, :], ab_ref[...], NT)
 
     def weight_grad(d):
-        lanes = pl.ds(pl.multiple_of(target(d) * 256, 256), 256)
+        lanes = pl.ds(pl.multiple_of(relative(y, c, d) * 256, 256), 256)
         value = mm(normed_ref[:, lanes], dproj_ref[...], TN)
-        store_rows(buf_ref, value, d, 0, slot)
+        store_rows(buf_ref, value, d, 0)
 
     loaded()
     for part in range(2):
@@ -919,157 +1283,141 @@
     for k in range(8):
         table[64 + k : 65 + k, :] = gain_sum[:, 128 * k : 128 * k + 128]
     for r in range(8):
-        buf_ref[slot(r), r // 2, SMALL_AT:IN_ROWS, :] = table[16 * r : 16 * r + 16, :].astype(bf16)
+
+        def store(ref):
+            ref[SMALL_AT:IN_ROWS, :] = table[16 * r : 16 * r + 16, :].astype(bf16)
+
+        buf_ref.put(r, store)
     scatter.finish()
 
 
 def project_backward(d_proj, d_small, weight, ab, normed, residual, gain, d_mid, g_two, g_taps, g_heads):
     size, width = residual.shape
     return call(
-        project_backward_kernel,
-        (like(size, width), like(2, 4, IN_ROWS, 128, dtype=bf16)),
+        partial(project_backward_kernel, len(weight)),
+        (like(size, width),) + (like(4, IN_ROWS, 128, dtype=bf16),) * 2,
         (d_proj, d_small, ab, normed, residual, gain, d_mid, g_two, g_taps, g_heads),
         [
             pltpu.VMEM((width, 1536), bf16),
-            pltpu.SemaphoreType.DMA((10,)),
+            pltpu.SemaphoreType.DMA((13,)),
             pltpu.VMEM((128, 128), f32),
         ]
         + Scatter.scratch(size, width),
-        4 if len(weight[2].shape) == 4 else 7,
+        4 if len(weight) == 1 else 7,
         "project_backward",
         weight,
     )
 
 
-def collect(final_ref, pieces, sems):
-    copy = pltpu.make_async_copy(final_ref, pieces, sems.at[0])
-    copy.start()
-    copy.wait()
-
-
-def offset_of(s):
+def assemble_kernel(
+    f1, f2, f3, f4, down_ref, out_ref, up_ref, in_ref, table_ref,
+    p1, p2, p3, p4, down, out, up, whole, loads, stores,
+):
     y, c = place()
+    copies = [
+        pltpu.make_async_copy(src, dst, loads.at[k])
+        for k, (src, dst) in enumerate(((f1, p1), (f2, p2), (f3, p3), (f4, p4)))
+    ]
+    for copy in copies:
+        copy.start()
+    left = grid_of((32, 128), 1) < 64
+
+    def ffn(layer, pieces):
+        def up_rows(r, carry):
+            rows = pl.ds(pl.multiple_of(32 * r, 32), 32)
+            for m in range(2):
+                tiles = []
+                for s in (2 * m, 2 * m + 1):
+                    at = UP_AT + offset_of(y, c, s) * 352
+                    tiles.append(
+                        [
+                            pieces[r, pl.ds(pl.multiple_of(at + 32 * j, 32), 32), :].astype(f32)
+                            for j in range(11)
+                        ]
+                    )
+                even, odd = tiles
+                middle = (
+                    jnp.where(left, even[10], odd[10]),
+                    pltpu.roll(jnp.where(left, odd[10], even[10]), 64, 1),
+                )
+                for side in range(2):
+                    part = slice(5 * side, 5 * side + 5)
+                    base = FF * side + 1408 * m
+                    for j, tile in enumerate(even[part] + [middle[side]] + odd[part]):
+                        up[layer, rows, base + 128 * j : base + 128 * j + 128] = tile
+            return carry
+
+        lax.fori_loop(0, 8, up_rows, 0)
+        done = [pltpu.make_async_copy(up.at[layer], up_ref.at[layer], stores.at[layer, 0])]
+        done[0].start()
+        for r in range(8):
+            lanes = slice(128 * r, 128 * r + 128)
+            down[layer, :, lanes] = pieces[r, DOWN_AT:OUT_AT, :].astype(f32)
+            out[layer, :, lanes] = pieces[r, OUT_AT:FFN_ROWS, :].astype(f32)
+        done.append(pltpu.make_async_copy(down.at[layer], down_ref.at[layer], stores.at[layer, 1]))
+        done.append(pltpu.make_async_copy(out.at[layer], out_ref.at[layer], stores.at[layer, 2]))
+        done[1].start()
+        done[2].start()
+        return done
+
+    def projection(layer, pieces):
+        def in_rows(r, carry):
+            rows = pl.ds(pl.multiple_of(32 * r, 32), 32)
+            for s in range(4):
+                at = offset_of(y, c, s) * 384
+                for lane, wide, to in in_lanes(s):
+                    for k in range(wide // 128):
+                        j = to // 128 + k
+                        tile = pieces[r, pl.ds(pl.multiple_of(at + 32 * j, 32), 32), :]
+                        column = lane + 128 * k
+                        whole[layer, rows, column : column + 128] = tile.astype(f32)
+            return carry
+
+        lax.fori_loop(0, 8, in_rows, 0)
+        done = pltpu.make_async_copy(whole.at[layer], in_ref.at[layer], stores.at[layer, 3])
+        done.start()
+        for s in range(4):
+            at = pl.ds(pl.multiple_of(SMALL_AT + 16 * offset_of(y, c, s), 16), 16)
+            for r in range(8):
+                table_ref[s, layer, 16 * r : 16 * r + 16, :] = pieces[r, at, :].astype(f32)
+        return [done]
+
+    waiting = []
+    copies[0].wait()
+    waiting += ffn(1, p1)
+    copies[1].wait()
+    waiting += projection(1, p2)
+    copies[2].wait()
+    waiting += ffn(0, p3)
+    copies[3].wait()
+    waiting += projection(0, p4)
+    for store in waiting:
+        store.wait()
+
+
+def offset_of(y, c, s):
     sy, sc = s // 2, s % 2
     return 2 * (y + sy - 2 * y * sy) + c + sc - 2 * c * sc
 
 
-def assemble_ffn_kernel(layer, earlier, final_ref, *refs):
-    down_ref, out_ref, up_ref, pieces, down, out, up, sems = refs[earlier:]
-    collect(final_ref, pieces, sems)
-    stores = [
-        pltpu.make_async_copy(down, down_ref.at[layer], sems.at[8]),
-        pltpu.make_async_copy(out, out_ref.at[layer], sems.at[9]),
-        pltpu.make_async_copy(up, up_ref.at[layer], sems.at[10]),
-    ]
-    for r in range(8):
-        lanes = slice(128 * r, 128 * r + 128)
-        down[:, lanes] = pieces[r, DOWN_AT:OUT_AT, :].astype(f32)
-    stores[0].start()
-    for r in range(8):
-        lanes = slice(128 * r, 128 * r + 128)
-        out[:, lanes] = pieces[r, OUT_AT:UP_AT, :].astype(f32)
-    stores[1].start()
-    left = grid_of((32, 128), 1) < 64
-
-    def turn(tile):
-        return pltpu.roll(tile, 64, 1)
-
-    def body(r, carry):
-        rows = pl.ds(pl.multiple_of(32 * r, 32), 32)
-        for m in range(2):
-            tiles = []
-            for s in (2 * m, 2 * m + 1):
-                at = UP_AT + offset_of(s) * 352
-                tiles.append(
-                    [
-                        pieces[r, pl.ds(pl.multiple_of(at + 32 * j, 32), 32), :].astype(f32)
-                        for j in range(11)
-                    ]
-                )
-            for side in range(2):
-                even = tiles[0][5 * side : 5 * side + 5]
-                odd = [turn(tile) for tile in tiles[1][5 * side : 5 * side + 5]]
-                even_tail = tiles[0][10] if side == 0 else turn(tiles[0][10])
-                odd_tail = turn(tiles[1][10]) if side == 0 else tiles[1][10]
-                row = even + [jnp.where(left, even_tail, odd[0])]
-                row += [jnp.where(left, odd[j - 1], odd[j]) for j in range(1, 5)]
-                row += [jnp.where(left, odd[4], odd_tail)]
-                base = FF * side + 1408 * m
-                for j, tile in enumerate(row):
-                    up[rows, base + 128 * j : base + 128 * j + 128] = tile
-        return carry
-
-    lax.fori_loop(0, 8, body, 0)
-    stores[2].start()
-    for store in stores:
-        store.wait()
-
-
-def assemble_in_kernel(layer, earlier, final_ref, *refs):
-    in_ref, table_ref, pieces, whole, sems = refs[earlier:]
-    collect(final_ref, pieces, sems)
-    store = pltpu.make_async_copy(whole, in_ref.at[layer], sems.at[8])
-
-    def body(r, carry):
-        rows = pl.ds(pl.multiple_of(32 * r, 32), 32)
-        for s in range(4):
-            at = offset_of(s) * 384
-            for j in range(12):
-                if j < 2:
-                    column = 256 * s + 128 * j
-                elif j < 4:
-                    column = HK + 256 * s + 128 * (j - 2)
-                elif j < 8:
-                    column = 2 * HK + 512 * s + 128 * (j - 4)
-                else:
-                    column = CH + 512 * s + 128 * (j - 8)
-                tile = pieces[r, pl.ds(pl.multiple_of(at + 32 * j, 32), 32), :]
-                whole[rows, column : column + 128] = tile.astype(f32)
-        return carry
-
-    lax.fori_loop(0, 8, body, 0)
-    store.start()
-    for r in range(8):
-        table_ref[16 * r : 16 * r + 16, :] = pieces[r, SMALL_AT:IN_ROWS, :].astype(f32)
-    store.wait()
-
-
-def assemble(kernel, layer, final, earlier, shapes, table, scratch, name):
+def assemble(finals):
     spot = pl.BlockSpec(memory_space=pl.ANY)
-    out_shape = tuple(like(LAYERS, *shape) for shape in shapes)
-    out_specs = (spot,) * len(shapes)
-    if table:
-        out_shape += (like(128, 128),)
-        out_specs += (pl.BlockSpec(memory_space=pltpu.VMEM),)
+    shapes = [(LAYERS, 704, 1024), (LAYERS, 512, 1024), (LAYERS, 256, 2 * FF), (LAYERS, 256, CH + HV)]
     return pl.pallas_call(
-        partial(kernel, layer, len(earlier)),
-        out_shape=out_shape,
-        in_specs=[spot] * (1 + len(earlier)),
-        out_specs=out_specs,
-        scratch_shapes=[pltpu.VMEM(final.shape, bf16)]
-        + [pltpu.VMEM(shape, f32) for shape in scratch]
-        + [pltpu.SemaphoreType.DMA((11,))],
-        input_output_aliases={1 + k: k for k in range(len(earlier))},
+        assemble_kernel,
+        out_shape=tuple(like(*shape) for shape in shapes) + (like(4, LAYERS, 128, 128),),
+        in_specs=[spot] * 4,
+        out_specs=(spot,) * 4 + (pl.BlockSpec(memory_space=pltpu.VMEM),),
+        scratch_shapes=[pltpu.VMEM(final.shape, bf16) for final in finals]
+        + [pltpu.VMEM(shape, f32) for shape in shapes]
+        + [pltpu.SemaphoreType.DMA((4,)), pltpu.SemaphoreType.DMA((2, 4))],
         compiler_params=pltpu.CompilerParams(vmem_limit_bytes=LIMIT),
-        name=name,
-    )(final, *earlier)
-
-
-def assemble_ffn(layer, final, earlier):
-    shapes = [(704, 1024), (512, 1024), (256, 2 * FF)]
-    return assemble(
-        assemble_ffn_kernel, layer, final, earlier, shapes, False, shapes, "assemble_ffn"
-    )
-
-
-def assemble_in(layer, final, earlier):
-    shapes = [(256, CH + HV)]
-    return assemble(
-        assemble_in_kernel, layer, final, earlier, shapes, True, shapes, "assemble_in"
-    )
+        name="assemble",
+    )(*finals)
 
 
 FFN_MOVE, IN_MOVE = (UP_AT, 352), (0, 384)
+GATHERED_ROWS = SMALL_AT + 4 * 16
 
 
 def add_into(dst, left, right):
@@ -1077,140 +1425,140 @@
 
 
 class Group:
-    def __init__(self, number, piece, moved, final, move, sems):
+    def __init__(self, number, piece, moved, final, move, sems, x_first=False):
         self.number, self.piece, self.moved, self.final = number, piece, moved, final
         self.at, self.part = move
         self.send, self.recv, self.local = sems
+        self.x_first = x_first
         rank = lax.axis_index("rep")
         self.rank, self.x, self.z = rank, rank % 2, (rank % 8) // 2
         self.y, self.c = place()
-
-    def swap(self, d):
-        dy, dc = d // 2, d % 2
-        target = 2 * (self.y + dy - 2 * self.y * dy) + self.c + dc - 2 * self.c * dc
+        self.extra = moved.shape[0] > piece.shape[0]
+
+    def swaps(self, d):
+        target = relative(self.y, self.c, d)
         rows = pl.ds(self.at + d * self.part, self.part)
-        return pltpu.make_async_remote_copy(
-            src_ref=self.piece.at[rows], dst_ref=self.moved.at[rows],
-            send_sem=self.send.at[self.number, d], recv_sem=self.recv.at[self.number, d],
-            device_id={"grp": target}, device_id_type=MESH,
-        )
+        spans = [(rows, rows, d)]
+        if self.extra:
+            spans.append((pl.ds(SMALL_AT, 16), pl.ds(SMALL_AT + 16 * d, 16), 20 + d))
+        return [
+            pltpu.make_async_remote_copy(
+                src_ref=self.piece.at[src], dst_ref=self.moved.at[dst],
+                send_sem=self.send.at[self.number, k], recv_sem=self.recv.at[self.number, k],
+                device_id={"grp": target}, device_id_type=MESH,
+            )
+            for src, dst, k in spans
+        ]
 
     def start_swap(self):
         for d in range(1, 4):
-            self.swap(d).start()
+            for copy in self.swaps(d):
+                copy.start()
         first = self.at + self.part
         self.moved[0:first, :] = self.piece[0:first, :]
-        rest = self.at + 4 * self.part
-        if rest < self.piece.shape[0]:
-            self.moved[rest:, :] = self.piece[rest:, :]
+        rest, last = self.at + 4 * self.part, self.piece.shape[0]
+        if rest < last:
+            self.moved[rest:last, :] = self.piece[rest:last, :]
 
     def wait_swap(self):
         for d in range(1, 4):
-            self.swap(d).wait_recv()
-
-    def move(self, step, source_z, kind):
-        owner = 2 * source_z + self.x
-        src = self.moved if step == 0 else self.final.at[owner]
-        side = 4 * kind if kind < 2 else 8
-        slot = side + (abs(step) if kind < 2 else step + 3)
-        target = (self.rank + 2, self.rank - 2, self.rank + 1 - 2 * self.x)[kind]
+            for copy in self.swaps(d):
+                copy.wait_recv()
+
+    def owner(self, source_z, which):
+        return 2 * source_z + (self.x if which == 0 else 1 - self.x)
+
+    def move(self, step, source_z, kind, which=0):
+        owner = self.owner(source_z, which)
+        src = self.moved if step == 0 and which == 0 else self.final.at[owner]
+        number = self.number if which == 0 else 4
+        slot = 4 + 4 * kind + step
         return pltpu.make_async_remote_copy(
             src_ref=src, dst_ref=self.final.at[owner],
-            send_sem=self.send.at[self.number, 4 + slot],
-            recv_sem=self.recv.at[self.number, 4 + (slot if kind < 2 else 8)],
-            device_id={"rep": target}, device_id_type=MESH,
+            send_sem=self.send.at[number, slot], recv_sem=self.recv.at[number, slot],
+            device_id={"rep": self.rank + 2 - 4 * kind}, device_id_type=MESH,
         )
 
     def x_move(self, step, source_z):
-        owner = 2 * source_z + self.x
+        owner = self.owner(source_z, 0)
         src = self.moved if step == 0 else self.final.at[owner]
         return pltpu.make_async_remote_copy(
             src_ref=src, dst_ref=self.final.at[owner],
             send_sem=self.send.at[self.number, 12 + step + 3],
             recv_sem=self.recv.at[self.number, 12 + source_z],
-            device_id={"rep": self.rank + 1 - 2 * self.x}, device_id_type=MESH,
+            device_id={"rep": flip(self.rank)}, device_id_type=MESH,
         )
 
     def own_copy(self):
         return pltpu.make_async_copy(
-            self.moved, self.final.at[2 * self.z + self.x], self.local.at[self.number]
-        )
-
-    def begin(self):
-        self.x_move(0, self.z).start()
-
+            self.moved, self.final.at[self.owner(self.z, 0)], self.local.at[self.number]
+        )
+
+    def both_ways(self, which, act):
         @pl.when(self.z < 3)
         def _():
-            self.move(0, self.z, 0).start()
+            act(self.move(0, self.z, 0, which))
 
         @pl.when(self.z > 0)
         def _():
-            self.move(0, self.z, 1).start()
-
+            act(self.move(0, self.z, 1, which))
+
+    def begin(self):
+        self.both_ways(0, lambda copy: copy.start())
+        self.x_move(0, self.z).start()
         self.own_copy().start()
 
-    def forward(self, k, act):
+    def begin_other(self):
+        self.x_move(0, self.z).wait_recv()
+        self.both_ways(1, lambda copy: copy.start())
+
+    def passes(self, k, which, arrive, onward):
         z = self.z
 
         @pl.when(z >= k)
         def _():
-            source = z - k
-            act(self, k, source, 0)
+            arrive(k, z - k, 0)
 
             @pl.when(z < 3)
             def _():
-                act(self, k, source, 2)
+                onward(self.move(k, z - k, 0, which))
 
         @pl.when(z + k <= 3)
         def _():
-            source = z + k
-            act(self, -k, source, 1)
+            arrive(-k, z + k, 1)
 
             @pl.when(z > 0)
             def _():
-                act(self, -k, source, 3)
+                onward(self.move(k, z + k, 1, which))
 
     def relay(self, k):
-        def act(self, step, source, what):
-            if what == 0:
-                self.move(step - 1, source, 0).wait_recv()
-                self.x_move(step, source).start()
-            elif what == 1:
-                self.move(step + 1, source, 1).wait_recv()
-                self.x_move(step, source).start()
-            elif what == 2:
-                self.move(step, source, 0).start()
-            else:
-                self.move(step, source, 1).start()
-
-        self.forward(k, act)
+        for which in range(2 if self.x_first else 1):
+
+            def arrive(step, source, kind):
+                self.move(abs(step) - 1, source, kind, which).wait_recv()
+                if not self.x_first:
+                    self.x_move(step, source).start()
+
+            self.passes(k, which, arrive, lambda copy: copy.start())
 
     def finish(self):
-        def act(self, step, source, what):
-            if what < 2:
-                self.x_move(step, source).wait_send()
-            elif what == 2:
-                self.move(step, source, 0).wait_send()
-            else:
-                self.move(step, source, 1).wait_send()
-
-        for k in range(1, 4):
-            self.forward(k, act)
+        for which in range(2 if self.x_first else 1):
+
+            def arrive(step, source, kind):
+                if not self.x_first:
+                    self.x_move(step, source).wait_send()
+
+            for k in range(1, 4):
+                self.passes(k, which, arrive, lambda copy: copy.wait_send())
+            self.both_ways(which, lambda copy: copy.wait_send())
         self.x_move(0, self.z).wait_send()
-
-        @pl.when(self.z < 3)
-        def _():
-            self.move(0, self.z, 0).wait_send()
-
-        @pl.when(self.z > 0)
-        def _():
-            self.move(0, self.z, 1).wait_send()
-
-        for source in range(4):
-            self.x_move(0, source).wait_recv()
+        if not self.x_first:
+            for source in range(4):
+                self.x_move(0, source).wait_recv()
         self.own_copy().wait()
         for d in range(1, 4):
-            self.swap(d).wait_send()
+            for copy in self.swaps(d):
+                copy.wait_send()
 
 
 class Line:
@@ -1228,32 +1576,34 @@
             device_id={"rep": self.rank + 2 - 4 * toward}, device_id_type=MESH,
         )
 
-    def edges(self):
+    def edge(self, step, act):
         @pl.when(self.z == 0)
         def _():
-            for o in (3, 2, 1):
-                self.go(o, 0).start()
+            act(self.go(3 - step, 0))
 
         @pl.when(self.z == 3)
         def _():
-            for o in (0, 1, 2):
-                self.go(o, 1).start()
-
-    def inner(self):
-        z = self.z
-        for o in (3, 2):
-
-            @pl.when((z > 0) & (z < o))
-            def _():
-                self.go(o, 0).wait_recv()
-                add_into(self.values.at[o], self.values.at[o], self.right.at[o])
-                self.go(o, 0).start()
-
-            @pl.when((z < 3) & (z > 3 - o))
-            def _():
-                self.go(3 - o, 1).wait_recv()
-                add_into(self.values.at[3 - o], self.values.at[3 - o], self.left.at[3 - o])
-                self.go(3 - o, 1).start()
+            act(self.go(step, 1))
+
+    def start_edge(self, step):
+        if step > 0:
+            self.edge(step - 1, lambda copy: copy.wait_send())
+        self.edge(step, lambda copy: copy.start())
+
+    def inner(self, step):
+        z, o = self.z, 3 - step
+
+        @pl.when((z > 0) & (z < o))
+        def _():
+            self.go(o, 0).wait_recv()
+            add_into(self.values.at[o], self.values.at[o], self.right.at[o])
+            self.go(o, 0).start()
+
+        @pl.when((z < 3) & (z > step))
+        def _():
+            self.go(step, 1).wait_recv()
+            add_into(self.values.at[step], self.values.at[step], self.left.at[step])
+            self.go(step, 1).start()
 
     def total(self, out):
         z = self.z
@@ -1271,19 +1621,20 @@
                 out[...] = value.astype(bf16)
 
     def finish(self):
+        self.edge(2, lambda copy: copy.wait_send())
         for o in range(4):
 
-            @pl.when(self.z < o)
+            @pl.when((self.z > 0) & (self.z < o))
             def _():
                 self.go(o, 0).wait_send()
 
-            @pl.when(self.z > o)
+            @pl.when((self.z < 3) & (self.z > o))
             def _():
                 self.go(o, 1).wait_send()
 
 
 def finish_kernel(
-    p1, p2, s3, b4, f1, f2, f3, f4,
+    p1, p2, s3, k4, b4, f1, f2, f3, f4,
     q1, q2, q3, q4, e1, e2, e3, e4, v3, r3, l3, v4, x4, r4, l4,
     send, recv, local, send3, recv3, send4, recv4, send5, recv5, loads,
 ):
@@ -1294,7 +1645,7 @@
         pltpu.make_async_copy(p1, q1, loads.at[0]),
         pltpu.make_async_copy(p2, q2, loads.at[1]),
         pltpu.make_async_copy(s3, v3, loads.at[2]),
-        pltpu.make_async_copy(b4.at[0], v4, loads.at[3]),
+        pltpu.make_async_copy(k4, v4, loads.at[3]),
     ]
     for load in loaded:
         load.start()
@@ -1325,7 +1676,7 @@
 
     def halves(o):
         return pltpu.make_async_remote_copy(
-            src_ref=b4.at[1, o], dst_ref=x4.at[o], send_sem=send5.at[o], recv_sem=recv5.at[o],
+            src_ref=b4.at[o], dst_ref=x4.at[o], send_sem=send5.at[o], recv_sem=recv5.at[o],
             device_id={"rep": rank + 1 - 2 * x}, device_id_type=MESH,
         )
 
@@ -1333,48 +1684,55 @@
         halves(o).start()
     sems = (send, recv, local)
     g1 = Group(0, q1, e1, f1, FFN_MOVE, sems)
-    g2 = Group(1, q2, e2, f2, IN_MOVE, sems)
+    g2 = Group(1, q2, e2, f2, IN_MOVE, sems, x_first=True)
     g3 = Group(2, q3, e3, f3, FFN_MOVE, sems)
     g4 = Group(3, q4, e4, f4, IN_MOVE, sems)
     line3 = Line(v3, r3, l3, send3, recv3)
     line4 = Line(v4, r4, l4, send4, recv4)
     loaded[0].wait()
     g1.start_swap()
+    loaded[2].wait()
+    line3.start_edge(0)
     loaded[1].wait()
     g2.start_swap()
-    loaded[2].wait()
-    line3.edges()
     g1.wait_swap()
     g1.begin()
+    line3.inner(0)
+    line3.start_edge(1)
     g2.wait_swap()
     g2.begin()
-    line3.inner()
     loaded[3].wait()
     for o in (3, 0, 2, 1):
         halves(o).wait_recv()
         add_into(v4.at[o], v4.at[o], x4.at[o])
-    line4.edges()
+    line4.start_edge(0)
+    line3.inner(1)
+    line3.start_edge(2)
+    g1.relay(1)
+    line4.inner(0)
+    line4.start_edge(1)
     line3.total(q3)
     g3.start_swap()
-    g1.relay(1)
+    line4.inner(1)
+    line4.start_edge(2)
+    g1.relay(2)
     g3.wait_swap()
     g3.begin()
-    line4.inner()
-    g2.relay(1)
     line4.total(q4)
     g4.start_swap()
-    g1.relay(2)
+    g2.begin_other()
+    g1.relay(3)
     g4.wait_swap()
     g4.begin()
+    g2.relay(1)
+    g3.relay(1)
+    g4.relay(1)
     g2.relay(2)
-    g3.relay(1)
-    g1.relay(3)
-    g4.relay(1)
-    g2.relay(3)
     g3.relay(2)
     g4.relay(2)
     g3.relay(3)
     g4.relay(3)
+    g2.relay(3)
     for group in (g1, g2, g3, g4):
         group.finish()
     line3.finish()
@@ -1383,22 +1741,23 @@
         halves(o).wait_send()
 
 
-def finish_reduction(p1, p2, s3, b4):
+def finish_reduction(p1, p2, s3, k4, b4):
     spot = pl.BlockSpec(memory_space=pl.ANY)
     big, small = p1.shape, p2.shape
+    wide = (GATHERED_ROWS, 128)
     dma = pltpu.SemaphoreType.DMA
     return pl.pallas_call(
         finish_kernel,
-        out_shape=tuple(like(8, *shape, dtype=bf16) for shape in (big, small, big, small)),
-        in_specs=[spot] * 4,
+        out_shape=tuple(like(8, *shape, dtype=bf16) for shape in (big, wide, big, wide)),
+        in_specs=[spot] * 5,
         out_specs=(spot,) * 4,
         scratch_shapes=[
             pltpu.VMEM(shape, bf16)
-            for shape in [big, small] * 4
+            for shape in [big, small] * 2 + [big, wide] * 2
             + [(4,) + big] * 3
             + [(4,) + small] * 4
         ]
-        + [dma((4, 20)), dma((4, 20)), dma((4,))]
+        + [dma((5, 24)), dma((5, 24)), dma((4,))]
         + [dma((2, 4))] * 4
         + [dma((4,)), dma((4,)), dma((4,))],
         compiler_params=pltpu.CompilerParams(
@@ -1406,7 +1765,7 @@
         ),
         cost_estimate=pl.CostEstimate(flops=1000, bytes_accessed=1000, transcendentals=0),
         name="finish_reduction",
-    )(p1, p2, s3, b4)
+    )(p1, p2, s3, k4, b4)
 
 
 def swap_route(bit, count):
@@ -1442,10 +1801,10 @@
 def exchange(piece, at, part):
     moved = [piece[: at + part]]
     for d in range(1, 4):
-        moved.append(
-            lax.ppermute(piece[at + d * part : at + (d + 1) * part], "grp", swap_route(d, 4))
-        )
+        moved.append(swap(piece[at + d * part : at + (d + 1) * part], d))
     moved.append(piece[at + 4 * part :])
+    if piece.shape[0] == IN_ROWS:
+        moved += [swap(piece[SMALL_AT:], d) for d in range(1, 4)]
     return jnp.concatenate(moved, axis=0)
 
 
@@ -1461,11 +1820,11 @@
     return pair.reshape((8,) + piece.shape)
 
 
-def finish_all(piece1, piece2, summed3, buf4, replicas):
+def finish_all(piece1, piece2, summed3, keep4, send4, replicas):
     if replicas == 8:
-        return finish_reduction(piece1, piece2, summed3, buf4)
+        return finish_reduction(piece1, piece2, summed3, keep4, send4)
     piece3 = reduce_z(summed3, replicas)
-    piece4 = reduce_z(add_arrived(buf4[0], swap_x(buf4[1], replicas)), replicas)
+    piece4 = reduce_z(add_arrived(keep4, swap_x(send4, replicas)), replicas)
     return [
         spread(exchange(piece, *move), replicas)
         for piece, move in (
@@ -1478,28 +1837,8 @@
     return lax.optimization_barrier(values)
 
 
-def by_source(blocks, mine):
-    y, c = mine // 2 == 1, mine % 2 == 1
-    blocks = jnp.where(c, jnp.stack([blocks[k ^ 1] for k in range(4)]), blocks)
-    return jnp.where(y, jnp.stack([blocks[k ^ 2] for k in range(4)]), blocks)
-
-
 def swap(array, d):
     return lax.ppermute(array, "grp", swap_route(d, 4))
-
-
-def reshard_near(pieces_of, mine):
-    pieces = [pieces_of(mine ^ d, 0, None) for d in range(4)]
-    return pieces[0], swap(pieces[1], 1), jnp.stack([swap(pieces[2], 2), swap(pieces[3], 3)])
-
-
-def reshard_wide(pieces_of, mine, replicas):
-    z = (lax.axis_index("rep") % 8) // 2
-    own, sibling = pieces_of(mine, 0, None), swap(pieces_of(mine ^ 1, 0, None), 1)
-    part = own.shape[0] // 4
-    far = [swap(pieces_of(mine ^ d, part * z, part), d) for d in (2, 3)]
-    far = lax.all_gather(jnp.stack(far), "rep", axis=0, axis_index_groups=planes_of(replicas))
-    return own, sibling, far
 
 
 def per_device(
@@ -1512,84 +1851,49 @@
     rows, width = x_input.shape[1], x_input.shape[2]
     shard = w_in.shape[1]
 
-    def cut(array, start, size):
-        return lax.dynamic_slice_in_dim(array, start, size, array.ndim - 1)
-
-    small_sizes = [part.size for part in (norm_gain, conv_w, out_gain, w_ab)]
-    packed = jnp.concatenate(
-        [part.reshape(-1) for part in (norm_gain, conv_w, out_gain, w_ab)]
-    )
-    packed = jnp.stack([packed] + [swap(packed, d) for d in range(1, 4)])
-    packed = by_source(packed, mine)
-    at = [sum(small_sizes[:k]) for k in range(5)]
-
-    def unpack(k, shape, dim):
-        part = packed[:, at[k] : at[k + 1]].reshape((parts,) + shape)
-        part = jnp.moveaxis(part, 0, dim)
-        return part.reshape(shape[:dim] + (parts * shape[dim],) + shape[dim + 1 :])
-
-    gains = unpack(0, norm_gain.shape, 2).astype(f32)
-    taps_all = unpack(1, conv_w.shape, 2).astype(f32)
-    out_gains = unpack(2, out_gain.shape, 1).astype(f32)
-    ab_all = unpack(3, w_ab.shape, 1)
-
-    def in_pieces(l):
-        def piece(t, start, count):
-            rows = w_in[l] if count is None else lax.dynamic_slice_in_dim(w_in[l], start, count, 0)
-            return jnp.concatenate(
-                [
-                    cut(rows, 256 * t, 256),
-                    cut(rows, HK + 256 * t, 256),
-                    cut(rows, 2 * HK + 512 * t, 512),
-                    cut(rows, CH + 512 * t, 512),
-                ],
-                axis=1,
-            )
-
-        return piece
-
-    def up_pieces(l):
-        def piece(t, start, count):
-            rows = ffn_in[l]
-            if count is not None:
-                rows = lax.dynamic_slice_in_dim(rows, start, count, 0)
-            gate = cut(rows, 704 * t, 704)
-            value = cut(rows, FF + 704 * t, 704)
-            return jnp.concatenate(
-                [gate[:, :640], value[:, :640], gate[:, 640:], value[:, 640:]], axis=1
-            )
-
-        return piece
-
+    pack = jnp.concatenate(
+        [
+            norm_gain.reshape(-1, 128),
+            conv_w.reshape(-1, 128),
+            jnp.swapaxes(w_ab, 1, 2).reshape(-1, 128),
+            out_gain.reshape(-1, 128),
+            jnp.zeros((PACK_ROWS - OUT_GAIN_AT - 1, 128), bf16),
+        ]
+    ).astype(f32)
+    normed, projected, small, in_weight, *rest = start(x_input[0], pack, w_in)
+    gains, taps_pair, ab_pair, out_pair = rest[0:4], rest[4:6], rest[6:8], rest[8:10]
     small_weights = []
     for l in range(LAYERS):
-        ab = jnp.concatenate([cut(ab_all[l], 2 * mine, 2), cut(ab_all[l], H + 2 * mine, 2)], axis=1)
-        ab = jnp.pad(ab, ((0, 0), (0, 124)))
-        taps = jnp.concatenate(
-            [
-                cut(taps_all[l], 256 * mine, 256),
-                cut(taps_all[l], HK + 256 * mine, 256),
-                cut(taps_all[l], 2 * HK + 512 * mine, 512),
-            ],
-            axis=1,
-        )
-        taps = jnp.pad(taps, ((0, 4), (0, 0)))
         heads = jnp.pad(jnp.stack([a_log[l], dt_bias[l]]).astype(f32), ((0, 6), (2, 124)))
-        gain = jnp.pad(out_gains[l][None], ((0, 7), (0, 0)))
-        small_weights.append((gains[l, 0:1], gains[l, 1:2], ab, taps, heads, gain, w_out[l], ffn_out[l]))
+        small_weights.append(
+            (
+                gains[2 * l], gains[2 * l + 1], ab_pair[l], taps_pair[l], heads, out_pair[l],
+            )
+        )
 
     residual = x_input[0].astype(f32)
     kept = []
-    in_weights = [reshard_near(in_pieces(0), mine)]
-    up_weights = [reshard_wide(up_pieces(0), mine, replicas)]
-    in_weights.append(reshard_wide(in_pieces(1), mine, replicas))
-    up_weights.append(reshard_wide(up_pieces(1), mine, replicas))
+    in_weights, up_weights = [(in_weight,)], []
     for l in range(LAYERS):
-        gain_one, gain_two, ab, taps, heads, gain, out_weight, down_weight = small_weights[l]
-        normed, projected, small = project(residual, gain_one, in_weights[l], ab)
-        gated, *saved = mixer_forward(projected, small, taps, heads, gain)
+        gain_one, gain_two, ab, taps, heads, gain = small_weights[l]
+        if l > 0:
+            normed, projected, small = project(residual, gain_one, ab, in_weights[l])
+        gated, *saved = mixer_forward(
+            l, projected, small, taps, heads, gain, (ffn_in, w_in)[: LAYERS - l]
+        )
+        up_weights.append((ffn_in, saved[4]))
+        if l == 0:
+            near, far = saved[5:]
+            in_weights.append(
+                (
+                    w_in,
+                    near,
+                    lax.all_gather(far, "rep", axis=0, axis_index_groups=planes_of(replicas)),
+                )
+            )
+        saved = saved[:4]
         mid, normed_two, up, hidden, residual_out = ffn_forward(
-            gated, out_weight, residual, gain_two, down_weight, up_weights[l]
+            l, gated, residual, gain_two, w_out, ffn_out, up_weights[l]
         )
         kept.append((residual, normed, projected, small, gated, saved, mid, normed_two, up, hidden))
         residual = residual_out
@@ -1598,20 +1902,20 @@
     d_residual = cotangent[0].astype(f32)
 
     def ffn_part(l, d_residual):
-        gain_one, gain_two, ab, taps, heads, gain, out_weight, down_weight = small_weights[l]
+        gain_one, gain_two, ab, taps, heads, gain = small_weights[l]
         residual, normed, projected, small, gated, saved, mid, normed_two, up, hidden = kept[l]
         return ffn_backward(
-            d_residual, up, hidden, normed_two, mid, gain_two, gated, out_weight, down_weight,
+            l, d_residual, up, hidden, normed_two, mid, gain_two, gated, w_out, ffn_out,
             up_weights[l],
         )
 
     def mixer_part(l, d_gated):
-        gain_one, gain_two, ab, taps, heads, gain, out_weight, down_weight = small_weights[l]
+        gain_one, gain_two, ab, taps, heads, gain = small_weights[l]
         residual, normed, projected, small, gated, saved, mid, normed_two, up, hidden = kept[l]
         return mixer_backward(projected, small, taps, heads, gain, saved, d_gated)
 
     def project_part(l, d_mid, g_gain_two, mixed):
-        gain_one, gain_two, ab, taps, heads, gain, out_weight, down_weight = small_weights[l]
+        gain_one, gain_two, ab, taps, heads, gain = small_weights[l]
         residual, normed, projected, small, gated, saved, mid, normed_two, up, hidden = kept[l]
         d_projected, d_small, g_taps, g_heads = mixed
         return project_backward(
@@ -1619,30 +1923,28 @@
             g_gain_two, g_taps, g_heads,
         )
 
-    d_mid, d_gated, g_gain_two, buf1 = ffn_part(1, d_residual)
-    arrived1 = swap_x(buf1[1], replicas)
+    d_mid, d_gated, g_gain_two, keep1, send1 = ffn_part(1, d_residual)
+    arrived1 = swap_x(send1, replicas)
     mixed = mixer_part(1, d_gated)
-    d_residual, buf2 = project_part(1, d_mid, g_gain_two, mixed)
+    d_residual, keep2, send2 = project_part(1, d_mid, g_gain_two, mixed)
     d_residual, arrived1 = tie(d_residual, arrived1)
-    piece1 = reduce_z(add_arrived(buf1[0], arrived1), replicas)
-    arrived2 = swap_x(buf2[1], replicas)
-    d_mid, d_gated, g_gain_two, buf3 = ffn_part(0, d_residual)
+    piece1 = reduce_z(add_arrived(keep1, arrived1), replicas)
+    arrived2 = swap_x(send2, replicas)
+    d_mid, d_gated, g_gain_two, keep3, send3 = ffn_part(0, d_residual)
     d_gated, piece1, arrived2 = tie(d_gated, piece1, arrived2)
-    piece2 = reduce_z(add_arrived(buf2[0], arrived2), replicas)
-    arrived3 = swap_x(buf3[1], replicas)
+    piece2 = reduce_z(add_arrived(keep2, arrived2), replicas)
+    arrived3 = swap_x(send3, replicas)
     mixed = mixer_part(0, d_gated)
-    d_residual, buf4 = project_part(0, d_mid, g_gain_two, mixed)
+    d_residual, keep4, send4 = project_part(0, d_mid, g_gain_two, mixed)
     d_residual, arrived3 = tie(d_residual, arrived3)
-    summed3 = add_arrived(buf3[0], arrived3)
-    final1, final2, final3, final4 = finish_all(piece1, piece2, summed3, buf4, replicas)
-    ffn_grads = assemble_ffn(1, final1, ())
-    *in_grads, table_one = assemble_in(1, final2, ())
-    down_grads, out_grads, up_grads = assemble_ffn(0, final3, tuple(ffn_grads))
-    w_in_grads, table_zero = assemble_in(0, final4, tuple(in_grads))
+    summed3 = add_arrived(keep3, arrived3)
+    final1, final2, final3, final4 = finish_all(piece1, piece2, summed3, keep4, send4, replicas)
+    down_grads, out_grads, up_grads, w_in_grads, everyone = assemble(
+        (final1, final2, final3, final4)
+    )
     input_grad = d_residual.astype(bf16)[None]
 
-    tables = jnp.stack([table_zero, table_one])
-    everyone = lax.all_gather(tables, "grp", axis=0)
+    tables = lax.dynamic_index_in_dim(everyone, mine, 0, keepdims=False)
     sums = jnp.sum(everyone[:, :, 64:82], axis=0)
     grad_gain = lax.dynamic_slice_in_dim(
         sums[:, :16].reshape(LAYERS, 2, width), mine * shard, shard, 2

time: 914 us -> 795 us (0.87)
  local copies, waits for them, and re-layouts: 84 us -> 16.6 us
  waiting for transfers between devices: 31.6 us -> 1.96 us
  Pallas kernels: 709 us -> 734 us
  other arithmetic: 37.3 us -> 17.1 us
  starting transfers between devices: 18.7 us -> 3.84 us
  blocking collectives: 9.2 us -> 0 us
    ppermute x15 -> x0, waiting for transfers between devices: 31.5 us -> none  [swap(): return lax.ppermute(array, 'grp', swap_route(d, 4))]
    pallas_call x8, Pallas kernels: 272 us -> 298 us  [call(): pl.pallas_call(kernel, out_shape=out_shape, in_specs=[vmem] * len(inputs)...]
    pallas_call x2, Pallas kernels: 90.8 us -> 68.9 us  [mixer_backward(): pl.pallas_call(mixer_backward_kernel, out_shape=(jax.ShapeDtypeStruct((to...]
    slice x43 -> x2, local copies, waits for them, and re-layouts: 19 us -> 1.37 us  [the longest x1 0.73 us: per_device(): dt_bias[l]]
    ppermute x15 -> x0, starting transfers between devices: 14.2 us -> none  [swap(): return lax.ppermute(array, 'grp', swap_route(d, 4))]
    squeeze x6 -> x1, local copies, waits for them, and re-layouts: 14.2 us -> 0.92 us  [per_device(): tables = lax.dynamic_index_in_dim(everyone, mine, 0, keepdims=False)]
    unnamed x124 -> x56, local copies, waits for them, and re-layouts: 20.7 us -> 8.21 us
    pallas_call x6 -> x3, Pallas kernels: 84.8 us -> 97.1 us  [the longest x2 80.5 us: mixer_forward(): pl.pallas_call(partial(mixer_forward_kernel, layer), out_shape=(jax.Shape...]
  transfers between devices with their start and end apart: 23 -> 6, of which waited for: 4 -> 1; matrix products, arithmetic and copies ran while one was open for 10% -> 2% of each run, Pallas kernels for 36% -> 27%
where the time goes in v3:
time: 795 us; the launch traced here: 787 us
  Pallas kernels  734 us (92%)
  other arithmetic  17.1 us (2%)
  local copies, waits for them, and re-layouts  16.6 us (2%)
  between operations  14.3 us (2%)
    pallas_call x8, Pallas kernels, call(): pl.pallas_call(kernel, out_shape=out_shape, in_specs=[vmem] * len(inputs)...  298 us
    pallas_call x1, Pallas kernels, finish_reduction(): pl.pallas_call(finish_kernel, out_shape=tuple((like(8, *shape, dtype=bf16...  270 us
    pallas_call x2, Pallas kernels, mixer_forward(): pl.pallas_call(partial(mixer_forward_kernel, layer), out_shape=(jax.Shape...  80.5 us
    pallas_call x2, Pallas kernels, mixer_backward(): pl.pallas_call(mixer_backward_kernel, out_shape=(jax.ShapeDtypeStruct((to...  68.9 us
    pallas_call x1, Pallas kernels, assemble(): pl.pallas_call(assemble_kernel, out_shape=tuple((like(*shape) for shape i...  16.7 us
  transfers between devices with their start and end apart: 6, of which 1 were waited for; matrix products, arithmetic and copies ran while one was open for 2% of the time, Pallas kernels for 27%

profile of v3, /device:TPU:0, one launch (start us, length us, event | category | flops | bytes accessed | tf_op | source)
XLA Modules:
  0.0 787.5 jit_solution(6535667500749751711)
XLA Ops:
  9.4 0.7 reshape.68
  12.3 43.1 %start.1 = (bf16[1024,1024]{1,0:T(8,128)(2,1)}, bf16[1024,1536]{1,0:T(8,128)(2,1)}, f32[1024,128]{1,0:T(8,128)}, bf16[1024,1536]{1,0:T(8,128)(2,1)}, f32[1,1024]...) custom-call(bf16[256,1024]{1,0:T(8,128)(2,1)} %bitcast.44, ...), custom_call_target="tpu_custom_call" | custom-call | flops 1000 | bytes 1000 | tf_op jit(solution)/shard_map/start/pallas_call | solution.py:553
  56.1 40.8 %mixer_forward.2 = (bf16[1024,512]{1,0:T(8,128)(2,1)}, f32[8,2,128,256]{3,2,1,0:T(8,128)}, f32[8,2,128,128]{3,2,1,0:T(8,128)}, f32[8,2,128,256]{3,2,1,0:T(8,128)...) custom-call(bf16[1024,1536]{1,0:T(8,128)(2,1)} %get-tuple-element.93, ...), custom_call_target="tpu_custom_call" | custom-call | tf_op jit(solution)/shard_map/mixer_forward/pallas_call | solution.py:228
  97.5 1.1 bitcast_convert_fusion.1.res_ref
  98.6 44.3 %ffn_forward.2 = (f32[256,1024]{1,0:T(8,128)}, bf16[1024,1024]{1,0:T(8,128)(2,1)}, bf16[1024,1536]{1,0:T(8,128)(2,1)}, bf16[1024,768]{1,0:T(8,128)(2,1)}, f32[256,1024]{1,0:T(8,128)}) custom-call(bf16[1024,512]{1,0:T(8,128)(2,1)} %get-tuple-element.97.gated_ref, f32[256,1024]{1,0:T(8,128)} %bitcast_convert_fusion.1.res_ref, ...), custom_call_target="tpu_custom_call" | custom-call | flops 1000 | bytes 1000 | tf_op jit(solution)/shard_map/ffn_forward/pallas_call | solution.py:553
  142.9 1.1 bitcast_convert_fusion.dres_ref
  144.0 19.4 %project.1 = (bf16[1024,1024]{1,0:T(8,128)(2,1)}, bf16[1024,1536]{1,0:T(8,128)(2,1)}, f32[1024,128]{1,0:T(8,128)}) custom-call(f32[256,1024]{1,0:T(8,128)} %get-tuple-element.100.res_ref, f32[1,1024]{1,0:T(1,128)} %get-tuple-element.101.gain_ref, bf16[1024,128]{1,0:T(8,128)(2,1)} %get-tuple-element.102.ab_ref, bf16[2,256,6144]{2,1,0:T(8,128)(2,1)} %refs_0_.7, ...), custom_call_target="tpu_custom_call" | custom-call | flops 1000 | bytes 1000 | tf_op jit(solution)/shard_map/project/pallas_call | solution.py:553
  163.4 39.6 %mixer_forward.3 = (bf16[1024,512]{1,0:T(8,128)(2,1)}, f32[8,2,128,256]{3,2,1,0:T(8,128)}, f32[8,2,128,128]{3,2,1,0:T(8,128)}, f32[8,2,128,256]{3,2,1,0:T(8,128)...) custom-call(bf16[1024,1536]{1,0:T(8,128)(2,1)} %get-tuple-element.105.proj_ref, ...), custom_call_target="tpu_custom_call" | custom-call | tf_op jit(solution)/shard_map/mixer_forward/pallas_call | solution.py:228
  203.0 44.2 %ffn_forward.3 = (f32[256,1024]{1,0:T(8,128)}, bf16[1024,1024]{1,0:T(8,128)(2,1)}, bf16[1024,1536]{1,0:T(8,128)(2,1)}, bf16[1024,768]{1,0:T(8,128)(2,1)}, f32[256,1024]{1,0:T(8,128)}) custom-call(bf16[1024,512]{1,0:T(8,128)(2,1)} %get-tuple-element.109.gated_ref, f32[256,1024]{1,0:T(8,128)} %get-tuple-element.100.res_ref, ...), custom_call_target="tpu_custom_call" | custom-call | flops 1000 | bytes 1000 | tf_op jit(solution)/shard_map/ffn_forward/pallas_call | solution.py:553
  247.3 49.5 %ffn_backward.2 = (f32[256,1024]{1,0:T(8,128)}, bf16[1024,512]{1,0:T(8,128)(2,1)}, f32[8,1024]{1,0:T(8,128)}, bf16[4,2624,128]{2,1,0:T(8,128)(2,1)}, bf16[4,2624,128]{2,1,0:T(8,128)(2,1)}) custom-call(f32[256,1024]{1,0:T(8,128)} %bitcast_convert_fusion.dres_ref, bf16[1024,1536]{1,0:T(8,128)(2,1)} %get-tuple-element.121.up_ref, ...), custom_call_target="tpu_custom_call" | custom-call | flops 1000 | bytes 1000 | tf_op jit(solution)/shard_map/ffn_backward/pallas_call | solution.py:553
  296.8 1.0 collective-permute-start
  297.8 1.2 copy-done.7
  299.0 34.3 %mixer_backward.2 = (bf16[1024,1536]{1,0:T(8,128)(2,1)}, bf16[1024,128]{1,0:T(8,128)(2,1)S(1)}, f32[8,1024]{1,0:T(8,128)S(1)}, f32[8,256]{1,0:T(8,128)S(1)}) custom-call(bf16[1024,1536]{1,0:T(8,128)(2,1)} %get-tuple-element.105.proj_ref, f32[1024,128]{1,0:T(8,128)S(1)} %copy-done.3, f32[8,1024]{1,0:T(8,128)S(1)} %copy-done.11, f32[8,128]{1,0:T(8,128)S(1)} %copy-done.12, ...), custom_call_target="tpu_custom_call" | custom-call | tf_op jit(solution)/shard_map/mixer_backward/pallas_call | solution.py:393
  335.2 23.8 %project_backward.2 = (f32[256,1024]{1,0:T(8,128)}, bf16[4,1552,128]{2,1,0:T(8,128)(2,1)}, bf16[4,1552,128]{2,1,0:T(8,128)(2,1)}) custom-call(bf16[1024,1536]{1,0:T(8,128)(2,1)} %get-tuple-element.126.dproj_ref, bf16[1024,128]{1,0:T(8,128)(2,1)} %copy-done.8, bf16[1024,128]{1,0:T(8,128)(2,1)} %get-tuple-element.102.ab_ref, ...), custom_call_target="tpu_custom_call" | custom-call | flops 1000 | bytes 1000 | tf_op jit(solution)/shard_map/project_backward/pallas_call | solution.py:553
  359.1 2.2 add_convert_fusion.1
  361.4 1.2 collective-permute-start.1
  362.6 49.6 %ffn_backward.3 = (f32[256,1024]{1,0:T(8,128)}, bf16[1024,512]{1,0:T(8,128)(2,1)}, f32[8,1024]{1,0:T(8,128)}, bf16[4,2624,128]{2,1,0:T(8,128)(2,1)}, bf16[4,2624,128]{2,1,0:T(8,128)(2,1)}) custom-call(f32[256,1024]{1,0:T(8,128)} %get-tuple-element.135.dres_ref, bf16[1024,1536]{1,0:T(8,128)(2,1)} %get-tuple-element.136.up_ref, ...), custom_call_target="tpu_custom_call" | custom-call | flops 1000 | bytes 1000 | tf_op jit(solution)/shard_map/ffn_backward/pallas_call | solution.py:553
  412.1 1.1 collective-permute-start.2
  413.2 1.9 reduce-scatter.3.cloned.1.call-done
  415.1 1.6 add_convert_fusion.2
  416.8 2.2 convert_bitcast_fusion.1
  419.0 1.2 copy-done.4
  420.3 1.2 copy-done.5
  421.5 34.6 %mixer_backward.3 = (bf16[1024,1536]{1,0:T(8,128)(2,1)}, bf16[1024,128]{1,0:T(8,128)(2,1)S(1)}, f32[8,1024]{1,0:T(8,128)S(1)}, f32[8,256]{1,0:T(8,128)S(1)}) custom-call(bf16[1024,1536]{1,0:T(8,128)(2,1)} %get-tuple-element.93.proj_ref, f32[1024,128]{1,0:T(8,128)S(1)} %copy-done.2, f32[8,1024]{1,0:T(8,128)S(1)} %copy-done.10, f32[8,128]{1,0:T(8,128)S(1)} %copy-done.13, ...), custom_call_target="tpu_custom_call" | custom-call | tf_op jit(solution)/shard_map/mixer_backward/pallas_call | solution.py:393
  458.0 24.3 %project_backward.3 = (f32[256,1024]{1,0:T(8,128)}, bf16[4,1552,128]{2,1,0:T(8,128)(2,1)}, bf16[4,1552,128]{2,1,0:T(8,128)(2,1)}) custom-call(bf16[1024,1536]{1,0:T(8,128)(2,1)} %get-tuple-element.145.dproj_ref, bf16[1024,128]{1,0:T(8,128)(2,1)} %copy-done.9, bf16[1024,128]{1,0:T(8,128)(2,1)} %get-tuple-element.147.ab_ref, ...), custom_call_target="tpu_custom_call" | custom-call | flops 1000 | bytes 1000 | tf_op jit(solution)/shard_map/project_backward/pallas_call | solution.py:553
  482.3 2.1 convert_bitcast_fusion
  484.4 4.0 add_convert_fusion.s3
  488.3 269.5 %finish_reduction.1 = (bf16[8,2624,128]{2,1,0:T(8,128)(2,1)}, bf16[8,1600,128]{2,1,0:T(8,128)(2,1)}, bf16[8,2624,128]{2,1,0:T(8,128)(2,1)}, bf16[8,1600,128]{2,1,0:T(8,128)(2,1)}) custom-call(bf16[2624,128]{1,0:T(8,128)(2,1)} %bitcast.45, bf16[1552,128]{1,0:T(8,128)(2,1)} %bitcast.46, bf16[4,2624,128]{2,1,0:T(8,128)(2,1)} %add_convert_fusion.s3, ...), custom_call_target="tpu_custom_call" | custom-call | flops 1000 | bytes 1000 | tf_op jit(solution)/shard_map/finish_reduction/pallas_call | solution.py:1749
  757.8 16.7 %assemble.1 = (f32[2,704,1024]{2,1,0:T(8,128)}, f32[2,512,1024]{2,1,0:T(8,128)}, f32[2,256,5632]{2,1,0:T(8,128)}, f32[2,256,6144]{2,1,0:T(8,128)}, f32[4,2,128,128]{3,2,1,0:T(8,128)}) custom-call(bf16[8,2624,128]{2,1,0:T(8,128)(2,1)} %get-tuple-element.165.f1, bf16[8,1600,128]{2,1,0:T(8,128)(2,1)} %get-tuple-element.166.f2, ...), custom_call_target="tpu_custom_call" | custom-call | tf_op jit(solution)/shard_map/assemble/pallas_call | solution.py:1406
  774.5 0.9 slice_reduce_fusion
  775.4 1.0 fusion.16
  777.9 0.9 dynamic-slice_bitcast_fusion
  (86 shorter events, 12.9 us)
Async XLA Ops:
  7.2 136.8 %all-gather.3.cloned.1.call-start = ((), (), s32[]{:S(2)}) async-start(), calls=%async_computation.4 | async-start | bytes 1966080 | tf_op jit(solution)/shard_map/all_gather | solution.py:1891
  56.1 41.4 %copy-start.22 = (bf16[1,256,1024]{2,1,0:T(8,128)(2,1)S(1)}, bf16[1,256,1024]{2,1,0:T(8,128)(2,1)}, u32[]{:S(2)}) copy-start(bf16[1,256,1024]{2,1,0:T(8,128)(2,1)} %param.12) | copy-start | bytes 1572868
  97.0 318.2 %reduce-scatter.3.cloned.1.call-start = ((), (), s32[]{:S(2)}) async-start(), calls=%async_computation.2 | async-start | bytes 3358720 | tf_op jit(solution)/shard_map/reduce_scatter | solution.py:1790
  98.6 44.3 %copy-start.24 = (bf16[1,256,1024]{2,1,0:T(8,128)(2,1)S(1)}, bf16[1,256,1024]{2,1,0:T(8,128)(2,1)}, u32[]{:S(2)}) copy-start(bf16[1,256,1024]{2,1,0:T(8,128)(2,1)} %param.23) | copy-start | bytes 1572868
  247.3 50.5 %copy-start.1 = (f32[8,2,128,256]{3,2,1,0:T(8,128)S(1)}, f32[8,2,128,256]{3,2,1,0:T(8,128)}, u32[]{:S(2)}) copy-start(f32[8,2,128,256]{3,2,1,0:T(8,128)} %get-tuple-element.117.start_ref) | copy-start | bytes 6291460
  247.3 50.5 %copy-start.3 = (f32[1024,128]{1,0:T(8,128)S(1)}, f32[1024,128]{1,0:T(8,128)}, u32[]{:S(2)}) copy-start(f32[1024,128]{1,0:T(8,128)} %get-tuple-element.106.small_ref) | copy-start | bytes 1572868
  247.3 50.5 %copy-start.6 = (f32[8,2,128,128]{3,2,1,0:T(8,128)S(1)}, f32[8,2,128,128]{3,2,1,0:T(8,128)}, u32[]{:S(2)}) copy-start(f32[8,2,128,128]{3,2,1,0:T(8,128)} %get-tuple-element.118.inv_ref) | copy-start | bytes 3145732
  247.3 50.5 %copy-start.11 = (f32[8,1024]{1,0:T(8,128)S(1)}, f32[8,1024]{1,0:T(8,128)}, u32[]{:S(2)}) copy-start(f32[8,1024]{1,0:T(8,128)} %get-tuple-element.107.taps_ref) | copy-start | bytes 98308
  247.3 50.5 %copy-start.12 = (f32[8,128]{1,0:T(8,128)S(1)}, f32[8,128]{1,0:T(8,128)}, u32[]{:S(2)}) copy-start(f32[8,128]{1,0:T(8,128)} %get-tuple-element.209.heads_ref) | copy-start | bytes 12292
  247.3 50.5 %copy-start.17 = (f32[8,256]{1,0:T(8,128)S(1)}, f32[8,256]{1,0:T(8,128)}, u32[]{:S(2)}) copy-start(f32[8,256]{1,0:T(8,128)} %get-tuple-element.108.gain_ref) | copy-start | bytes 24580
  296.8 62.3 %collective-permute-start = (bf16[4,2624,128]{2,1,0:T(8,128)(2,1)}, bf16[4,2624,128]{2,1,0:T(8,128)(2,1)S(1)}, u32[]{:S(2)}, u32[]{:S(2)}) collective-permute-start(bf16[4,2624,128]{2,1,0:T(8,128)(2,1)} %get-tuple-element.134), channel_id=1, source_target_pairs={{0,4},{4,0},{8,12},{12,8},{16,20},{20,16},{24,28},{28,24},{1,5},{5... | collective-permute-start | bytes 8060936 | tf_op jit(solution)/shard_map/ppermute | solution.py:1782
  297.8 1.2 copy-start.7
  333.3 0.7 copy-start.8
  334.0 0.6 copy-start.14
  334.6 0.6 copy-start.18
  335.2 23.9 %copy-start.21 = (bf16[4,2624,128]{2,1,0:T(8,128)(2,1)S(1)}, bf16[4,2624,128]{2,1,0:T(8,128)(2,1)}, u32[]{:S(2)}) copy-start(bf16[4,2624,128]{2,1,0:T(8,128)(2,1)} %get-tuple-element.141) | copy-start | bytes 8060932
  361.3 127.0 %reduce-scatter.5.cloned.1.call-start = ((), (), s32[]{:S(2)}) async-start(), calls=%async_computation.3 | async-start | bytes 1986560 | tf_op jit(solution)/shard_map/reduce_scatter | solution.py:1790
  361.4 51.9 %collective-permute-start.1 = (bf16[4,1552,128]{2,1,0:T(8,128)(2,1)}, bf16[4,1552,128]{2,1,0:T(8,128)(2,1)S(1)}, u32[]{:S(2)}, u32[]{:S(2)}) collective-permute-start(bf16[4,1552,128]{2,1,0:T(8,128)(2,1)} %get-tuple-element.143), channel_id=1, source_target_pairs={{0,4},{4,0},{8,12},{12,8},{16,20},{20,16},{24,28},{28,24},{1,5},{5... | collective-permute-start | bytes 4767752 | tf_op jit(solution)/shard_map/ppermute | solution.py:1782
  362.6 52.6 %copy-start.23 = (bf16[4,1552,128]{2,1,0:T(8,128)(2,1)S(1)}, bf16[4,1552,128]{2,1,0:T(8,128)(2,1)}, u32[]{:S(2)}) copy-start(bf16[4,1552,128]{2,1,0:T(8,128)(2,1)} %get-tuple-element.159) | copy-start | bytes 4767748
  412.1 70.1 %collective-permute-start.2 = (bf16[4,2624,128]{2,1,0:T(8,128)(2,1)}, bf16[4,2624,128]{2,1,0:T(8,128)(2,1)}, u32[]{:S(2)}, u32[]{:S(2)}) collective-permute-start(bf16[4,2624,128]{2,1,0:T(8,128)(2,1)} %get-tuple-element.156), channel_id=1, source_target_pairs={{0,4},{4,0},{8,12},{12,8},{16,20},{20,16},{24,28},{28,24},{1,5},{5... | collective-permute-start | bytes 8060936 | tf_op jit(solution)/shard_map/ppermute | solution.py:1782
  416.7 2.3 copy-start
  416.7 2.3 copy-start.2
  416.7 2.3 copy-start.10
  416.7 2.3 copy-start.13
  416.7 2.3 copy-start.16
  419.0 1.2 copy-start.4
  420.3 1.2 copy-start.5
  456.1 0.7 copy-start.9
  456.8 0.6 copy-start.15
  457.4 0.6 copy-start.19
  458.0 26.4 %copy-start.20 = (bf16[4,2624,128]{2,1,0:T(8,128)(2,1)S(1)}, bf16[4,2624,128]{2,1,0:T(8,128)(2,1)}, u32[]{:S(2)}) copy-start(bf16[4,2624,128]{2,1,0:T(8,128)(2,1)} %get-tuple-element.161) | copy-start | bytes 8060932
Sparse Core Ops, SparseCore 0:
  97.1 37.3 all-gather.2
  361.5 53.6 reduce-scatter.2
  418.1 35.4 reduce-scatter.4

commit v4 on v3

--- a/solution.py
+++ b/solution.py
@@ -108,21 +108,38 @@
     return total
 
 
-UNROLL = 2
-
-
 def mixer_forward_kernel(
-    layer, proj_ref, small_ref, taps_ref, heads_ref, gain_ref, *refs
+    layer, proj_hbm, small_ref, taps_ref, heads_ref, gain_ref, *refs
 ):
     if layer == 0:
         up_source, in_source, *refs = refs
         *outs, up_whole, near, far = refs[:8]
-        halo, state, *sems = refs[8:]
+        refs = refs[8:]
     else:
         up_source, *refs = refs
         *outs, up_whole = refs[:6]
-        halo, state, *sems = refs[6:]
-    gated_ref, start_ref, inv_ref, pseudo_ref, mixed_ref = outs
+        refs = refs[6:]
+    proj_ref, gated_ref, start_ref, inv_ref, pseudo_ref, mixed_ref = refs[:6]
+    load_sem, store_sem, halo, state, *sems = refs[6:]
+
+    def chunk_rows(c):
+        return pl.ds(pl.multiple_of(c * CHUNK, CHUNK), CHUNK)
+
+    def load(c):
+        rows = chunk_rows(c)
+        return pltpu.make_async_copy(proj_hbm.at[rows], proj_ref.at[rows], load_sem.at[c])
+
+    def stores(c):
+        rows = chunk_rows(c)
+        pairs = zip(refs[1:6], outs, (rows, c, c, c, rows))
+        return [
+            pltpu.make_async_copy(src.at[at], dst.at[at], store_sem.at[k, c])
+            for k, (src, dst, at) in enumerate(pairs)
+        ]
+
+    chunks = proj_ref.shape[0] // CHUNK
+    for c in range(chunks):
+        load(c).start()
     ready = greet_wide(*place())
     shard = Reshard(up_source.at[layer], up_lanes, up_whole, *sems[:5])
     if layer == 0:
@@ -175,9 +192,10 @@
             last = c_col[CHUNK - 1 :, :]
             before = state[h]
             start_ref[c, h] = before
+            inv = inv.astype(bf16)
             inv_ref[c, h] = inv
             read = mm2(jnp.concatenate([q, k], axis=0), before)
-            pseudo = mb(inv, v.astype(f32) - growth * read[CHUNK:])
+            pseudo = mm(inv, (v.astype(f32) - growth * read[CHUNK:]).astype(bf16))
             pseudo_ref[c, h] = pseudo
             tail = jnp.exp(last - c_col) * beta_col
             state[h] = jnp.exp(last) * before + mm2(k, tail * pseudo, TN)
@@ -189,32 +207,36 @@
             gated_ref[rows, 256 * h : 256 * h + 256] = gated.astype(bf16)
 
     def body(step, carry):
-        ready = [prepare(step * UNROLL + u) for u in range(UNROLL)]
-        for u in range(UNROLL):
-            advance(step * UNROLL + u, *ready[u])
+        load(step).wait()
+        advance(step, *prepare(step))
+        for store in stores(step):
+            store.start()
         @pl.when(step == 0)
         def _():
             shard.start_far(1)
             if layer == 0:
                 quarter.start_near()
 
-        @pl.when(step == 1)
+        @pl.when(step == 2)
         def _():
             shard.forward(0)
             if layer == 0:
                 quarter.start_quarter()
 
-        @pl.when(step == 2)
+        @pl.when(step == 4)
         def _():
             shard.forward(1)
 
         return carry
 
-    lax.fori_loop(0, proj_ref.shape[0] // (CHUNK * UNROLL), body, 0)
+    lax.fori_loop(0, chunks, body, 0)
     shard.wait()
     shard.finish()
     if layer == 0:
         quarter.wait_quarter()
+    for c in range(chunks):
+        for store in stores(c):
+            store.wait()
 
 
 def mixer_forward(layer, projected, small, taps, heads, gain, sources):
@@ -230,14 +252,24 @@
         out_shape=(
             jax.ShapeDtypeStruct((tokens, 512), bf16),
             jax.ShapeDtypeStruct((chunks, 2, DK, DV), f32),
-            jax.ShapeDtypeStruct((chunks, 2, CHUNK, CHUNK), f32),
+            jax.ShapeDtypeStruct((chunks, 2, CHUNK, CHUNK), bf16),
             jax.ShapeDtypeStruct((chunks, 2, CHUNK, DV), f32),
             jax.ShapeDtypeStruct((tokens, 512), f32),
         )
         + wholes,
-        in_specs=[vmem] * 5 + [spot] * len(sources),
-        out_specs=(vmem,) * 5 + (spot,) * len(wholes),
-        scratch_shapes=[pltpu.VMEM((8, 1024), f32), pltpu.VMEM((2, DK, DV), f32)]
+        in_specs=[spot] + [vmem] * 4 + [spot] * len(sources),
+        out_specs=(spot,) * (5 + len(wholes)),
+        scratch_shapes=[
+            pltpu.VMEM((tokens, 1536), bf16),
+            pltpu.VMEM((tokens, 512), bf16),
+            pltpu.VMEM((chunks, 2, DK, DV), f32),
+            pltpu.VMEM((chunks, 2, CHUNK, CHUNK), bf16),
+            pltpu.VMEM((chunks, 2, CHUNK, DV), f32),
+            pltpu.VMEM((tokens, 512), f32),
+            pltpu.SemaphoreType.DMA((chunks,)),
+            pltpu.SemaphoreType.DMA((5, chunks)),
+        ]
+        + [pltpu.VMEM((8, 1024), f32), pltpu.VMEM((2, DK, DV), f32)]
         + Reshard.scratch() * len(sources),
         compiler_params=pltpu.CompilerParams(
             collective_id=8 + layer, has_side_effects=True, vmem_limit_bytes=LIMIT
@@ -247,11 +279,25 @@
 
 
 def mixer_backward_kernel(
-    proj_ref, small_ref, taps_ref, heads_ref, gain_ref,
-    start_ref, inv_ref, pseudo_ref, mixed_ref, dgated_ref,
-    dproj_ref, dsmall_ref, gtaps_ref, gheads_ref,
-    halo, dstate,
+    small_ref, taps_ref, heads_ref, gain_ref, *refs
 ):
+    sources, refs = refs[:6], refs[6:]
+    dproj_hbm, dsmall_ref, gtaps_ref, gheads_ref, *refs = refs
+    held, refs = refs[:6], refs[6:]
+    proj_ref, start_ref, inv_ref, pseudo_ref, mixed_ref, dgated_ref = held
+    dproj_ref, load_sem, store_sem, halo, dstate = refs
+
+    def chunk_rows(c):
+        return pl.ds(pl.multiple_of(c * CHUNK, CHUNK), CHUNK)
+
+    def load(k, c):
+        at = c if k in (1, 2, 3) else chunk_rows(c)
+        return pltpu.make_async_copy(sources[k].at[at], held[k].at[at], load_sem.at[k, c])
+
+    def store(c):
+        rows = chunk_rows(c)
+        return pltpu.make_async_copy(dproj_ref.at[rows], dproj_hbm.at[rows], store_sem.at[c])
+
     halo[...] = jnp.zeros_like(halo)
     dstate[...] = jnp.zeros_like(dstate)
     gtaps_ref[...] = jnp.zeros_like(gtaps_ref)
@@ -261,9 +307,20 @@
     lane = col
     token = grid_of((CHUNK, 1), 0)
     chunks = proj_ref.shape[0] // CHUNK
+    for c in reversed(range(chunks)):
+        for k in range(6):
+            load(k, c).start()
+    load(0, chunks - 1).wait()
 
     def body(step, carry):
         c = chunks - 1 - step
+        for k in range(1, 6):
+            load(k, c).wait()
+
+        @pl.when(c > 0)
+        def _():
+            load(0, c - 1).wait()
+
         rows = pl.ds(pl.multiple_of(c * CHUNK, CHUNK), CHUNK)
         x = proj_ref[rows, 0:1024].astype(f32)
         before_rows = pl.ds(pl.multiple_of(jnp.maximum(c * CHUNK - 16, 0), 16), 16)
@@ -317,7 +374,7 @@
             kf = k.astype(f32)
             qf = q.astype(f32)
             d_pseudo = mb(mixing, d_mixed, TN) + tail * mm(k, d_end.astype(bf16))
-            d_right = mm3(inv, d_pseudo, TN)
+            d_right = mm2(inv, d_pseudo, TN)
             pair = jnp.concatenate([d_mixed, d_right], axis=0)
             reads = mm3(pair, jnp.concatenate([start, pseudo], axis=0), NT)
             read_q = reads[:CHUNK, :DK]
@@ -382,14 +439,20 @@
         )
         halo[...] = d_conv[:8]
         dproj_ref[rows, 0:1024] = d_x.astype(bf16)
+        store(c).start()
         return carry
 
     lax.fori_loop(0, chunks, body, 0)
+    for c in range(chunks):
+        store(c).wait()
 
 
 def mixer_backward(projected, small, taps, heads, gain, saved, d_gated):
     tokens = projected.shape[0]
     vmem = pl.BlockSpec(memory_space=pltpu.VMEM)
+    spot = pl.BlockSpec(memory_space=pl.ANY)
+    held = (projected, *saved, d_gated)
+    chunks = tokens // CHUNK
     return pl.pallas_call(
         mixer_backward_kernel,
         out_shape=(
@@ -398,12 +461,18 @@
             jax.ShapeDtypeStruct((8, 1024), f32),
             jax.ShapeDtypeStruct((8, DV), f32),
         ),
-        in_specs=[vmem] * 10,
-        out_specs=(vmem,) * 4,
-        scratch_shapes=[pltpu.VMEM((8, 1024), f32), pltpu.VMEM((2, DK, DV), f32)],
-        compiler_params=pltpu.CompilerParams(vmem_limit_bytes=48 << 20),
+        in_specs=[vmem] * 4 + [spot] * 6,
+        out_specs=(spot,) + (vmem,) * 3,
+        scratch_shapes=[pltpu.VMEM(array.shape, array.dtype) for array in held]
+        + [
+            pltpu.VMEM((tokens, 1536), bf16),
+            pltpu.SemaphoreType.DMA((6, chunks)),
+            pltpu.SemaphoreType.DMA((chunks,)),
+        ]
+        + [pltpu.VMEM((8, 1024), f32), pltpu.VMEM((2, DK, DV), f32)],
+        compiler_params=pltpu.CompilerParams(vmem_limit_bytes=LIMIT),
         name="mixer_backward",
-    )(projected, small, taps, heads, gain, *saved, d_gated)
+    )(small, taps, heads, gain, *held)
 
 
 SUB = 128
@@ -547,14 +616,14 @@
         yield gather.diagonal(i)
 
 
-def call(kernel, out_shape, inputs, scratch, collective, name, spots=()):
+def call(kernel, out_shape, inputs, scratch, collective, name, spots=(), out_spots=()):
     vmem = pl.BlockSpec(memory_space=pltpu.VMEM)
     spot = pl.BlockSpec(memory_space=pl.ANY)
     return pl.pallas_call(
         kernel,
         out_shape=out_shape,
         in_specs=[vmem] * len(inputs) + [spot] * len(spots),
-        out_specs=tuple(vmem for _ in out_shape),
+        out_specs=tuple(spot if k in out_spots else vmem for k in range(len(out_shape))),
         scratch_shapes=scratch,
         compiler_params=pltpu.CompilerParams(
             collective_id=collective, has_side_effects=True, vmem_limit_bytes=LIMIT
@@ -573,6 +642,20 @@
     copy = pltpu.make_async_copy(src, whole, sem)
     copy.start()
     return copy.wait
+
+
+class Outgoing:
+    def __init__(self, sems):
+        self.sems, self.copies = sems, []
+
+    def put(self, src, dst):
+        copy = pltpu.make_async_copy(src, dst, self.sems.at[len(self.copies)])
+        copy.start()
+        self.copies.append(copy)
+
+    def wait(self):
+        for copy in self.copies:
+            copy.wait()
 
 
 def load_down(src, whole, sem):
@@ -815,10 +898,11 @@
 
 def start_kernel(
     x_ref, pack_ref, win_ref,
-    normed_ref, proj_ref, small_ref, whole_ref,
+    normed_hbm, proj_hbm, small_ref, whole_hbm,
     gain0, gain1, gain2, gain3, taps0, taps1, ab0, ab1, out0, out1,
-    everyone, ab_rows, *scratch,
+    everyone, ab_rows, normed_ref, proj_ref, whole_ref, out_sems, *scratch,
 ):
+    outgoing = Outgoing(out_sems)
     size = x_ref.shape[0]
     y, c = place()
     me = 2 * y + c
@@ -884,11 +968,15 @@
         shard.forward(q)
     shard.wait()
     shard.wait_own()
+    outgoing.put(whole_ref, whole_hbm)
     for rows in in_order(gather):
         normed = normed_ref[rows, :]
         proj_ref[rows, :] = mm(normed, whole_ref[...]).astype(bf16)
         small_ref[rows, :] = mm(normed, ab0[...])
+        outgoing.put(proj_ref.at[rows], proj_hbm.at[rows])
+        outgoing.put(normed_ref.at[rows], normed_hbm.at[rows])
     gather.finish()
+    outgoing.wait()
     shard.finish()
     for d in (1, 2, 3):
         share(d).wait_send()
@@ -912,19 +1000,28 @@
             like(8, DV), like(8, DV),
         ),
         (x, pack),
-        [pltpu.VMEM((4, PACK_ROWS, 128), f32), pltpu.VMEM((128, width), f32)]
+        [
+            pltpu.VMEM((4, PACK_ROWS, 128), f32),
+            pltpu.VMEM((128, width), f32),
+            pltpu.VMEM((tokens, width), bf16),
+            pltpu.VMEM((tokens, 1536), bf16),
+            pltpu.VMEM((width, 1536), bf16),
+            dma((17,)),
+        ]
         + Reshard.scratch()
         + [dma((4,)), dma((4,))]
         + gather_sems(size),
         1,
         "start",
         (w_in,),
+        (0, 1, 3),
     )
 
 
 def project_kernel(count, res_ref, gain_ref, ab_ref, *refs):
     parts, refs = refs[:count], refs[count:]
-    normed_ref, proj_ref, small_ref, w_ref, loads, send, recv = refs
+    normed_hbm, proj_hbm, small_ref, w_ref, loads, normed_ref, proj_ref, out_sems, send, recv = refs
+    outgoing = Outgoing(out_sems)
     loaded = load_shard(in_parts(parts), w_ref, loads)
     size = res_ref.shape[0]
     y, c = place()
@@ -941,7 +1038,10 @@
         normed = normed_ref[rows, :]
         proj_ref[rows, :] = mm(normed, w_ref[...]).astype(bf16)
         small_ref[rows, :] = mm(normed, ab_ref[...])
+        outgoing.put(proj_ref.at[rows], proj_hbm.at[rows])
+        outgoing.put(normed_ref.at[rows], normed_hbm.at[rows])
     gather.finish()
+    outgoing.wait()
 
 
 def project(residual, gain, ab, weight):
@@ -951,10 +1051,18 @@
         partial(project_kernel, len(weight)),
         (like(tokens, width, dtype=bf16), like(tokens, 1536, dtype=bf16), like(tokens, 128)),
         (residual, gain, ab),
-        [pltpu.VMEM((width, 1536), bf16), pltpu.SemaphoreType.DMA((13,))] + gather_sems(size),
+        [
+            pltpu.VMEM((width, 1536), bf16),
+            pltpu.SemaphoreType.DMA((13,)),
+            pltpu.VMEM((tokens, width), bf16),
+            pltpu.VMEM((tokens, 1536), bf16),
+            pltpu.SemaphoreType.DMA((16,)),
+        ]
+        + gather_sems(size),
         6,
         "project",
         weight,
+        (0, 1),
     )
 
 
@@ -972,9 +1080,11 @@
 
 def ffn_forward_kernel(
     layer, gated_ref, res_ref, gain_ref, raw_ref, down_ref, ffn_ref, whole_ref,
-    mid_ref, normed_ref, up_ref, hidden_ref, out_ref,
-    wup_ref, wdown_ref, wout_ref, loads, shard_loads, *scratch,
+    mid_hbm, normed_hbm, up_hbm, hidden_hbm, out_ref,
+    wup_ref, wdown_ref, wout_ref, loads, shard_loads,
+    mid_ref, normed_ref, up_ref, hidden_ref, out_sems, *scratch,
 ):
+    outgoing = Outgoing(out_sems)
     loaded_out = load_whole(raw_ref.at[layer], wout_ref, loads.at[2])
     loaded = load_shard((ffn_ref.at[layer], up_lanes, whole_ref), wup_ref, shard_loads)
     loaded_down = load_down(down_ref.at[layer], wdown_ref, loads.at[1])
@@ -1013,8 +1123,12 @@
         up_ref[rows, :] = up.astype(bf16)
         hidden = swiglu(up).astype(bf16)
         hidden_ref[rows, :] = hidden
+        outgoing.put(normed_ref.at[rows], normed_hbm.at[rows])
+        outgoing.put(up_ref.at[rows], up_hbm.at[rows])
+        outgoing.put(hidden_ref.at[rows], hidden_hbm.at[rows])
         return mm(hidden, wdown_ref[...])
 
+    outgoing.put(mid_ref, mid_hbm)
     loaded()
     loaded_down()
     for i in range(count):
@@ -1032,6 +1146,7 @@
     first.finish()
     second.finish()
     gather.finish()
+    outgoing.wait()
 
 
 def ffn_forward(layer, gated, residual, gain, w_out, w_down, w_up):
@@ -1053,6 +1168,11 @@
             pltpu.VMEM((512, width), bf16),
             pltpu.SemaphoreType.DMA((3,)),
             pltpu.SemaphoreType.DMA((13,)),
+            pltpu.VMEM((size, width), f32),
+            pltpu.VMEM((tokens, width), bf16),
+            pltpu.VMEM((tokens, 1536), bf16),
+            pltpu.VMEM((tokens, 768), bf16),
+            pltpu.SemaphoreType.DMA((25,)),
         ]
         + Scatter.scratch(size, width)
         + Scatter.scratch(size, width)
@@ -1060,6 +1180,7 @@
         (2, 12)[layer],
         "ffn_forward",
         (w_out, w_down) + w_up,
+        (0, 1, 2, 3),
     )
 
 
@@ -1128,12 +1249,15 @@
 
 
 def ffn_backward_kernel(
-    layer, dres_ref, up_ref, hidden_ref, normed_ref, mid_ref, gain_ref, gated_ref,
+    layer, dres_ref, gain_ref, up_hbm, hidden_hbm, normed_hbm, mid_hbm, gated_hbm,
     raw_ref, down_ref, ffn_ref, whole_ref,
-    dmid_ref, dgated_ref, ggain_ref, keep_ref, send_ref,
-    wup_ref, wdown_ref, wout_ref, loads, shard_loads, ddown_ref, dup_ref, dbranch_ref, staged, *scratch,
+    dmid_ref, dgated_hbm, ggain_ref, keep_hbm, send_hbm,
+    wup_ref, wdown_ref, wout_ref, loads, shard_loads, ddown_ref, dup_ref, dbranch_ref, staged,
+    up_ref, hidden_ref, normed_ref, mid_ref, gated_ref, dgated_ref, keep_ref, send_ref,
+    late_sems, out_sems, *scratch,
 ):
     buf_ref = Owners(keep_ref, send_ref)
+    outgoing = Outgoing(out_sems)
     loaded_out = load_whole(raw_ref.at[layer], wout_ref, loads.at[2])
     loaded = load_shard((ffn_ref.at[layer], up_lanes, whole_ref), wup_ref, shard_loads)
     loaded_down = load_down(down_ref.at[layer], wdown_ref, loads.at[1])
@@ -1144,6 +1268,18 @@
     first = Gather(ddown_ref, *scratch[:2], size)
     second = Gather(dbranch_ref, *scratch[2:4], size)
     scatter = Scatter(*scratch[4:], size)
+    late = [
+        load_whole(src, dst, late_sems.at[k])
+        for k, (src, dst) in enumerate(
+            (
+                (up_hbm, up_ref),
+                (hidden_hbm, hidden_ref),
+                (mid_hbm, mid_ref),
+                (normed_hbm, normed_ref),
+                (gated_hbm, gated_ref),
+            )
+        )
+    ]
     for i in range(count):
         ddown_ref[first.own(i), :] = dres_ref[i * SUB : (i + 1) * SUB, :].astype(bf16)
         if i == 0:
@@ -1158,6 +1294,7 @@
 
     loaded()
     loaded_down()
+    late[0]()
     for i in range(count):
         scatter.hold(1, i, feed(first.own(i)))
     for i in range(count):
@@ -1167,10 +1304,12 @@
         scatter.hold(0, i, feed(near))
         scatter.give(0, i, feed(first.diagonal(i)))
         scatter.relay(i)
+    late[1]()
     for m in range(6):
         value = mm(hidden_ref[:, 128 * m : 128 * m + 128], ddown_ref[...], TN)
         store_columns(buf_ref, value, pl.multiple_of(DOWN_AT + 128 * m - 64 * c, 64))
     ggain_ref[...] = jnp.zeros_like(ggain_ref)
+    late[2]()
     for i in range(count):
         rows = slice(i * SUB, (i + 1) * SUB)
         d_norm, g_gain = normalise_back(mid_ref[rows, :], gain_ref[...], scatter.total(i))
@@ -1179,19 +1318,29 @@
         ggain_ref[0:1, :] += g_gain
         dbranch_ref[second.own(i), :] = d_mid.astype(bf16)
         second.start(i)
+    late[3]()
     for d in range(4):
         lanes = pl.ds(pl.multiple_of(relative(y, c, d) * 256, 256), 256)
         staged[...] = mm(normed_ref[:, lanes], dup_ref[...], TN)
         store_up(buf_ref, staged, d, c)
+    for keep, hbm in ((keep_ref, keep_hbm), (send_ref, send_hbm)):
+        rows = pl.ds(0, OUT_AT)
+        outgoing.put(keep.at[:, rows], hbm.at[:, rows])
     loaded_out()
     for rows in in_order(second):
         dgated_ref[rows, :] = mm(dbranch_ref[rows, :], wout_ref[...], NT).astype(bf16)
+    outgoing.put(dgated_ref, dgated_hbm)
+    late[4]()
     for m in range(4):
         value = mm(gated_ref[:, 128 * m : 128 * m + 128], dbranch_ref[...], TN)
         store_columns(buf_ref, value, OUT_AT + 128 * m)
+    for keep, hbm in ((keep_ref, keep_hbm), (send_ref, send_hbm)):
+        rows = pl.ds(OUT_AT, FFN_ROWS - OUT_AT)
+        outgoing.put(keep.at[:, rows], hbm.at[:, rows])
     first.finish()
     second.finish()
     scatter.finish()
+    outgoing.wait()
 
 
 def ffn_backward(layer, d_res, up, hidden, normed, mid, gain, gated, w_out, w_down, w_up):
@@ -1206,7 +1355,7 @@
             like(4, FFN_ROWS, 128, dtype=bf16),
             like(4, FFN_ROWS, 128, dtype=bf16),
         ),
-        (d_res, up, hidden, normed, mid, gain, gated),
+        (d_res, gain),
         [
             pltpu.VMEM((width, 1536), bf16),
             pltpu.VMEM((768, width), bf16),
@@ -1218,23 +1367,35 @@
             pltpu.VMEM((tokens, width), bf16),
             pltpu.VMEM((256, 1536), f32),
         ]
+        + [pltpu.VMEM(array.shape, array.dtype) for array in (up, hidden, normed, mid, gated, gated)]
+        + [pltpu.VMEM((4, FFN_ROWS, 128), bf16)] * 2
+        + [pltpu.SemaphoreType.DMA((5,)), pltpu.SemaphoreType.DMA((5,))]
         + gather_sems(size)
         + gather_sems(size)
         + Scatter.scratch(size, width),
         (3, 13)[layer],
         "ffn_backward",
-        (w_out, w_down) + w_up,
+        (up, hidden, normed, mid, gated, w_out, w_down) + w_up,
+        (1, 3, 4),
     )
 
 
 def project_backward_kernel(
-    parts, dproj_ref, dsmall_ref, ab_ref, normed_ref, res_ref, gain_ref, dmid_ref,
-    gtwo_ref, gtaps_ref, gheads_ref, *refs
+    parts, dproj_ref, dsmall_ref, ab_ref, gain_ref, gtwo_ref, gtaps_ref, gheads_ref, *refs
 ):
+    normed_hbm, res_hbm, dmid_hbm, *refs = refs
     parts, refs = refs[:parts], refs[parts:]
-    dres_ref, keep_ref, send_ref, w_ref, loads, table, *scratch = refs
+    dres_ref, keep_hbm, send_hbm, w_ref, loads, table, *refs = refs
+    normed_ref, res_ref, dmid_ref, keep_ref, send_ref, late_sems, out_sems, *scratch = refs
     buf_ref = Owners(keep_ref, send_ref)
+    outgoing = Outgoing(out_sems)
     loaded = load_shard(in_parts(parts), w_ref, loads)
+    late = [
+        load_whole(src, dst, late_sems.at[k])
+        for k, (src, dst) in enumerate(
+            ((normed_hbm, normed_ref), (res_hbm, res_ref), (dmid_hbm, dmid_ref))
+        )
+    ]
     size = res_ref.shape[0]
     count = size // SUB
     y, c = place()
@@ -1260,8 +1421,12 @@
             scatter.hold(part, i, back(shard_rows(yy, c, i, size)))
             if part == 0:
                 scatter.relay(i)
+    late[0]()
     for d in range(4):
         weight_grad(d)
+    for keep, hbm in ((keep_ref, keep_hbm), (send_ref, send_hbm)):
+        rows = pl.ds(0, SMALL_AT)
+        outgoing.put(keep.at[:, rows], hbm.at[:, rows])
     ab_grad = mm(dsmall_ref[...], normed_ref[...], TN)
     table[...] = jnp.zeros_like(table)
     for k in range(8):
@@ -1275,6 +1440,8 @@
     table[82:83, :] = gheads_ref[1:2, 0:128]
     table[83:84, :] = gheads_ref[2:3, 0:128]
     gain_sum = jnp.zeros((1, res_ref.shape[1]), f32)
+    late[1]()
+    late[2]()
     for i in range(count):
         rows = slice(i * SUB, (i + 1) * SUB)
         d_norm, g_gain = normalise_back(res_ref[rows, :], gain_ref[...], scatter.total(i))
@@ -1288,7 +1455,11 @@
             ref[SMALL_AT:IN_ROWS, :] = table[16 * r : 16 * r + 16, :].astype(bf16)
 
         buf_ref.put(r, store)
+    for keep, hbm in ((keep_ref, keep_hbm), (send_ref, send_hbm)):
+        rows = pl.ds(SMALL_AT, IN_ROWS - SMALL_AT)
+        outgoing.put(keep.at[:, rows], hbm.at[:, rows])
     scatter.finish()
+    outgoing.wait()
 
 
 def project_backward(d_proj, d_small, weight, ab, normed, residual, gain, d_mid, g_two, g_taps, g_heads):
@@ -1296,21 +1467,26 @@
     return call(
         partial(project_backward_kernel, len(weight)),
         (like(size, width),) + (like(4, IN_ROWS, 128, dtype=bf16),) * 2,
-        (d_proj, d_small, ab, normed, residual, gain, d_mid, g_two, g_taps, g_heads),
+        (d_proj, d_small, ab, gain, g_two, g_taps, g_heads),
         [
             pltpu.VMEM((width, 1536), bf16),
             pltpu.SemaphoreType.DMA((13,)),
             pltpu.VMEM((128, 128), f32),
         ]
+        + [pltpu.VMEM(array.shape, array.dtype) for array in (normed, residual, d_mid)]
+        + [pltpu.VMEM((4, IN_ROWS, 128), bf16)] * 2
+        + [pltpu.SemaphoreType.DMA((3,)), pltpu.SemaphoreType.DMA((4,))]
         + Scatter.scratch(size, width),
         4 if len(weight) == 1 else 7,
         "project_backward",
-        weight,
+        (normed, residual, d_mid) + tuple(weight),
+        (1, 2),
     )
 
 
 def assemble_kernel(
-    f1, f2, f3, f4, down_ref, out_ref, up_ref, in_ref, table_ref,
+    f1, f2, f3, f4, last_ref, grad_ref,
+    down_ref, out_ref, up_ref, in_ref, table_ref, block_ref, input_ref,
     p1, p2, p3, p4, down, out, up, whole, loads, stores,
 ):
     y, c = place()
@@ -1320,6 +1496,8 @@
     ]
     for copy in copies:
         copy.start()
+    block_ref[...] = last_ref[...].astype(bf16)
+    input_ref[...] = grad_ref[...].astype(bf16)
     left = grid_of((32, 128), 1) < 64
 
     def ffn(layer, pieces):
@@ -1400,20 +1578,23 @@
     return 2 * (y + sy - 2 * y * sy) + c + sc - 2 * c * sc
 
 
-def assemble(finals):
+def assemble(finals, last, grad):
     spot = pl.BlockSpec(memory_space=pl.ANY)
+    vmem = pl.BlockSpec(memory_space=pltpu.VMEM)
     shapes = [(LAYERS, 704, 1024), (LAYERS, 512, 1024), (LAYERS, 256, 2 * FF), (LAYERS, 256, CH + HV)]
     return pl.pallas_call(
         assemble_kernel,
-        out_shape=tuple(like(*shape) for shape in shapes) + (like(4, LAYERS, 128, 128),),
-        in_specs=[spot] * 4,
-        out_specs=(spot,) * 4 + (pl.BlockSpec(memory_space=pltpu.VMEM),),
+        out_shape=tuple(like(*shape) for shape in shapes)
+        + (like(4, LAYERS, 128, 128),)
+        + (like(*last.shape, dtype=bf16),) * 2,
+        in_specs=[spot] * 4 + [vmem] * 2,
+        out_specs=(spot,) * 4 + (vmem,) * 3,
         scratch_shapes=[pltpu.VMEM(final.shape, bf16) for final in finals]
         + [pltpu.VMEM(shape, f32) for shape in shapes]
         + [pltpu.SemaphoreType.DMA((4,)), pltpu.SemaphoreType.DMA((2, 4))],
         compiler_params=pltpu.CompilerParams(vmem_limit_bytes=LIMIT),
         name="assemble",
-    )(*finals)
+    )(*finals, last, grad)
 
 
 FFN_MOVE, IN_MOVE = (UP_AT, 352), (0, 384)
@@ -1531,15 +1712,13 @@
             def _():
                 onward(self.move(k, z + k, 1, which))
 
-    def relay(self, k):
-        for which in range(2 if self.x_first else 1):
-
-            def arrive(step, source, kind):
-                self.move(abs(step) - 1, source, kind, which).wait_recv()
-                if not self.x_first:
-                    self.x_move(step, source).start()
-
-            self.passes(k, which, arrive, lambda copy: copy.start())
+    def relay(self, k, which=0):
+        def arrive(step, source, kind):
+            self.move(abs(step) - 1, source, kind, which).wait_recv()
+            if not self.x_first:
+                self.x_move(step, source).start()
+
+        self.passes(k, which, arrive, lambda copy: copy.start())
 
     def finish(self):
         for which in range(2 if self.x_first else 1):
@@ -1634,8 +1813,8 @@
 
 
 def finish_kernel(
-    p1, p2, s3, k4, b4, f1, f2, f3, f4,
-    q1, q2, q3, q4, e1, e2, e3, e4, v3, r3, l3, v4, x4, r4, l4,
+    p1, p2, k3, a3, k4, b4, f1, f2, f3, f4,
+    q1, q2, q3, q4, e1, e2, e3, e4, v3, x3, r3, l3, v4, x4, r4, l4,
     send, recv, local, send3, recv3, send4, recv4, send5, recv5, loads,
 ):
     rank = lax.axis_index("rep")
@@ -1644,8 +1823,9 @@
     loaded = [
         pltpu.make_async_copy(p1, q1, loads.at[0]),
         pltpu.make_async_copy(p2, q2, loads.at[1]),
-        pltpu.make_async_copy(s3, v3, loads.at[2]),
+        pltpu.make_async_copy(k3, v3, loads.at[2]),
         pltpu.make_async_copy(k4, v4, loads.at[3]),
+        pltpu.make_async_copy(a3, x3, loads.at[4]),
     ]
     for load in loaded:
         load.start()
@@ -1683,56 +1863,67 @@
     for o in (3, 0, 2, 1):
         halves(o).start()
     sems = (send, recv, local)
+
+    def merge(*owners):
+        for o in owners:
+            add_into(v3.at[o], v3.at[o], x3.at[o])
+
+    def arrive(*owners):
+        for o in owners:
+            halves(o).wait_recv()
+            add_into(v4.at[o], v4.at[o], x4.at[o])
+
     g1 = Group(0, q1, e1, f1, FFN_MOVE, sems)
-    g2 = Group(1, q2, e2, f2, IN_MOVE, sems, x_first=True)
+    g2 = Group(1, q2, e2, f2, IN_MOVE, sems)
     g3 = Group(2, q3, e3, f3, FFN_MOVE, sems)
     g4 = Group(3, q4, e4, f4, IN_MOVE, sems)
     line3 = Line(v3, r3, l3, send3, recv3)
     line4 = Line(v4, r4, l4, send4, recv4)
     loaded[0].wait()
     g1.start_swap()
-    loaded[2].wait()
-    line3.start_edge(0)
     loaded[1].wait()
     g2.start_swap()
     g1.wait_swap()
     g1.begin()
-    line3.inner(0)
-    line3.start_edge(1)
+    loaded[3].wait()
+    arrive(3, 0)
+    loaded[2].wait()
+    loaded[4].wait()
+    merge(3, 0)
+    line3.start_edge(0)
     g2.wait_swap()
     g2.begin()
-    loaded[3].wait()
-    for o in (3, 0, 2, 1):
-        halves(o).wait_recv()
-        add_into(v4.at[o], v4.at[o], x4.at[o])
+    merge(2, 1)
+    line3.start_edge(1)
+    g1.relay(1)
+    line3.inner(0)
+    line3.inner(1)
     line4.start_edge(0)
-    line3.inner(1)
+    g2.relay(1)
+    g1.relay(2)
     line3.start_edge(2)
-    g1.relay(1)
+    arrive(2, 1)
+    line3.total(q3)
+    g3.start_swap()
+    g2.relay(2)
+    g3.wait_swap()
+    g3.begin()
     line4.inner(0)
     line4.start_edge(1)
-    line3.total(q3)
-    g3.start_swap()
     line4.inner(1)
     line4.start_edge(2)
-    g1.relay(2)
-    g3.wait_swap()
-    g3.begin()
+    g2.relay(3)
+    g1.relay(3)
+    g3.relay(1)
     line4.total(q4)
     g4.start_swap()
-    g2.begin_other()
-    g1.relay(3)
     g4.wait_swap()
     g4.begin()
-    g2.relay(1)
-    g3.relay(1)
+    g3.relay(2)
     g4.relay(1)
-    g2.relay(2)
-    g3.relay(2)
     g4.relay(2)
     g3.relay(3)
     g4.relay(3)
-    g2.relay(3)
     for group in (g1, g2, g3, g4):
         group.finish()
     line3.finish()
@@ -1741,7 +1932,7 @@
         halves(o).wait_send()
 
 
-def finish_reduction(p1, p2, s3, k4, b4):
+def finish_reduction(p1, p2, k3, a3, k4, b4):
     spot = pl.BlockSpec(memory_space=pl.ANY)
     big, small = p1.shape, p2.shape
     wide = (GATHERED_ROWS, 128)
@@ -1749,23 +1940,23 @@
     return pl.pallas_call(
         finish_kernel,
         out_shape=tuple(like(8, *shape, dtype=bf16) for shape in (big, wide, big, wide)),
-        in_specs=[spot] * 5,
+        in_specs=[spot] * 6,
         out_specs=(spot,) * 4,
         scratch_shapes=[
             pltpu.VMEM(shape, bf16)
             for shape in [big, small] * 2 + [big, wide] * 2
-            + [(4,) + big] * 3
+            + [(4,) + big] * 4
             + [(4,) + small] * 4
         ]
         + [dma((5, 24)), dma((5, 24)), dma((4,))]
         + [dma((2, 4))] * 4
-        + [dma((4,)), dma((4,)), dma((4,))],
+        + [dma((4,)), dma((4,)), dma((5,))],
         compiler_params=pltpu.CompilerParams(
             collective_id=5, has_side_effects=True, vmem_limit_bytes=LIMIT
         ),
         cost_estimate=pl.CostEstimate(flops=1000, bytes_accessed=1000, transcendentals=0),
         name="finish_reduction",
-    )(p1, p2, s3, k4, b4)
+    )(p1, p2, k3, a3, k4, b4)
 
 
 def swap_route(bit, count):
@@ -1820,10 +2011,10 @@
     return pair.reshape((8,) + piece.shape)
 
 
-def finish_all(piece1, piece2, summed3, keep4, send4, replicas):
+def finish_all(piece1, piece2, keep3, arrived3, keep4, send4, replicas):
     if replicas == 8:
-        return finish_reduction(piece1, piece2, summed3, keep4, send4)
-    piece3 = reduce_z(summed3, replicas)
+        return finish_reduction(piece1, piece2, keep3, arrived3, keep4, send4)
+    piece3 = reduce_z(add_arrived(keep3, arrived3), replicas)
     piece4 = reduce_z(add_arrived(keep4, swap_x(send4, replicas)), replicas)
     return [
         spread(exchange(piece, *move), replicas)
@@ -1897,7 +2088,6 @@
         )
         kept.append((residual, normed, projected, small, gated, saved, mid, normed_two, up, hidden))
         residual = residual_out
-    block_output = residual.astype(bf16)[None]
 
     d_residual = cotangent[0].astype(f32)
 
@@ -1937,12 +2127,12 @@
     mixed = mixer_part(0, d_gated)
     d_residual, keep4, send4 = project_part(0, d_mid, g_gain_two, mixed)
     d_residual, arrived3 = tie(d_residual, arrived3)
-    summed3 = add_arrived(keep3, arrived3)
-    final1, final2, final3, final4 = finish_all(piece1, piece2, summed3, keep4, send4, replicas)
-    down_grads, out_grads, up_grads, w_in_grads, everyone = assemble(
-        (final1, final2, final3, final4)
+    final1, final2, final3, final4 = finish_all(piece1, piece2, keep3, arrived3, keep4, send4, replicas)
+    finals = (final1, final2, final3, final4)
+    down_grads, out_grads, up_grads, w_in_grads, everyone, *ends = assemble(
+        finals, residual, d_residual
     )
-    input_grad = d_residual.astype(bf16)[None]
+    block_output, input_grad = (end[None] for end in ends)
 
     tables = lax.dynamic_index_in_dim(everyone, mine, 0, keepdims=False)
     sums = jnp.sum(everyone[:, :, 64:82], axis=0)

time: 795 us -> 725 us (0.912)
  Pallas kernels: 734 us -> 673 us
  other arithmetic: 17.1 us -> 8.82 us
    pallas_call x1, Pallas kernels: 270 us -> 230 us  [finish_reduction(): pl.pallas_call(finish_kernel, out_shape=tuple((like(8, *shape, dtype=bf16...]
    pallas_call x8, Pallas kernels: 298 us -> 286 us  [call(): pl.pallas_call(kernel, out_shape=out_shape, in_specs=[vmem] * len(inputs)...]
    pallas_call x2, Pallas kernels: 80.5 us -> 69 us  [mixer_forward(): pl.pallas_call(partial(mixer_forward_kernel, layer), out_shape=(jax.Shape...]
  transfers between devices with their start and end apart: 6 -> 6, of which waited for: 1 -> 3; matrix products, arithmetic and copies ran while one was open for 2% -> 0% of each run, Pallas kernels for 27% -> 29%
where the time goes in v4:
time: 725 us; the launch traced here: 718 us
  Pallas kernels  673 us (93%)
  between operations  14.2 us (2%)
  local copies, waits for them, and re-layouts  10.5 us (1%)
  other arithmetic  8.82 us (1%)
  waiting for transfers between devices  7.85 us (1%)
    pallas_call x8, Pallas kernels, call(): pl.pallas_call(kernel, out_shape=out_shape, in_specs=[vmem] * len(inputs)...  286 us
    pallas_call x1, Pallas kernels, finish_reduction(): pl.pallas_call(finish_kernel, out_shape=tuple((like(8, *shape, dtype=bf16...  230 us
    pallas_call x2, Pallas kernels, mixer_backward(): pl.pallas_call(mixer_backward_kernel, out_shape=(jax.ShapeDtypeStruct((to...  69.9 us
    pallas_call x2, Pallas kernels, mixer_forward(): pl.pallas_call(partial(mixer_forward_kernel, layer), out_shape=(jax.Shape...  69 us
    pallas_call x1, Pallas kernels, assemble(): pl.pallas_call(assemble_kernel, out_shape=tuple((like(*shape) for shape i...  18.5 us
  transfers between devices with their start and end apart: 6, of which 3 were waited for; matrix products, arithmetic and copies ran while one was open for 0% of the time, Pallas kernels for 29%

profile of v4, /device:TPU:0, one launch (start us, length us, event | category | flops | bytes accessed | tf_op | source)
XLA Modules:
  0.0 718.0 jit_solution(14258040515643264921)
XLA Ops:
  7.2 0.7 reshape.65
  7.9 0.7 reshape.66
  8.6 0.7 reshape.67
  9.4 0.7 reshape.68
  10.8 0.7 fusion.19
  11.6 0.7 fusion.18
  12.3 41.4 %start.1 = (bf16[1024,1024]{1,0:T(8,128)(2,1)}, bf16[1024,1536]{1,0:T(8,128)(2,1)}, f32[1024,128]{1,0:T(8,128)}, bf16[1024,1536]{1,0:T(8,128)(2,1)}, f32[1,1024]...) custom-call(bf16[256,1024]{1,0:T(8,128)(2,1)} %bitcast.42, ...), custom_call_target="tpu_custom_call" | custom-call | flops 1000 | bytes 1000 | tf_op jit(solution)/shard_map/start/pallas_call | solution.py:622
  54.3 35.1 %mixer_forward.2 = (bf16[1024,512]{1,0:T(8,128)(2,1)}, f32[8,2,128,256]{3,2,1,0:T(8,128)}, bf16[8,2,128,128]{3,2,1,0:T(8,128)(2,1)}, f32[8,2,128,256]{3,2,1,0:T(...) custom-call(bf16[1024,1536]{1,0:T(8,128)(2,1)} %get-tuple-element.95, ...), custom_call_target="tpu_custom_call" | custom-call | tf_op jit(solution)/shard_map/mixer_forward/pallas_call | solution.py:250
  90.0 1.1 bitcast_convert_fusion.1.res_ref.refs_1_
  91.1 42.3 %ffn_forward.2 = (f32[256,1024]{1,0:T(8,128)}, bf16[1024,1024]{1,0:T(8,128)(2,1)}, bf16[1024,1536]{1,0:T(8,128)(2,1)}, bf16[1024,768]{1,0:T(8,128)(2,1)}, f32[256,1024]{1,0:T(8,128)}) custom-call(bf16[1024,512]{1,0:T(8,128)(2,1)} %get-tuple-element.99.gated_ref.gated_hbm, f32[256,1024]{1,0:T(8,128)} %bitcast_convert_fusion.1.res_ref.refs_1_, ...), custom_call_target="tpu_custom_call" | custom-call | flops 1000 | bytes 1000 | tf_op jit(solution)/shard_map/ffn_forward/pallas_call | solution.py:622
  133.4 1.1 bitcast_convert_fusion.dres_ref
  134.5 18.3 %project.1 = (bf16[1024,1024]{1,0:T(8,128)(2,1)}, bf16[1024,1536]{1,0:T(8,128)(2,1)}, f32[1024,128]{1,0:T(8,128)}) custom-call(f32[256,1024]{1,0:T(8,128)} %get-tuple-element.102.res_ref.refs_1_, f32[1,1024]{1,0:T(1,128)} %get-tuple-element.103.gain_ref, bf16[1024,128]{1,0:T(8,128)(2,1)} %get-tuple-element.104.ab_ref, bf16[2,256,6144]{2,1,0:T(8,128)(2,1)} %refs_3_.1, ...), custom_call_target="tpu_custom_call" | custom-call | flops 1000 | bytes 1000 | tf_op jit(solution)/shard_map/project/pallas_call | solution.py:622
  152.9 33.8 %mixer_forward.3 = (bf16[1024,512]{1,0:T(8,128)(2,1)}, f32[8,2,128,256]{3,2,1,0:T(8,128)}, bf16[8,2,128,128]{3,2,1,0:T(8,128)(2,1)}, f32[8,2,128,256]{3,2,1,0:T(...) custom-call(bf16[1024,1536]{1,0:T(8,128)(2,1)} %get-tuple-element.110.proj_hbm.refs_0_, ...), custom_call_target="tpu_custom_call" | custom-call | tf_op jit(solution)/shard_map/mixer_forward/pallas_call | solution.py:250
  186.7 42.5 %ffn_forward.3 = (f32[256,1024]{1,0:T(8,128)}, bf16[1024,1024]{1,0:T(8,128)(2,1)}, bf16[1024,1536]{1,0:T(8,128)(2,1)}, bf16[1024,768]{1,0:T(8,128)(2,1)}, f32[256,1024]{1,0:T(8,128)}) custom-call(bf16[1024,512]{1,0:T(8,128)(2,1)} %get-tuple-element.116.gated_ref.gated_hbm, f32[256,1024]{1,0:T(8,128)} %get-tuple-element.102.res_ref.refs_1_, ...), custom_call_target="tpu_custom_call" | custom-call | flops 1000 | bytes 1000 | tf_op jit(solution)/shard_map/ffn_forward/pallas_call | solution.py:622
  229.2 47.0 %ffn_backward.2 = (f32[256,1024]{1,0:T(8,128)}, bf16[1024,512]{1,0:T(8,128)(2,1)}, f32[8,1024]{1,0:T(8,128)}, bf16[4,2624,128]{2,1,0:T(8,128)(2,1)}, bf16[4,2624,128]{2,1,0:T(8,128)(2,1)}) custom-call(f32[256,1024]{1,0:T(8,128)} %bitcast_convert_fusion.dres_ref, f32[1,1024]{1,0:T(1,128)} %get-tuple-element.115.gain_ref, ...), custom_call_target="tpu_custom_call" | custom-call | flops 1000 | bytes 1000 | tf_op jit(solution)/shard_map/ffn_backward/pallas_call | solution.py:622
  276.1 0.7 collective-permute-start
  276.8 34.9 %mixer_backward.2 = (bf16[1024,1536]{1,0:T(8,128)(2,1)}, bf16[1024,128]{1,0:T(8,128)(2,1)}, f32[8,1024]{1,0:T(8,128)}, f32[8,256]{1,0:T(8,128)}) custom-call(f32[1024,128]{1,0:T(8,128)} %get-tuple-element.107.small_ref, f32[8,1024]{1,0:T(8,128)} %get-tuple-element.108.taps_ref, f32[8,128]{1,0:T(8,128)} %get-tuple-element.213.heads_ref, ...), custom_call_target="tpu_custom_call" | custom-call | tf_op jit(solution)/shard_map/mixer_backward/pallas_call | solution.py:456
  311.8 23.7 %project_backward.2 = (f32[256,1024]{1,0:T(8,128)}, bf16[4,1552,128]{2,1,0:T(8,128)(2,1)}, bf16[4,1552,128]{2,1,0:T(8,128)(2,1)}) custom-call(bf16[1024,1536]{1,0:T(8,128)(2,1)} %get-tuple-element.123.dproj_ref, bf16[1024,128]{1,0:T(8,128)(2,1)} %get-tuple-element.124.dsmall_ref, bf16[1024,128]{1,0:T(8,128)(2,1)} %get-tuple-element.104.ab_ref, ...), custom_call_target="tpu_custom_call" | custom-call | flops 1000 | bytes 1000 | tf_op jit(solution)/shard_map/project_backward/pallas_call | solution.py:622
  335.5 1.8 collective-permute-done
  337.4 2.2 add_convert_fusion
  340.3 47.0 %ffn_backward.3 = (f32[256,1024]{1,0:T(8,128)}, bf16[1024,512]{1,0:T(8,128)(2,1)}, f32[8,1024]{1,0:T(8,128)}, bf16[4,2624,128]{2,1,0:T(8,128)(2,1)}, bf16[4,2624,128]{2,1,0:T(8,128)(2,1)}) custom-call(f32[256,1024]{1,0:T(8,128)} %get-tuple-element.132.dres_ref, f32[1,1024]{1,0:T(1,128)} %get-tuple-element.100.gain_ref, ...), custom_call_target="tpu_custom_call" | custom-call | flops 1000 | bytes 1000 | tf_op jit(solution)/shard_map/ffn_backward/pallas_call | solution.py:622
  387.4 5.8 reduce-scatter.3.cloned.1.call-done
  393.2 1.6 add_convert_fusion.1
  394.8 1.6 collective-permute-start.2
  396.3 34.9 %mixer_backward.3 = (bf16[1024,1536]{1,0:T(8,128)(2,1)}, bf16[1024,128]{1,0:T(8,128)(2,1)}, f32[8,1024]{1,0:T(8,128)}, f32[8,256]{1,0:T(8,128)}) custom-call(f32[1024,128]{1,0:T(8,128)} %get-tuple-element.96.small_ref, f32[8,1024]{1,0:T(8,128)} %get-tuple-element.97.taps_ref, f32[8,128]{1,0:T(8,128)} %get-tuple-element.212.heads_ref, ...), custom_call_target="tpu_custom_call" | custom-call | tf_op jit(solution)/shard_map/mixer_backward/pallas_call | solution.py:456
  431.3 23.5 %project_backward.3 = (f32[256,1024]{1,0:T(8,128)}, bf16[4,1552,128]{2,1,0:T(8,128)(2,1)}, bf16[4,1552,128]{2,1,0:T(8,128)(2,1)}) custom-call(bf16[1024,1536]{1,0:T(8,128)(2,1)} %get-tuple-element.150.dproj_ref, bf16[1024,128]{1,0:T(8,128)(2,1)} %get-tuple-element.151.dsmall_ref, bf16[1024,128]{1,0:T(8,128)(2,1)} %get-tuple-element.152.ab_ref, ...), custom_call_target="tpu_custom_call" | custom-call | flops 1000 | bytes 1000 | tf_op jit(solution)/shard_map/project_backward/pallas_call | solution.py:622
  454.9 1.5 copy-done
  456.4 230.0 %finish_reduction.1 = (bf16[8,2624,128]{2,1,0:T(8,128)(2,1)}, bf16[8,1600,128]{2,1,0:T(8,128)(2,1)}, bf16[8,2624,128]{2,1,0:T(8,128)(2,1)}, bf16[8,1600,128]{2,1,0:T(8,128)(2,1)}) custom-call(bf16[2624,128]{1,0:T(8,128)(2,1)} %bitcast.43, bf16[1552,128]{1,0:T(8,128)(2,1)} %bitcast.44, bf16[4,2624,128]{2,1,0:T(8,128)(2,1)} %get-tuple-element.144.k3, ...), custom_call_target="tpu_custom_call" | custom-call | flops 1000 | bytes 1000 | tf_op jit(solution)/shard_map/finish_reduction/pallas_call | solution.py:1940
  686.5 18.5 %assemble.1 = (f32[2,704,1024]{2,1,0:T(8,128)}, f32[2,512,1024]{2,1,0:T(8,128)}, f32[2,256,5632]{2,1,0:T(8,128)}, f32[2,256,6144]{2,1,0:T(8,128)}, f32[4,2,128,1...) custom-call(bf16[8,2624,128]{2,1,0:T(8,128)(2,1)} %get-tuple-element.165.f1, ...), custom_call_target="tpu_custom_call" | custom-call | tf_op jit(solution)/shard_map/assemble/pallas_call | solution.py:1585
  705.0 0.9 slice_reduce_fusion
  705.9 1.0 fusion.16
  708.4 0.9 dynamic-slice_bitcast_fusion
  (43 shorter events, 6.2 us)
Async XLA Ops:
  7.2 127.4 %all-gather.3.cloned.1.call-start = ((), (), s32[]{:S(2)}) async-start(), calls=%async_computation.4 | async-start | bytes 1966080 | tf_op jit(solution)/shard_map/all_gather | solution.py:2082
  54.3 35.7 %copy-start.2 = (bf16[1,256,1024]{2,1,0:T(8,128)(2,1)S(1)}, bf16[1,256,1024]{2,1,0:T(8,128)(2,1)}, u32[]{:S(2)}) copy-start(bf16[1,256,1024]{2,1,0:T(8,128)(2,1)} %param.12) | copy-start | bytes 1572868
  89.5 303.7 %reduce-scatter.3.cloned.1.call-start = ((), (), s32[]{:S(2)}) async-start(), calls=%async_computation.2 | async-start | bytes 3358720 | tf_op jit(solution)/shard_map/reduce_scatter | solution.py:1981
  91.1 42.3 %copy-start.4 = (bf16[1,256,1024]{2,1,0:T(8,128)(2,1)S(1)}, bf16[1,256,1024]{2,1,0:T(8,128)(2,1)}, u32[]{:S(2)}) copy-start(bf16[1,256,1024]{2,1,0:T(8,128)(2,1)} %param.23) | copy-start | bytes 1572868
  276.1 61.2 %collective-permute-start = (bf16[4,2624,128]{2,1,0:T(8,128)(2,1)}, bf16[4,2624,128]{2,1,0:T(8,128)(2,1)S(1)}, u32[]{:S(2)}, u32[]{:S(2)}) collective-permute-start(bf16[4,2624,128]{2,1,0:T(8,128)(2,1)} %get-tuple-element.131), channel_id=1, source_target_pairs={{0,4},{4,0},{8,12},{12,8},{16,20},{20,16},{24,28},{28,24},{1,5},{5... | collective-permute-start | bytes 8060936 | tf_op jit(solution)/shard_map/ppermute | solution.py:1973
  311.8 25.6 %copy-start.1 = (bf16[4,2624,128]{2,1,0:T(8,128)(2,1)S(1)}, bf16[4,2624,128]{2,1,0:T(8,128)(2,1)}, u32[]{:S(2)}) copy-start(bf16[4,2624,128]{2,1,0:T(8,128)(2,1)} %get-tuple-element.138) | copy-start | bytes 8060932
  339.6 115.3 %reduce-scatter.5.cloned.1.call-start = ((), (), s32[]{:S(2)}) async-start(), calls=%async_computation.3 | async-start | bytes 1986560 | tf_op jit(solution)/shard_map/reduce_scatter | solution.py:1981
  339.6 47.7 %collective-permute-start.1 = (bf16[4,1552,128]{2,1,0:T(8,128)(2,1)}, bf16[4,1552,128]{2,1,0:T(8,128)(2,1)S(1)}, u32[]{:S(2)}, u32[]{:S(2)}) collective-permute-start(bf16[4,1552,128]{2,1,0:T(8,128)(2,1)} %get-tuple-element.140), channel_id=1, source_target_pairs={{0,4},{4,0},{8,12},{12,8},{16,20},{20,16},{24,28},{28,24},{1,5},{5... | collective-permute-start | bytes 4767752 | tf_op jit(solution)/shard_map/ppermute | solution.py:1973
  340.3 52.9 %copy-start.3 = (bf16[4,1552,128]{2,1,0:T(8,128)(2,1)S(1)}, bf16[4,1552,128]{2,1,0:T(8,128)(2,1)}, u32[]{:S(2)}) copy-start(bf16[4,1552,128]{2,1,0:T(8,128)(2,1)} %get-tuple-element.142) | copy-start | bytes 4767748
  394.8 60.1 %collective-permute-start.2 = (bf16[4,2624,128]{2,1,0:T(8,128)(2,1)}, bf16[4,2624,128]{2,1,0:T(8,128)(2,1)S(1)}, u32[]{:S(2)}, u32[]{:S(2)}) collective-permute-start(bf16[4,2624,128]{2,1,0:T(8,128)(2,1)} %get-tuple-element.161), channel_id=1, source_target_pairs={{0,4},{4,0},{8,12},{12,8},{16,20},{20,16},{24,28},{28,24},{1,5},{5... | collective-permute-start | bytes 8060936 | tf_op jit(solution)/shard_map/ppermute | solution.py:1973
  454.9 1.5 copy-start
Sparse Core Ops, SparseCore 0:
  89.6 37.8 all-gather.2
  339.7 53.4 reduce-scatter.2
  396.2 35.4 reduce-scatter.4

commit v5 on v4

--- a/solution.py
+++ b/solution.py
@@ -116,9 +116,9 @@
         *outs, up_whole, near, far = refs[:8]
         refs = refs[8:]
     else:
-        up_source, *refs = refs
-        *outs, up_whole = refs[:6]
-        refs = refs[6:]
+        up_source, cotangent_hbm, *refs = refs
+        *outs, up_whole, ddown_hbm = refs[:7]
+        refs = refs[7:]
     proj_ref, gated_ref, start_ref, inv_ref, pseudo_ref, mixed_ref = refs[:6]
     load_sem, store_sem, halo, state, *sems = refs[6:]
 
@@ -147,6 +147,12 @@
     ready()
     shard.start_far(0)
     shard.start_near()
+    if layer == 1:
+        ddown, ddown_sems, *gather_refs = sems[5:]
+        gather = Gather(ddown, *gather_refs, cotangent_hbm.shape[0])
+        count = gather.size // SUB
+        own_rows = ddown.at[block_rows(gather.y, gather.c, gather.size)]
+        pltpu.make_async_copy(cotangent_hbm, own_rows, ddown_sems.at[0]).start()
     halo[...] = jnp.zeros_like(halo)
     state[...] = jnp.zeros_like(state)
     row = grid_of((CHUNK, CHUNK), 0)
@@ -222,6 +228,10 @@
             shard.forward(0)
             if layer == 0:
                 quarter.start_quarter()
+            else:
+                pltpu.make_async_copy(cotangent_hbm, own_rows, ddown_sems.at[0]).wait()
+                for i in range(count):
+                    gather.start(i)
 
         @pl.when(step == 4)
         def _():
@@ -234,6 +244,16 @@
     shard.finish()
     if layer == 0:
         quarter.wait_quarter()
+    else:
+        for i in range(count):
+            gather.across(i)
+        for i in range(count):
+            gather.sibling(i)
+            gather.diagonal(i)
+        whole_out = pltpu.make_async_copy(ddown, ddown_hbm, ddown_sems.at[1])
+        whole_out.start()
+        gather.finish()
+        whole_out.wait()
     for c in range(chunks):
         for store in stores(c):
             store.wait()
@@ -247,6 +267,14 @@
     wholes = (jax.ShapeDtypeStruct((1024, 1536), bf16),)
     if layer == 0:
         wholes = wholes * 2 + (jax.ShapeDtypeStruct((2, PART, 1536), bf16),)
+        carried = Reshard.scratch() * 2
+    else:
+        wholes = wholes + (jax.ShapeDtypeStruct((tokens, 1024), bf16),)
+        carried = Reshard.scratch() + [
+            pltpu.VMEM((tokens, 1024), bf16),
+            pltpu.SemaphoreType.DMA((2,)),
+        ]
+        carried += gather_sems(tokens // 4)
     return pl.pallas_call(
         partial(mixer_forward_kernel, layer),
         out_shape=(
@@ -270,7 +298,7 @@
             pltpu.SemaphoreType.DMA((5, chunks)),
         ]
         + [pltpu.VMEM((8, 1024), f32), pltpu.VMEM((2, DK, DV), f32)]
-        + Reshard.scratch() * len(sources),
+        + carried,
         compiler_params=pltpu.CompilerParams(
             collective_id=8 + layer, has_side_effects=True, vmem_limit_bytes=LIMIT
         ),
@@ -490,6 +518,10 @@
     return pl.ds(pl.multiple_of((2 * y + c) * size + i * SUB, SUB), SUB)
 
 
+def block_rows(y, c, size):
+    return pl.ds(pl.multiple_of((2 * y + c) * size, size), size)
+
+
 def greet(y, c):
     barrier = pltpu.get_barrier_semaphore()
     for target in (2 * y + 1 - c, 2 * (1 - y) + c):
@@ -1080,14 +1112,18 @@
 
 def ffn_forward_kernel(
     layer, gated_ref, res_ref, gain_ref, raw_ref, down_ref, ffn_ref, whole_ref,
-    mid_hbm, normed_hbm, up_hbm, hidden_hbm, out_ref,
-    wup_ref, wdown_ref, wout_ref, loads, shard_loads,
-    mid_ref, normed_ref, up_ref, hidden_ref, out_sems, *scratch,
+    mid_hbm, normed_hbm, up_hbm, hidden_hbm, *refs
 ):
+    last = layer == LAYERS - 1
+    if not last:
+        out_ref, *refs = refs
+    wup_ref, wdown_ref, wout_ref, loads, shard_loads, *refs = refs
+    mid_ref, normed_ref, up_ref, hidden_ref, out_sems, *scratch = refs
     outgoing = Outgoing(out_sems)
     loaded_out = load_whole(raw_ref.at[layer], wout_ref, loads.at[2])
     loaded = load_shard((ffn_ref.at[layer], up_lanes, whole_ref), wup_ref, shard_loads)
-    loaded_down = load_down(down_ref.at[layer], wdown_ref, loads.at[1])
+    if not last:
+        loaded_down = load_down(down_ref.at[layer], wdown_ref, loads.at[1])
     size = res_ref.shape[0]
     count = size // SUB
     y, c = place()
@@ -1126,25 +1162,30 @@
         outgoing.put(normed_ref.at[rows], normed_hbm.at[rows])
         outgoing.put(up_ref.at[rows], up_hbm.at[rows])
         outgoing.put(hidden_ref.at[rows], hidden_hbm.at[rows])
-        return mm(hidden, wdown_ref[...])
+        return None if last else mm(hidden, wdown_ref[...])
 
     outgoing.put(mid_ref, mid_hbm)
     loaded()
-    loaded_down()
-    for i in range(count):
-        second.hold(1, i, feed(gather.own(i)))
-    for i in range(count):
-        second.give(1, i, feed(gather.sibling(i)))
-    for i in range(count):
-        near = gather.across(i)
-        second.hold(0, i, feed(near))
-        second.give(0, i, feed(gather.diagonal(i)))
-        second.relay(i)
-    for i in range(count):
-        rows = slice(i * SUB, (i + 1) * SUB)
-        out_ref[rows, :] = mid_ref[rows, :] + second.total(i)
+    if last:
+        for rows in in_order(gather):
+            feed(rows)
+    else:
+        loaded_down()
+        for i in range(count):
+            second.hold(1, i, feed(gather.own(i)))
+        for i in range(count):
+            second.give(1, i, feed(gather.sibling(i)))
+        for i in range(count):
+            near = gather.across(i)
+            second.hold(0, i, feed(near))
+            second.give(0, i, feed(gather.diagonal(i)))
+            second.relay(i)
+        for i in range(count):
+            rows = slice(i * SUB, (i + 1) * SUB)
+            out_ref[rows, :] = mid_ref[rows, :] + second.total(i)
     first.finish()
-    second.finish()
+    if not last:
+        second.finish()
     gather.finish()
     outgoing.wait()
 
@@ -1159,8 +1200,8 @@
             like(tokens, width, dtype=bf16),
             like(tokens, 1536, dtype=bf16),
             like(tokens, 768, dtype=bf16),
-            like(size, width),
-        ),
+        )
+        + (like(size, width),) * (layer < LAYERS - 1),
         (gated, residual, gain),
         [
             pltpu.VMEM((width, 1536), bf16),
@@ -1249,7 +1290,7 @@
 
 
 def ffn_backward_kernel(
-    layer, dres_ref, gain_ref, up_hbm, hidden_hbm, normed_hbm, mid_hbm, gated_hbm,
+    layer, dres_ref, gain_ref, ddown_hbm, up_hbm, hidden_hbm, normed_hbm, mid_hbm, gated_hbm,
     raw_ref, down_ref, ffn_ref, whole_ref,
     dmid_ref, dgated_hbm, ggain_ref, keep_hbm, send_hbm,
     wup_ref, wdown_ref, wout_ref, loads, shard_loads, ddown_ref, dup_ref, dbranch_ref, staged,
@@ -1265,7 +1306,11 @@
     count = size // SUB
     y, c = place()
     ready = greet(y, c)
-    first = Gather(ddown_ref, *scratch[:2], size)
+    gathered = layer == LAYERS - 1
+    if gathered:
+        loaded_rows = load_whole(ddown_hbm, ddown_ref, late_sems.at[5])
+    else:
+        first = Gather(ddown_ref, *scratch[:2], size)
     second = Gather(dbranch_ref, *scratch[2:4], size)
     scatter = Scatter(*scratch[4:], size)
     late = [
@@ -1280,11 +1325,12 @@
             )
         )
     ]
-    for i in range(count):
-        ddown_ref[first.own(i), :] = dres_ref[i * SUB : (i + 1) * SUB, :].astype(bf16)
-        if i == 0:
-            ready()
-        first.start(i)
+    if not gathered:
+        for i in range(count):
+            ddown_ref[first.own(i), :] = dres_ref[i * SUB : (i + 1) * SUB, :].astype(bf16)
+            if i == 0:
+                ready()
+            first.start(i)
 
     def feed(rows):
         d_hidden = mm(ddown_ref[rows, :], wdown_ref[...], NT)
@@ -1295,15 +1341,28 @@
     loaded()
     loaded_down()
     late[0]()
-    for i in range(count):
-        scatter.hold(1, i, feed(first.own(i)))
-    for i in range(count):
-        scatter.give(1, i, feed(first.sibling(i)))
-    for i in range(count):
-        near = first.across(i)
-        scatter.hold(0, i, feed(near))
-        scatter.give(0, i, feed(first.diagonal(i)))
-        scatter.relay(i)
+    if gathered:
+        loaded_rows()
+        for part in range(2):
+            yy = 1 - y if part == 0 else y
+            for i in range(count):
+                value = feed(shard_rows(yy, 1 - c, i, size))
+                if part == 0 and i == 0:
+                    ready()
+                scatter.give(part, i, value)
+                scatter.hold(part, i, feed(shard_rows(yy, c, i, size)))
+                if part == 0:
+                    scatter.relay(i)
+    else:
+        for i in range(count):
+            scatter.hold(1, i, feed(first.own(i)))
+        for i in range(count):
+            scatter.give(1, i, feed(first.sibling(i)))
+        for i in range(count):
+            near = first.across(i)
+            scatter.hold(0, i, feed(near))
+            scatter.give(0, i, feed(first.diagonal(i)))
+            scatter.relay(i)
     late[1]()
     for m in range(6):
         value = mm(hidden_ref[:, 128 * m : 128 * m + 128], ddown_ref[...], TN)
@@ -1337,13 +1396,14 @@
     for keep, hbm in ((keep_ref, keep_hbm), (send_ref, send_hbm)):
         rows = pl.ds(OUT_AT, FFN_ROWS - OUT_AT)
         outgoing.put(keep.at[:, rows], hbm.at[:, rows])
-    first.finish()
+    if not gathered:
+        first.finish()
     second.finish()
     scatter.finish()
     outgoing.wait()
 
 
-def ffn_backward(layer, d_res, up, hidden, normed, mid, gain, gated, w_out, w_down, w_up):
+def ffn_backward(layer, d_res, d_down, up, hidden, normed, mid, gain, gated, w_out, w_down, w_up):
     size, width = d_res.shape
     tokens = 4 * size
     return call(
@@ -1369,13 +1429,13 @@
         ]
         + [pltpu.VMEM(array.shape, array.dtype) for array in (up, hidden, normed, mid, gated, gated)]
         + [pltpu.VMEM((4, FFN_ROWS, 128), bf16)] * 2
-        + [pltpu.SemaphoreType.DMA((5,)), pltpu.SemaphoreType.DMA((5,))]
+        + [pltpu.SemaphoreType.DMA((6,)), pltpu.SemaphoreType.DMA((5,))]
         + gather_sems(size)
         + gather_sems(size)
         + Scatter.scratch(size, width),
         (3, 13)[layer],
         "ffn_backward",
-        (up, hidden, normed, mid, gated, w_out, w_down) + w_up,
+        (d_down, up, hidden, normed, mid, gated, w_out, w_down) + w_up,
         (1, 3, 4),
     )
 
@@ -1813,10 +1873,15 @@
 
 
 def finish_kernel(
-    p1, p2, k3, a3, k4, b4, f1, f2, f3, f4,
+    p1, p2, k3, a3, k4, b4, hidden_hbm, down_raw, mid_ref, f1, f2, f3, f4, last_ref,
     q1, q2, q3, q4, e1, e2, e3, e4, v3, x3, r3, l3, v4, x4, r4, l4,
     send, recv, local, send3, recv3, send4, recv4, send5, recv5, loads,
+    hidden_ref, wdown_ref, down_loads, *scratch,
 ):
+    loaded_hidden = load_whole(hidden_hbm, hidden_ref, down_loads.at[0])
+    loaded_down = load_down(down_raw.at[LAYERS - 1], wdown_ref, down_loads.at[1])
+    scatter = Scatter(*scratch, mid_ref.shape[0])
+    count = scatter.size // SUB
     rank = lax.axis_index("rep")
     x, z = rank % 2, (rank % 8) // 2
     y, c = place()
@@ -1864,6 +1929,24 @@
         halves(o).start()
     sems = (send, recv, local)
 
+    def down_begin():
+        loaded_hidden()
+        loaded_down()
+        for part in range(2):
+            yy = 1 - y if part == 0 else y
+            for i in range(count):
+                for cc, take in ((1 - c, scatter.give), (c, scatter.hold)):
+                    rows = shard_rows(yy, cc, i, scatter.size)
+                    take(part, i, mm(hidden_ref[rows, :], wdown_ref[...]))
+                if part == 0:
+                    scatter.relay(i)
+
+    def down_end():
+        for i in range(count):
+            rows = slice(i * SUB, (i + 1) * SUB)
+            last_ref[rows, :] = mid_ref[rows, :] + scatter.total(i)
+        scatter.finish()
+
     def merge(*owners):
         for o in owners:
             add_into(v3.at[o], v3.at[o], x3.at[o])
@@ -1885,6 +1968,7 @@
     g2.start_swap()
     g1.wait_swap()
     g1.begin()
+    down_begin()
     loaded[3].wait()
     arrive(3, 0)
     loaded[2].wait()
@@ -1919,6 +2003,7 @@
     g4.start_swap()
     g4.wait_swap()
     g4.begin()
+    down_end()
     g3.relay(2)
     g4.relay(1)
     g4.relay(2)
@@ -1932,16 +2017,18 @@
         halves(o).wait_send()
 
 
-def finish_reduction(p1, p2, k3, a3, k4, b4):
+def finish_reduction(p1, p2, k3, a3, k4, b4, hidden, w_down, mid):
     spot = pl.BlockSpec(memory_space=pl.ANY)
+    vmem = pl.BlockSpec(memory_space=pltpu.VMEM)
     big, small = p1.shape, p2.shape
     wide = (GATHERED_ROWS, 128)
     dma = pltpu.SemaphoreType.DMA
     return pl.pallas_call(
         finish_kernel,
-        out_shape=tuple(like(8, *shape, dtype=bf16) for shape in (big, wide, big, wide)),
-        in_specs=[spot] * 6,
-        out_specs=(spot,) * 4,
+        out_shape=tuple(like(8, *shape, dtype=bf16) for shape in (big, wide, big, wide))
+        + (like(*mid.shape),),
+        in_specs=[spot] * 8 + [vmem],
+        out_specs=(spot,) * 4 + (vmem,),
         scratch_shapes=[
             pltpu.VMEM(shape, bf16)
             for shape in [big, small] * 2 + [big, wide] * 2
@@ -1950,13 +2037,15 @@
         ]
         + [dma((5, 24)), dma((5, 24)), dma((4,))]
         + [dma((2, 4))] * 4
-        + [dma((4,)), dma((4,)), dma((5,))],
+        + [dma((4,)), dma((4,)), dma((5,))]
+        + [pltpu.VMEM(hidden.shape, bf16), pltpu.VMEM((768, mid.shape[1]), bf16), dma((2,))]
+        + Scatter.scratch(*mid.shape),
         compiler_params=pltpu.CompilerParams(
             collective_id=5, has_side_effects=True, vmem_limit_bytes=LIMIT
         ),
         cost_estimate=pl.CostEstimate(flops=1000, bytes_accessed=1000, transcendentals=0),
         name="finish_reduction",
-    )(p1, p2, k3, a3, k4, b4)
+    )(p1, p2, k3, a3, k4, b4, hidden, w_down, mid)
 
 
 def swap_route(bit, count):
@@ -2011,17 +2100,27 @@
     return pair.reshape((8,) + piece.shape)
 
 
-def finish_all(piece1, piece2, keep3, arrived3, keep4, send4, replicas):
+def finish_all(
+    piece1, piece2, keep3, arrived3, keep4, send4, hidden, w_down, mid, replicas
+):
     if replicas == 8:
-        return finish_reduction(piece1, piece2, keep3, arrived3, keep4, send4)
+        return finish_reduction(
+            piece1, piece2, keep3, arrived3, keep4, send4, hidden, w_down, mid
+        )
     piece3 = reduce_z(add_arrived(keep3, arrived3), replicas)
     piece4 = reduce_z(add_arrived(keep4, swap_x(send4, replicas)), replicas)
-    return [
+    finals = [
         spread(exchange(piece, *move), replicas)
         for piece, move in (
             (piece1, FFN_MOVE), (piece2, IN_MOVE), (piece3, FFN_MOVE), (piece4, IN_MOVE)
         )
     ]
+    padded = jnp.zeros((hidden.shape[1], mid.shape[1]), bf16)
+    offset = 64 * (lax.axis_index("grp") % 2)
+    padded = lax.dynamic_update_slice_in_dim(padded, w_down[LAYERS - 1], offset, 0)
+    partial_sum = mm(hidden, padded).astype(bf16)
+    down = lax.psum_scatter(partial_sum, "grp", scatter_dimension=0, tiled=True)
+    return finals + [mid + down.astype(f32)]
 
 
 def tie(*values):
@@ -2070,7 +2169,7 @@
         if l > 0:
             normed, projected, small = project(residual, gain_one, ab, in_weights[l])
         gated, *saved = mixer_forward(
-            l, projected, small, taps, heads, gain, (ffn_in, w_in)[: LAYERS - l]
+            l, projected, small, taps, heads, gain, (ffn_in, (w_in, cotangent[0])[l])
         )
         up_weights.append((ffn_in, saved[4]))
         if l == 0:
@@ -2082,12 +2181,15 @@
                     lax.all_gather(far, "rep", axis=0, axis_index_groups=planes_of(replicas)),
                 )
             )
+        else:
+            d_down = saved[5]
         saved = saved[:4]
-        mid, normed_two, up, hidden, residual_out = ffn_forward(
+        mid, normed_two, up, hidden, *residual_out = ffn_forward(
             l, gated, residual, gain_two, w_out, ffn_out, up_weights[l]
         )
         kept.append((residual, normed, projected, small, gated, saved, mid, normed_two, up, hidden))
-        residual = residual_out
+        if l == 0:
+            (residual,) = residual_out
 
     d_residual = cotangent[0].astype(f32)
 
@@ -2095,7 +2197,7 @@
         gain_one, gain_two, ab, taps, heads, gain = small_weights[l]
         residual, normed, projected, small, gated, saved, mid, normed_two, up, hidden = kept[l]
         return ffn_backward(
-            l, d_residual, up, hidden, normed_two, mid, gain_two, gated, w_out, ffn_out,
+            l, d_residual, d_down, up, hidden, normed_two, mid, gain_two, gated, w_out, ffn_out,
             up_weights[l],
         )
 
@@ -2127,8 +2229,11 @@
     mixed = mixer_part(0, d_gated)
     d_residual, keep4, send4 = project_part(0, d_mid, g_gain_two, mixed)
     d_residual, arrived3 = tie(d_residual, arrived3)
-    final1, final2, final3, final4 = finish_all(piece1, piece2, keep3, arrived3, keep4, send4, replicas)
+    final1, final2, final3, final4, last = finish_all(
+        piece1, piece2, keep3, arrived3, keep4, send4, kept[-1][-1], ffn_out, kept[-1][6], replicas
+    )
     finals = (final1, final2, final3, final4)
+    residual = last
     down_grads, out_grads, up_grads, w_in_grads, everyone, *ends = assemble(
         finals, residual, d_residual
     )

time: 725 us -> 715 us (0.986)
  Pallas kernels: 673 us -> 662 us
    pallas_call x8, Pallas kernels: 286 us -> 269 us  [call(): pl.pallas_call(kernel, out_shape=out_shape, in_specs=[vmem] * len(inputs)...]
where the time goes in v5:
time: 715 us; the launch traced here: 708 us
  Pallas kernels  662 us (93%)
  between operations  14.2 us (2%)
  local copies, waits for them, and re-layouts  10.5 us (1%)
  other arithmetic  8.82 us (1%)
  waiting for transfers between devices  7.7 us (1%)
    pallas_call x8, Pallas kernels, call(): pl.pallas_call(kernel, out_shape=out_shape, in_specs=[vmem] * len(inputs)...  269 us
    pallas_call x1, Pallas kernels, finish_reduction(): pl.pallas_call(finish_kernel, out_shape=tuple((like(8, *shape, dtype=bf16...  232 us
    pallas_call x2, Pallas kernels, mixer_forward(): pl.pallas_call(partial(mixer_forward_kernel, layer), out_shape=(jax.Shape...  72 us
    pallas_call x2, Pallas kernels, mixer_backward(): pl.pallas_call(mixer_backward_kernel, out_shape=(jax.ShapeDtypeStruct((to...  69.9 us
    pallas_call x1, Pallas kernels, assemble(): pl.pallas_call(assemble_kernel, out_shape=tuple((like(*shape) for shape i...  18.5 us
  transfers between devices with their start and end apart: 6, of which 3 were waited for; matrix products, arithmetic and copies ran while one was open for 0% of the time, Pallas kernels for 29%

profile of v5, /device:TPU:0, one launch (start us, length us, event | category | flops | bytes accessed | tf_op | source)
XLA Modules:
  0.0 708.1 jit_solution(13796480578753627821)
XLA Ops:
  7.9 0.7 reshape.64
  8.6 0.7 reshape.65
  9.4 0.7 reshape.66
  10.8 0.7 fusion.19
  11.6 0.7 fusion.18
  12.3 41.4 %start.1 = (bf16[1024,1024]{1,0:T(8,128)(2,1)}, bf16[1024,1536]{1,0:T(8,128)(2,1)}, f32[1024,128]{1,0:T(8,128)}, bf16[1024,1536]{1,0:T(8,128)(2,1)}, f32[1,1024]...) custom-call(bf16[256,1024]{1,0:T(8,128)(2,1)} %bitcast.41, ...), custom_call_target="tpu_custom_call" | custom-call | flops 1000 | bytes 1000 | tf_op jit(solution)/shard_map/start/pallas_call | solution.py:654
  54.4 35.1 %mixer_forward.2 = (bf16[1024,512]{1,0:T(8,128)(2,1)}, f32[8,2,128,256]{3,2,1,0:T(8,128)}, bf16[8,2,128,128]{3,2,1,0:T(8,128)(2,1)}, f32[8,2,128,256]{3,2,1,0:T(...) custom-call(bf16[1024,1536]{1,0:T(8,128)(2,1)} %get-tuple-element.96, ...), custom_call_target="tpu_custom_call" | custom-call | tf_op jit(solution)/shard_map/mixer_forward/pallas_call | solution.py:278
  90.0 1.1 bitcast_convert_fusion.1.res_ref.refs_1_
  91.1 42.2 %ffn_forward.2 = (f32[256,1024]{1,0:T(8,128)}, bf16[1024,1024]{1,0:T(8,128)(2,1)}, bf16[1024,1536]{1,0:T(8,128)(2,1)}, bf16[1024,768]{1,0:T(8,128)(2,1)}, f32[256,1024]{1,0:T(8,128)}) custom-call(bf16[1024,512]{1,0:T(8,128)(2,1)} %get-tuple-element.100.gated_ref.gated_hbm, f32[256,1024]{1,0:T(8,128)} %bitcast_convert_fusion.1.res_ref.refs_1_, ...), custom_call_target="tpu_custom_call" | custom-call | flops 1000 | bytes 1000 | tf_op jit(solution)/shard_map/ffn_forward/pallas_call | solution.py:654
  133.4 1.1 bitcast_convert_fusion.dres_ref
  134.5 18.3 %project.1 = (bf16[1024,1024]{1,0:T(8,128)(2,1)}, bf16[1024,1536]{1,0:T(8,128)(2,1)}, f32[1024,128]{1,0:T(8,128)}) custom-call(f32[256,1024]{1,0:T(8,128)} %get-tuple-element.103.res_ref.refs_1_, f32[1,1024]{1,0:T(1,128)} %get-tuple-element.104.gain_ref, bf16[1024,128]{1,0:T(8,128)(2,1)} %get-tuple-element.105.ab_ref, bf16[2,256,6144]{2,1,0:T(8,128)(2,1)} %refs_3_.1, ...), custom_call_target="tpu_custom_call" | custom-call | flops 1000 | bytes 1000 | tf_op jit(solution)/shard_map/project/pallas_call | solution.py:654
  152.8 36.9 %mixer_forward.3 = (bf16[1024,512]{1,0:T(8,128)(2,1)}, f32[8,2,128,256]{3,2,1,0:T(8,128)}, bf16[8,2,128,128]{3,2,1,0:T(8,128)(2,1)}, f32[8,2,128,256]{3,2,1,0:T(...) custom-call(bf16[1024,1536]{1,0:T(8,128)(2,1)} %get-tuple-element.111.proj_hbm.refs_0_, ...), custom_call_target="tpu_custom_call" | custom-call | tf_op jit(solution)/shard_map/mixer_forward/pallas_call | solution.py:278
  189.7 31.9 %ffn_forward.3 = (f32[256,1024]{1,0:T(8,128)}, bf16[1024,1024]{1,0:T(8,128)(2,1)}, bf16[1024,1536]{1,0:T(8,128)(2,1)}, bf16[1024,768]{1,0:T(8,128)(2,1)}) custom-call(bf16[1024,512]{1,0:T(8,128)(2,1)} %get-tuple-element.118.gated_ref.gated_hbm, f32[256,1024]{1,0:T(8,128)} %get-tuple-element.103.res_ref.refs_1_, f32[1,1024]{1,0:T(1,128)} %get-tuple-element.116.gain_ref, ...), custom_call_target="tpu_custom_call" | custom-call | flops 1000 | bytes 1000 | tf_op jit(solution)/shard_map/ffn_forward/pallas_call | solution.py:654
  221.6 42.6 %ffn_backward.2 = (f32[256,1024]{1,0:T(8,128)}, bf16[1024,512]{1,0:T(8,128)(2,1)}, f32[8,1024]{1,0:T(8,128)}, bf16[4,2624,128]{2,1,0:T(8,128)(2,1)}, bf16[4,2624,128]{2,1,0:T(8,128)(2,1)}) custom-call(f32[256,1024]{1,0:T(8,128)} %bitcast_convert_fusion.dres_ref, f32[1,1024]{1,0:T(1,128)} %get-tuple-element.116.gain_ref, ...), custom_call_target="tpu_custom_call" | custom-call | flops 1000 | bytes 1000 | tf_op jit(solution)/shard_map/ffn_backward/pallas_call | solution.py:654
  264.2 1.5 collective-permute-start
  265.8 34.9 %mixer_backward.2 = (bf16[1024,1536]{1,0:T(8,128)(2,1)}, bf16[1024,128]{1,0:T(8,128)(2,1)}, f32[8,1024]{1,0:T(8,128)}, f32[8,256]{1,0:T(8,128)}) custom-call(f32[1024,128]{1,0:T(8,128)} %get-tuple-element.108.small_ref, f32[8,1024]{1,0:T(8,128)} %get-tuple-element.109.taps_ref, f32[8,128]{1,0:T(8,128)} %get-tuple-element.215.heads_ref, ...), custom_call_target="tpu_custom_call" | custom-call | tf_op jit(solution)/shard_map/mixer_backward/pallas_call | solution.py:484
  300.7 22.8 %project_backward.2 = (f32[256,1024]{1,0:T(8,128)}, bf16[4,1552,128]{2,1,0:T(8,128)(2,1)}, bf16[4,1552,128]{2,1,0:T(8,128)(2,1)}) custom-call(bf16[1024,1536]{1,0:T(8,128)(2,1)} %get-tuple-element.125.dproj_ref, bf16[1024,128]{1,0:T(8,128)(2,1)} %get-tuple-element.126.dsmall_ref, bf16[1024,128]{1,0:T(8,128)(2,1)} %get-tuple-element.105.ab_ref, ...), custom_call_target="tpu_custom_call" | custom-call | flops 1000 | bytes 1000 | tf_op jit(solution)/shard_map/project_backward/pallas_call | solution.py:654
  323.5 1.6 collective-permute-done
  325.2 2.2 add_convert_fusion
  327.5 1.5 collective-permute-start.1
  329.0 46.2 %ffn_backward.3 = (f32[256,1024]{1,0:T(8,128)}, bf16[1024,512]{1,0:T(8,128)(2,1)}, f32[8,1024]{1,0:T(8,128)}, bf16[4,2624,128]{2,1,0:T(8,128)(2,1)}, bf16[4,2624,128]{2,1,0:T(8,128)(2,1)}) custom-call(f32[256,1024]{1,0:T(8,128)} %get-tuple-element.134.dres_ref, f32[1,1024]{1,0:T(1,128)} %get-tuple-element.101.gain_ref, ...), custom_call_target="tpu_custom_call" | custom-call | flops 1000 | bytes 1000 | tf_op jit(solution)/shard_map/ffn_backward/pallas_call | solution.py:654
  375.2 5.8 reduce-scatter.3.cloned.1.call-done
  381.0 1.6 add_convert_fusion.1
  382.6 1.5 collective-permute-start.2
  384.1 34.9 %mixer_backward.3 = (bf16[1024,1536]{1,0:T(8,128)(2,1)}, bf16[1024,128]{1,0:T(8,128)(2,1)}, f32[8,1024]{1,0:T(8,128)}, f32[8,256]{1,0:T(8,128)}) custom-call(f32[1024,128]{1,0:T(8,128)} %get-tuple-element.97.small_ref, f32[8,1024]{1,0:T(8,128)} %get-tuple-element.98.taps_ref, f32[8,128]{1,0:T(8,128)} %get-tuple-element.214.heads_ref, ...), custom_call_target="tpu_custom_call" | custom-call | tf_op jit(solution)/shard_map/mixer_backward/pallas_call | solution.py:484
  419.1 23.5 %project_backward.3 = (f32[256,1024]{1,0:T(8,128)}, bf16[4,1552,128]{2,1,0:T(8,128)(2,1)}, bf16[4,1552,128]{2,1,0:T(8,128)(2,1)}) custom-call(bf16[1024,1536]{1,0:T(8,128)(2,1)} %get-tuple-element.152.dproj_ref, bf16[1024,128]{1,0:T(8,128)(2,1)} %get-tuple-element.153.dsmall_ref, bf16[1024,128]{1,0:T(8,128)(2,1)} %get-tuple-element.154.ab_ref, ...), custom_call_target="tpu_custom_call" | custom-call | flops 1000 | bytes 1000 | tf_op jit(solution)/shard_map/project_backward/pallas_call | solution.py:654
  442.7 1.5 copy-done
  444.2 232.4 %finish_reduction.1 = (bf16[8,2624,128]{2,1,0:T(8,128)(2,1)}, bf16[8,1600,128]{2,1,0:T(8,128)(2,1)}, bf16[8,2624,128]{2,1,0:T(8,128)(2,1)}, bf16[8,1600,128]{2,1,0:T(8,128)(2,1)}, f32[256,1024]{1,0:T(8,128)}) custom-call(bf16[2624,128]{1,0:T(8,128)(2,1)} %bitcast.43, bf16[1552,128]{1,0:T(8,128)(2,1)} %bitcast.44, ...), custom_call_target="tpu_custom_call" | custom-call | flops 1000 | bytes 1000 | tf_op jit(solution)/shard_map/finish_reduction/pallas_call | solution.py:2026
  676.6 18.5 %assemble.1 = (f32[2,704,1024]{2,1,0:T(8,128)}, f32[2,512,1024]{2,1,0:T(8,128)}, f32[2,256,5632]{2,1,0:T(8,128)}, f32[2,256,6144]{2,1,0:T(8,128)}, f32[4,2,128,1...) custom-call(bf16[8,2624,128]{2,1,0:T(8,128)(2,1)} %get-tuple-element.167.f1, ...), custom_call_target="tpu_custom_call" | custom-call | tf_op jit(solution)/shard_map/assemble/pallas_call | solution.py:1645
  695.1 0.9 slice_reduce_fusion
  696.0 1.0 fusion.16
  698.5 0.9 dynamic-slice_bitcast_fusion
  (43 shorter events, 6.2 us)
Async XLA Ops:
  7.2 127.3 %all-gather.3.cloned.1.call-start = ((), (), s32[]{:S(2)}) async-start(), calls=%async_computation.4 | async-start | bytes 1966080 | tf_op jit(solution)/shard_map/all_gather | solution.py:2181
  54.4 35.7 %copy-start.2 = (bf16[1,256,1024]{2,1,0:T(8,128)(2,1)S(1)}, bf16[1,256,1024]{2,1,0:T(8,128)(2,1)}, u32[]{:S(2)}) copy-start(bf16[1,256,1024]{2,1,0:T(8,128)(2,1)} %param.12) | copy-start | bytes 1572868
  89.5 291.5 %reduce-scatter.3.cloned.1.call-start = ((), (), s32[]{:S(2)}) async-start(), calls=%async_computation.2 | async-start | bytes 3358720 | tf_op jit(solution)/shard_map/reduce_scatter | solution.py:2070
  91.1 42.3 %copy-start.3 = (bf16[1,256,1024]{2,1,0:T(8,128)(2,1)S(1)}, bf16[1,256,1024]{2,1,0:T(8,128)(2,1)}, u32[]{:S(2)}) copy-start(bf16[1,256,1024]{2,1,0:T(8,128)(2,1)} %param.23) | copy-start | bytes 1572868
  264.2 60.9 %collective-permute-start = (bf16[4,2624,128]{2,1,0:T(8,128)(2,1)}, bf16[4,2624,128]{2,1,0:T(8,128)(2,1)S(1)}, u32[]{:S(2)}, u32[]{:S(2)}) collective-permute-start(bf16[4,2624,128]{2,1,0:T(8,128)(2,1)} %get-tuple-element.133), channel_id=1, source_target_pairs={{0,4},{4,0},{8,12},{12,8},{16,20},{20,16},{24,28},{28,24},{1,5},{5... | collective-permute-start | bytes 8060936 | tf_op jit(solution)/shard_map/ppermute | solution.py:2062
  300.7 24.5 %copy-start.1 = (bf16[4,2624,128]{2,1,0:T(8,128)(2,1)S(1)}, bf16[4,2624,128]{2,1,0:T(8,128)(2,1)}, u32[]{:S(2)}) copy-start(bf16[4,2624,128]{2,1,0:T(8,128)(2,1)} %get-tuple-element.140) | copy-start | bytes 8060932
  327.4 115.3 %reduce-scatter.5.cloned.1.call-start = ((), (), s32[]{:S(2)}) async-start(), calls=%async_computation.3 | async-start | bytes 1986560 | tf_op jit(solution)/shard_map/reduce_scatter | solution.py:2070
  327.5 47.7 %collective-permute-start.1 = (bf16[4,1552,128]{2,1,0:T(8,128)(2,1)}, bf16[4,1552,128]{2,1,0:T(8,128)(2,1)S(1)}, u32[]{:S(2)}, u32[]{:S(2)}) collective-permute-start(bf16[4,1552,128]{2,1,0:T(8,128)(2,1)} %get-tuple-element.142), channel_id=1, source_target_pairs={{0,4},{4,0},{8,12},{12,8},{16,20},{20,16},{24,28},{28,24},{1,5},{5... | collective-permute-start | bytes 4767752 | tf_op jit(solution)/shard_map/ppermute | solution.py:2062
  329.0 52.0 %copy-start.4 = (bf16[4,1552,128]{2,1,0:T(8,128)(2,1)S(1)}, bf16[4,1552,128]{2,1,0:T(8,128)(2,1)}, u32[]{:S(2)}) copy-start(bf16[4,1552,128]{2,1,0:T(8,128)(2,1)} %get-tuple-element.144) | copy-start | bytes 4767748
  382.6 60.1 %collective-permute-start.2 = (bf16[4,2624,128]{2,1,0:T(8,128)(2,1)}, bf16[4,2624,128]{2,1,0:T(8,128)(2,1)S(1)}, u32[]{:S(2)}, u32[]{:S(2)}) collective-permute-start(bf16[4,2624,128]{2,1,0:T(8,128)(2,1)} %get-tuple-element.163), channel_id=1, source_target_pairs={{0,4},{4,0},{8,12},{12,8},{16,20},{20,16},{24,28},{28,24},{1,5},{5... | collective-permute-start | bytes 8060936 | tf_op jit(solution)/shard_map/ppermute | solution.py:2062
  442.7 1.5 copy-start
Sparse Core Ops, SparseCore 0:
  89.6 37.8 all-gather.2
  327.5 53.4 reduce-scatter.2
  384.0 35.4 reduce-scatter.4

commit v6 on v5

--- a/solution.py
+++ b/solution.py
@@ -1149,7 +1149,7 @@
                 first.relay(i)
     for i in range(count):
         rows = slice(i * SUB, (i + 1) * SUB)
-        mid = res_ref[rows, :] + first.total(i)
+        mid = res_ref[rows, :].astype(f32) + first.total(i)
         mid_ref[rows, :] = mid
         normed_ref[gather.own(i), :] = normalise(mid, gain_ref[...]).astype(bf16)
         gather.start(i)
@@ -1372,7 +1372,7 @@
     for i in range(count):
         rows = slice(i * SUB, (i + 1) * SUB)
         d_norm, g_gain = normalise_back(mid_ref[rows, :], gain_ref[...], scatter.total(i))
-        d_mid = dres_ref[rows, :] + d_norm
+        d_mid = dres_ref[rows, :].astype(f32) + d_norm
         dmid_ref[rows, :] = d_mid
         ggain_ref[0:1, :] += g_gain
         dbranch_ref[second.own(i), :] = d_mid.astype(bf16)
@@ -1504,7 +1504,9 @@
     late[2]()
     for i in range(count):
         rows = slice(i * SUB, (i + 1) * SUB)
-        d_norm, g_gain = normalise_back(res_ref[rows, :], gain_ref[...], scatter.total(i))
+        d_norm, g_gain = normalise_back(
+            res_ref[rows, :].astype(f32), gain_ref[...], scatter.total(i)
+        )
         dres_ref[rows, :] = dmid_ref[rows, :] + d_norm
         gain_sum = gain_sum + g_gain
     for k in range(8):
@@ -1554,8 +1556,8 @@
         pltpu.make_async_copy(src, dst, loads.at[k])
         for k, (src, dst) in enumerate(((f1, p1), (f2, p2), (f3, p3), (f4, p4)))
     ]
-    for copy in copies:
-        copy.start()
+    copies[0].start()
+    copies[1].start()
     block_ref[...] = last_ref[...].astype(bf16)
     input_ref[...] = grad_ref[...].astype(bf16)
     left = grid_of((32, 128), 1) < 64
@@ -1622,8 +1624,10 @@
 
     waiting = []
     copies[0].wait()
+    copies[2].start()
     waiting += ffn(1, p1)
     copies[1].wait()
+    copies[3].start()
     waiting += projection(1, p2)
     copies[2].wait()
     waiting += ffn(0, p3)
@@ -2161,7 +2165,7 @@
             )
         )
 
-    residual = x_input[0].astype(f32)
+    residual = x_input[0]
     kept = []
     in_weights, up_weights = [(in_weight,)], []
     for l in range(LAYERS):
@@ -2191,7 +2195,7 @@
         if l == 0:
             (residual,) = residual_out
 
-    d_residual = cotangent[0].astype(f32)
+    d_residual = cotangent[0]
 
     def ffn_part(l, d_residual):
         gain_one, gain_two, ab, taps, heads, gain = small_weights[l]

time: 715 us -> 712 us (level)
  no operation moved by 1% of the time
where the time goes in v6:
time: 712 us; the launch traced here: 705 us
  Pallas kernels  661 us (93%)
  between operations  14.2 us (2%)
  local copies, waits for them, and re-layouts  10.5 us (1%)
  waiting for transfers between devices  7.89 us (1%)
    pallas_call x8, Pallas kernels, call(): pl.pallas_call(kernel, out_shape=out_shape, in_specs=[vmem] * len(inputs)...  268 us
    pallas_call x1, Pallas kernels, finish_reduction(): pl.pallas_call(finish_kernel, out_shape=tuple((like(8, *shape, dtype=bf16...  232 us
    pallas_call x2, Pallas kernels, mixer_forward(): pl.pallas_call(partial(mixer_forward_kernel, layer), out_shape=(jax.Shape...  71.9 us
    pallas_call x2, Pallas kernels, mixer_backward(): pl.pallas_call(mixer_backward_kernel, out_shape=(jax.ShapeDtypeStruct((to...  69.9 us
    pallas_call x1, Pallas kernels, assemble(): pl.pallas_call(assemble_kernel, out_shape=tuple((like(*shape) for shape i...  18.5 us
  transfers between devices with their start and end apart: 6, of which 3 were waited for; matrix products, arithmetic and copies ran while one was open for 0% of the time, Pallas kernels for 29%

profile of v6, /device:TPU:0, one launch (start us, length us, event | category | flops | bytes accessed | tf_op | source)
XLA Modules:
  0.0 705.5 jit_solution(7503178104188670428)
XLA Ops:
  7.2 0.7 reshape.63
  7.9 0.7 reshape.64
  8.6 0.7 reshape.65
  9.4 0.7 reshape.66
  10.8 0.7 fusion.19
  11.6 0.7 fusion.18
  12.3 41.4 %start.1 = (bf16[1024,1024]{1,0:T(8,128)(2,1)}, bf16[1024,1536]{1,0:T(8,128)(2,1)}, f32[1024,128]{1,0:T(8,128)}, bf16[1024,1536]{1,0:T(8,128)(2,1)}, f32[1,1024]...) custom-call(bf16[256,1024]{1,0:T(8,128)(2,1)} %bitcast.39, ...), custom_call_target="tpu_custom_call" | custom-call | flops 1000 | bytes 1000 | tf_op jit(solution)/shard_map/start/pallas_call | solution.py:654
  53.7 0.7 fusion.10
  54.4 35.1 %mixer_forward.2 = (bf16[1024,512]{1,0:T(8,128)(2,1)}, f32[8,2,128,256]{3,2,1,0:T(8,128)}, bf16[8,2,128,128]{3,2,1,0:T(8,128)(2,1)}, f32[8,2,128,256]{3,2,1,0:T(...) custom-call(bf16[1024,1536]{1,0:T(8,128)(2,1)} %get-tuple-element.96, ...), custom_call_target="tpu_custom_call" | custom-call | tf_op jit(solution)/shard_map/mixer_forward/pallas_call | solution.py:278
  90.0 42.1 %ffn_forward.2 = (f32[256,1024]{1,0:T(8,128)}, bf16[1024,1024]{1,0:T(8,128)(2,1)}, bf16[1024,1536]{1,0:T(8,128)(2,1)}, bf16[1024,768]{1,0:T(8,128)(2,1)}, f32[256,1024]{1,0:T(8,128)}) custom-call(bf16[1024,512]{1,0:T(8,128)(2,1)} %get-tuple-element.100.gated_ref.gated_hbm, bf16[256,1024]{1,0:T(8,128)(2,1)} %bitcast.40, ...), custom_call_target="tpu_custom_call" | custom-call | flops 1000 | bytes 1000 | tf_op jit(solution)/shard_map/ffn_forward/pallas_call | solution.py:654
  132.1 18.3 %project.1 = (bf16[1024,1024]{1,0:T(8,128)(2,1)}, bf16[1024,1536]{1,0:T(8,128)(2,1)}, f32[1024,128]{1,0:T(8,128)}) custom-call(f32[256,1024]{1,0:T(8,128)} %get-tuple-element.103.res_ref.refs_1_, f32[1,1024]{1,0:T(1,128)} %get-tuple-element.104.gain_ref, bf16[1024,128]{1,0:T(8,128)(2,1)} %get-tuple-element.105.ab_ref, bf16[2,256,6144]{2,1,0:T(8,128)(2,1)} %refs_3_.1, ...), custom_call_target="tpu_custom_call" | custom-call | flops 1000 | bytes 1000 | tf_op jit(solution)/shard_map/project/pallas_call | solution.py:654
  150.4 36.9 %mixer_forward.3 = (bf16[1024,512]{1,0:T(8,128)(2,1)}, f32[8,2,128,256]{3,2,1,0:T(8,128)}, bf16[8,2,128,128]{3,2,1,0:T(8,128)(2,1)}, f32[8,2,128,256]{3,2,1,0:T(...) custom-call(bf16[1024,1536]{1,0:T(8,128)(2,1)} %get-tuple-element.111.proj_hbm.refs_0_, ...), custom_call_target="tpu_custom_call" | custom-call | tf_op jit(solution)/shard_map/mixer_forward/pallas_call | solution.py:278
  187.3 31.9 %ffn_forward.3 = (f32[256,1024]{1,0:T(8,128)}, bf16[1024,1024]{1,0:T(8,128)(2,1)}, bf16[1024,1536]{1,0:T(8,128)(2,1)}, bf16[1024,768]{1,0:T(8,128)(2,1)}) custom-call(bf16[1024,512]{1,0:T(8,128)(2,1)} %get-tuple-element.118.gated_ref.gated_hbm, f32[256,1024]{1,0:T(8,128)} %get-tuple-element.103.res_ref.refs_1_, f32[1,1024]{1,0:T(1,128)} %get-tuple-element.116.gain_ref, ...), custom_call_target="tpu_custom_call" | custom-call | flops 1000 | bytes 1000 | tf_op jit(solution)/shard_map/ffn_forward/pallas_call | solution.py:654
  219.2 42.4 %ffn_backward.2 = (f32[256,1024]{1,0:T(8,128)}, bf16[1024,512]{1,0:T(8,128)(2,1)}, f32[8,1024]{1,0:T(8,128)}, bf16[4,2624,128]{2,1,0:T(8,128)(2,1)}, bf16[4,2624,128]{2,1,0:T(8,128)(2,1)}) custom-call(bf16[256,1024]{1,0:T(8,128)(2,1)} %bitcast.43, f32[1,1024]{1,0:T(1,128)} %get-tuple-element.116.gain_ref, bf16[1024,1024]{1,0:T(8,128)(2,1)} %get-tuple-element.117.ddown_hbm, ...), custom_call_target="tpu_custom_call" | custom-call | flops 1000 | bytes 1000 | tf_op jit(solution)/shard_map/ffn_backward/pallas_call | solution.py:654
  261.7 1.5 collective-permute-start
  263.1 34.9 %mixer_backward.2 = (bf16[1024,1536]{1,0:T(8,128)(2,1)}, bf16[1024,128]{1,0:T(8,128)(2,1)}, f32[8,1024]{1,0:T(8,128)}, f32[8,256]{1,0:T(8,128)}) custom-call(f32[1024,128]{1,0:T(8,128)} %get-tuple-element.108.small_ref, f32[8,1024]{1,0:T(8,128)} %get-tuple-element.109.taps_ref, f32[8,128]{1,0:T(8,128)} %get-tuple-element.215.heads_ref, ...), custom_call_target="tpu_custom_call" | custom-call | tf_op jit(solution)/shard_map/mixer_backward/pallas_call | solution.py:484
  298.1 22.8 %project_backward.2 = (f32[256,1024]{1,0:T(8,128)}, bf16[4,1552,128]{2,1,0:T(8,128)(2,1)}, bf16[4,1552,128]{2,1,0:T(8,128)(2,1)}) custom-call(bf16[1024,1536]{1,0:T(8,128)(2,1)} %get-tuple-element.125.dproj_ref, bf16[1024,128]{1,0:T(8,128)(2,1)} %get-tuple-element.126.dsmall_ref, bf16[1024,128]{1,0:T(8,128)(2,1)} %get-tuple-element.105.ab_ref, ...), custom_call_target="tpu_custom_call" | custom-call | flops 1000 | bytes 1000 | tf_op jit(solution)/shard_map/project_backward/pallas_call | solution.py:654
  320.9 1.7 collective-permute-done
  322.6 2.2 add_convert_fusion
  324.9 1.5 collective-permute-start.1
  326.4 46.2 %ffn_backward.3 = (f32[256,1024]{1,0:T(8,128)}, bf16[1024,512]{1,0:T(8,128)(2,1)}, f32[8,1024]{1,0:T(8,128)}, bf16[4,2624,128]{2,1,0:T(8,128)(2,1)}, bf16[4,2624,128]{2,1,0:T(8,128)(2,1)}) custom-call(f32[256,1024]{1,0:T(8,128)} %get-tuple-element.134.dres_ref, f32[1,1024]{1,0:T(1,128)} %get-tuple-element.101.gain_ref, ...), custom_call_target="tpu_custom_call" | custom-call | flops 1000 | bytes 1000 | tf_op jit(solution)/shard_map/ffn_backward/pallas_call | solution.py:654
  372.5 5.8 reduce-scatter.3.cloned.1.call-done
  378.4 1.6 add_convert_fusion.1
  380.0 1.5 collective-permute-start.2
  381.5 34.9 %mixer_backward.3 = (bf16[1024,1536]{1,0:T(8,128)(2,1)}, bf16[1024,128]{1,0:T(8,128)(2,1)}, f32[8,1024]{1,0:T(8,128)}, f32[8,256]{1,0:T(8,128)}) custom-call(f32[1024,128]{1,0:T(8,128)} %get-tuple-element.97.small_ref, f32[8,1024]{1,0:T(8,128)} %get-tuple-element.98.taps_ref, f32[8,128]{1,0:T(8,128)} %get-tuple-element.214.heads_ref, ...), custom_call_target="tpu_custom_call" | custom-call | tf_op jit(solution)/shard_map/mixer_backward/pallas_call | solution.py:484
  416.5 23.3 %project_backward.3 = (f32[256,1024]{1,0:T(8,128)}, bf16[4,1552,128]{2,1,0:T(8,128)(2,1)}, bf16[4,1552,128]{2,1,0:T(8,128)(2,1)}) custom-call(bf16[1024,1536]{1,0:T(8,128)(2,1)} %get-tuple-element.152.dproj_ref, bf16[1024,128]{1,0:T(8,128)(2,1)} %get-tuple-element.153.dsmall_ref, bf16[1024,128]{1,0:T(8,128)(2,1)} %get-tuple-element.154.ab_ref, ...), custom_call_target="tpu_custom_call" | custom-call | flops 1000 | bytes 1000 | tf_op jit(solution)/shard_map/project_backward/pallas_call | solution.py:654
  440.1 1.5 copy-done
  441.6 232.4 %finish_reduction.1 = (bf16[8,2624,128]{2,1,0:T(8,128)(2,1)}, bf16[8,1600,128]{2,1,0:T(8,128)(2,1)}, bf16[8,2624,128]{2,1,0:T(8,128)(2,1)}, bf16[8,1600,128]{2,1,0:T(8,128)(2,1)}, f32[256,1024]{1,0:T(8,128)}) custom-call(bf16[2624,128]{1,0:T(8,128)(2,1)} %bitcast.44, bf16[1552,128]{1,0:T(8,128)(2,1)} %bitcast.45, ...), custom_call_target="tpu_custom_call" | custom-call | flops 1000 | bytes 1000 | tf_op jit(solution)/shard_map/finish_reduction/pallas_call | solution.py:2030
  674.0 18.5 %assemble.1 = (f32[2,704,1024]{2,1,0:T(8,128)}, f32[2,512,1024]{2,1,0:T(8,128)}, f32[2,256,5632]{2,1,0:T(8,128)}, f32[2,256,6144]{2,1,0:T(8,128)}, f32[4,2,128,1...) custom-call(bf16[8,2624,128]{2,1,0:T(8,128)(2,1)} %get-tuple-element.167.f1, ...), custom_call_target="tpu_custom_call" | custom-call | tf_op jit(solution)/shard_map/assemble/pallas_call | solution.py:1649
  692.5 0.9 slice_reduce_fusion
  693.4 1.0 fusion.16
  695.9 0.9 dynamic-slice_bitcast_fusion
  (37 shorter events, 5.0 us)
Async XLA Ops:
  7.2 124.9 %all-gather.3.cloned.1.call-start = ((), (), s32[]{:S(2)}) async-start(), calls=%async_computation.4 | async-start | bytes 1966080 | tf_op jit(solution)/shard_map/all_gather | solution.py:2185
  89.5 288.9 %reduce-scatter.3.cloned.1.call-start = ((), (), s32[]{:S(2)}) async-start(), calls=%async_computation.2 | async-start | bytes 3358720 | tf_op jit(solution)/shard_map/reduce_scatter | solution.py:2074
  261.7 60.9 %collective-permute-start = (bf16[4,2624,128]{2,1,0:T(8,128)(2,1)}, bf16[4,2624,128]{2,1,0:T(8,128)(2,1)S(1)}, u32[]{:S(2)}, u32[]{:S(2)}) collective-permute-start(bf16[4,2624,128]{2,1,0:T(8,128)(2,1)} %get-tuple-element.133), channel_id=1, source_target_pairs={{0,4},{4,0},{8,12},{12,8},{16,20},{20,16},{24,28},{28,24},{1,5},{5... | collective-permute-start | bytes 8060936 | tf_op jit(solution)/shard_map/ppermute | solution.py:2066
  298.1 24.5 %copy-start.1 = (bf16[4,2624,128]{2,1,0:T(8,128)(2,1)S(1)}, bf16[4,2624,128]{2,1,0:T(8,128)(2,1)}, u32[]{:S(2)}) copy-start(bf16[4,2624,128]{2,1,0:T(8,128)(2,1)} %get-tuple-element.140) | copy-start | bytes 8060932
  324.8 115.3 %reduce-scatter.5.cloned.1.call-start = ((), (), s32[]{:S(2)}) async-start(), calls=%async_computation.3 | async-start | bytes 1986560 | tf_op jit(solution)/shard_map/reduce_scatter | solution.py:2074
  324.9 47.7 %collective-permute-start.1 = (bf16[4,1552,128]{2,1,0:T(8,128)(2,1)}, bf16[4,1552,128]{2,1,0:T(8,128)(2,1)S(1)}, u32[]{:S(2)}, u32[]{:S(2)}) collective-permute-start(bf16[4,1552,128]{2,1,0:T(8,128)(2,1)} %get-tuple-element.142), channel_id=1, source_target_pairs={{0,4},{4,0},{8,12},{12,8},{16,20},{20,16},{24,28},{28,24},{1,5},{5... | collective-permute-start | bytes 4767752 | tf_op jit(solution)/shard_map/ppermute | solution.py:2066
  326.4 52.0 %copy-start.2 = (bf16[4,1552,128]{2,1,0:T(8,128)(2,1)S(1)}, bf16[4,1552,128]{2,1,0:T(8,128)(2,1)}, u32[]{:S(2)}) copy-start(bf16[4,1552,128]{2,1,0:T(8,128)(2,1)} %get-tuple-element.144) | copy-start | bytes 4767748
  380.0 60.1 %collective-permute-start.2 = (bf16[4,2624,128]{2,1,0:T(8,128)(2,1)}, bf16[4,2624,128]{2,1,0:T(8,128)(2,1)S(1)}, u32[]{:S(2)}, u32[]{:S(2)}) collective-permute-start(bf16[4,2624,128]{2,1,0:T(8,128)(2,1)} %get-tuple-element.163), channel_id=1, source_target_pairs={{0,4},{4,0},{8,12},{12,8},{16,20},{20,16},{24,28},{28,24},{1,5},{5... | collective-permute-start | bytes 8060936 | tf_op jit(solution)/shard_map/ppermute | solution.py:2066
  440.1 1.5 copy-start
Sparse Core Ops, SparseCore 0:
  89.6 37.8 all-gather.2
  324.9 53.3 reduce-scatter.2
  381.4 35.4 reduce-scatter.4
